TPU v7x, 32 devices: a whole 2x2x4 slice. The times are simulated.
32 devices in a mesh: ctx: 8 (over y, x, core), wt: 4 (over z).
Axes of the slice: x: 2, y: 2, z: 4, core: 2. Of those that a mesh axis runs over, the one named last changes fastest.
Arguments:
- tokens: bfloat16 [4, 2560, 1152], P('wt', 'ctx'), may hold values from -6 to 6
- assign: int32 [4, 8], P('wt'), may hold values from 0 to 7, each once within a row
- cotangent: bfloat16 [4, 2560, 1152], P('wt', 'ctx'), may hold values from -6 to 6
- attn_gain: bfloat16 [2, 1152], P(None, 'wt'), may hold values from 0.5 to 1.5
- w_query: bfloat16 [2, 1152, 1152], P(None, 'wt'), may hold values from -0.1875 to 0.1875
- w_key: bfloat16 [2, 1152, 384], P(None, 'wt'), may hold values from -0.1875 to 0.1875
- w_value: bfloat16 [2, 1152, 384], P(None, 'wt'), may hold values from -0.1875 to 0.1875
- w_out: bfloat16 [2, 1152, 1152], P(None, 'wt'), may hold values from -4 to 4
- mlp_gain: bfloat16 [2, 1152], P(None, 'wt'), may hold values from 0.5 to 1.5
- w_gate: bfloat16 [2, 1152, 3072], P(None, 'wt'), may hold values from -0.1875 to 0.1875
- w_up: bfloat16 [2, 1152, 3072], P(None, 'wt'), may hold values from -0.1875 to 0.1875
- w_down: bfloat16 [2, 3072, 1152], P(None, 'wt'), may hold values from -0.109375 to 0.109375
Outputs:
- layer_out: float32 [4, 2560, 1152], P('wt', 'ctx')
- token_grad: float32 [4, 2560, 1152], P('wt', 'ctx')
- attn_gain_grad: float32 [2, 1152], P(None, 'wt')
- w_query_grad: float32 [2, 1152, 1152], P(None, 'wt')
- w_key_grad: float32 [2, 1152, 384], P(None, 'wt')
- w_value_grad: float32 [2, 1152, 384], P(None, 'wt')
- w_out_grad: float32 [2, 1152, 1152], P(None, 'wt')
- mlp_gain_grad: float32 [2, 1152], P(None, 'wt')
- w_gate_grad: float32 [2, 1152, 3072], P(None, 'wt')
- w_up_grad: float32 [2, 1152, 3072], P(None, 'wt')
- w_down_grad: float32 [2, 3072, 1152], P(None, 'wt')
Inputs may be any that keep to these rules, and one draw needn't show every extreme that they name: Each row names every index of ctx once; ctx index c of group g holds prompt blocks assign[g, c] and 15 - assign[g, c], block b being prompt positions b * 32 to (b + 1) * 32 - 1.
All inputs are finite; a program needn't handle non-finite values.
Results may differ from a plain program's by a relative error of at most 0.025.
Values may be sent and summed in bfloat16 or wider, within the bound.
No kernel may reach another device: no remote copies, remote signals or barrier semaphores. Data moves between devices by JAX's collectives and lax.ppermute only.
A program may use at most 448 MiB of HBM per device.

v0:
```python
import jax
import jax.numpy as jnp
from jax import lax
from jax.sharding import PartitionSpec as P

HEADS = 18
KV_HEADS = 6
HEAD_DIM = 64
HALF = 32
CONT = 256


EPSILON = 1e-05
SCORE_SCALE = 0.125
MASKED = -1e30


def positions(deal_row, ctx_count):
    row_ids = jnp.arange(2 * HALF + CONT, dtype=jnp.int32)
    block_ids = deal_row[..., None]
    lower_block = block_ids * HALF + row_ids
    upper_block = (2 * ctx_count - 1 - block_ids) * HALF + row_ids - HALF
    continued = 2 * HALF * ctx_count + row_ids - 2 * HALF
    return jnp.where(
        row_ids < HALF, lower_block, jnp.where(row_ids < 2 * HALF, upper_block, continued)
    )


def angles(position):
    half_dim = HEAD_DIM // 2
    frequency = jnp.exp(jnp.arange(half_dim, dtype=jnp.float32) * (-jnp.log(10000.0) / half_dim))
    phase_angle = position.astype(jnp.float32)[..., None] * frequency
    return (jnp.cos(phase_angle), jnp.sin(phase_angle))


def rotate(value, cosine, sine):
    half_dim = value.shape[-1] // 2
    lower_half = value[..., :half_dim]
    upper_half = value[..., half_dim:]
    return jnp.concatenate(
        [lower_half * cosine - upper_half * sine, upper_half * cosine + lower_half * sine], axis=-1
    )


def rotate_back(grad_value, cosine, sine):
    half_dim = grad_value.shape[-1] // 2
    lower_half = grad_value[..., :half_dim]
    upper_half = grad_value[..., half_dim:]
    return jnp.concatenate(
        [lower_half * cosine + upper_half * sine, upper_half * cosine - lower_half * sine], axis=-1
    )


def normed_parts(value):
    inverse = lax.rsqrt(jnp.mean(value * value, axis=-1, keepdims=True) + EPSILON)
    return (value * inverse, inverse)


def norm_back(grad_normed, plain, inverse, gain_vec):
    scaled = grad_normed * gain_vec
    grad_gain = jnp.sum(grad_normed * plain, axis=0)
    grad_input = inverse * (scaled - plain * jnp.mean(scaled * plain, axis=-1, keepdims=True))
    return (grad_input, grad_gain)


def head_scores(head_q, head_k, allowed):
    scores = (
        jnp.einsum("tgd,sd->gts", head_q, head_k, preferred_element_type=jnp.float32) * SCORE_SCALE
    )
    return jnp.where(allowed[None], scores, MASKED)


def per_device(
    tokens,
    assign,
    cotangent,
    attn_gain,
    w_query,
    w_key,
    w_value,
    w_out,
    mlp_gain,
    w_gate,
    w_up,
    w_down,
):
    ctx_count = lax.axis_size("ctx")
    ctx_index = lax.axis_index("ctx")
    every_pos = positions(assign[0], ctx_count)
    is_mine = jnp.arange(ctx_count, dtype=jnp.int32) == ctx_index
    own_pos = jnp.sum(jnp.where(is_mine[:, None], every_pos, 0), axis=0)
    key_pos = jnp.concatenate([every_pos[:, : 2 * HALF].reshape(-1), own_pos[2 * HALF :]], axis=0)
    allowed = key_pos[None, :] <= own_pos[:, None]
    cos_t, sin_t = angles(own_pos)
    shared = HEADS // KV_HEADS
    tok_rows = own_pos.shape[0]
    key_width = KV_HEADS * HEAD_DIM
    query_width = HEADS * HEAD_DIM
    layer_count = attn_gain.shape[0]
    residual = tokens[0].astype(jnp.float32)
    saved_layers = []
    for layer_index in range(layer_count):
        gathered = (
            lax.all_gather(attn_gain[layer_index], "wt", axis=0, tiled=True),
            lax.all_gather(w_query[layer_index], "wt", axis=0, tiled=True),
            lax.all_gather(w_key[layer_index], "wt", axis=0, tiled=True),
            lax.all_gather(w_value[layer_index], "wt", axis=0, tiled=True),
            lax.all_gather(w_out[layer_index], "wt", axis=0, tiled=True),
            lax.all_gather(mlp_gain[layer_index], "wt", axis=0, tiled=True),
            lax.all_gather(w_gate[layer_index], "wt", axis=0, tiled=True),
            lax.all_gather(w_up[layer_index], "wt", axis=0, tiled=True),
            lax.all_gather(w_down[layer_index], "wt", axis=0, tiled=True),
        )
        gain_attn, query_w, key_w, value_w, out_w, gain_mlp, gate_w, up_w, down_w = gathered
        plain_attn, inverse_attn = normed_parts(residual)
        normed_attn = (plain_attn * gain_attn.astype(jnp.float32)).astype(jnp.bfloat16)
        query_pre = jnp.dot(normed_attn, query_w, preferred_element_type=jnp.float32).reshape(
            tok_rows, KV_HEADS, shared, HEAD_DIM
        )
        key_pre = jnp.dot(normed_attn, key_w, preferred_element_type=jnp.float32).reshape(
            tok_rows, KV_HEADS, HEAD_DIM
        )
        value_loc = jnp.dot(normed_attn, value_w, preferred_element_type=jnp.float32).astype(
            jnp.bfloat16
        )
        queries = rotate(query_pre, cos_t[:, None, None], sin_t[:, None, None]).astype(jnp.bfloat16)
        key_loc = (
            rotate(key_pre, cos_t[:, None], sin_t[:, None])
            .reshape(tok_rows, key_width)
            .astype(jnp.bfloat16)
        )
        prompt_key, prompt_value = (
            lax.all_gather(key_loc[: 2 * HALF], "ctx", axis=0, tiled=True),
            lax.all_gather(value_loc[: 2 * HALF], "ctx", axis=0, tiled=True),
        )
        keys = jnp.concatenate([prompt_key, key_loc[2 * HALF :]], axis=0).reshape(
            -1, KV_HEADS, HEAD_DIM
        )
        values = jnp.concatenate([prompt_value, value_loc[2 * HALF :]], axis=0).reshape(
            -1, KV_HEADS, HEAD_DIM
        )
        head_outs = []
        log_totals = []
        for head_index in range(KV_HEADS):
            scores = head_scores(queries[:, head_index], keys[:, head_index], allowed)
            row_max = jnp.max(scores, axis=-1, keepdims=True)
            log_total = row_max + jnp.log(
                jnp.sum(jnp.exp(scores - row_max), axis=-1, keepdims=True)
            )
            softmax_p = jnp.exp(scores - log_total).astype(jnp.bfloat16)
            head_outs.append(
                jnp.einsum(
                    "gts,sd->tgd",
                    softmax_p,
                    values[:, head_index],
                    preferred_element_type=jnp.float32,
                )
            )
            log_totals.append(log_total)
        attended = jnp.stack(head_outs, axis=1).reshape(tok_rows, query_width).astype(jnp.bfloat16)
        residual_mid = residual + jnp.dot(attended, out_w, preferred_element_type=jnp.float32)
        plain_mlp, inverse_mlp = normed_parts(residual_mid)
        normed_mlp = (plain_mlp * gain_mlp.astype(jnp.float32)).astype(jnp.bfloat16)
        gate_pre = jnp.dot(normed_mlp, gate_w, preferred_element_type=jnp.float32)
        up_pre = jnp.dot(normed_mlp, up_w, preferred_element_type=jnp.float32)
        swish_out = (jax.nn.silu(gate_pre) * up_pre).astype(jnp.bfloat16)
        residual = residual_mid + jnp.dot(swish_out, down_w, preferred_element_type=jnp.float32)
        kept_weights = None
        saved_layers.append(
            (
                kept_weights,
                plain_attn,
                inverse_attn,
                normed_attn,
                queries,
                keys,
                values,
                log_totals,
                attended,
                plain_mlp,
                inverse_mlp,
                normed_mlp,
                gate_pre,
                up_pre,
                swish_out,
            )
        )
    grad_flow = cotangent[0].astype(jnp.float32)
    layer_shares = [None] * layer_count
    for layer_index in reversed(range(layer_count)):
        (
            kept_weights,
            plain_attn,
            inverse_attn,
            normed_attn,
            queries,
            keys,
            values,
            log_totals,
            attended,
            plain_mlp,
            inverse_mlp,
            normed_mlp,
            gate_pre,
            up_pre,
            swish_out,
        ) = saved_layers[layer_index]
        gathered = (
            lax.all_gather(attn_gain[layer_index], "wt", axis=0, tiled=True),
            lax.all_gather(w_query[layer_index], "wt", axis=0, tiled=True),
            lax.all_gather(w_key[layer_index], "wt", axis=0, tiled=True),
            lax.all_gather(w_value[layer_index], "wt", axis=0, tiled=True),
            lax.all_gather(w_out[layer_index], "wt", axis=0, tiled=True),
            lax.all_gather(mlp_gain[layer_index], "wt", axis=0, tiled=True),
            lax.all_gather(w_gate[layer_index], "wt", axis=0, tiled=True),
            lax.all_gather(w_up[layer_index], "wt", axis=0, tiled=True),
            lax.all_gather(w_down[layer_index], "wt", axis=0, tiled=True),
        )
        gain_attn, query_w, key_w, value_w, out_w, gain_mlp, gate_w, up_w, down_w = gathered
        grad_down = grad_flow.astype(jnp.bfloat16)
        grad_down_w = jnp.einsum(
            "tf,td->fd", swish_out, grad_down, preferred_element_type=jnp.float32
        )
        grad_swish = jnp.einsum("td,fd->tf", grad_down, down_w, preferred_element_type=jnp.float32)
        sigmoid_g = jax.nn.sigmoid(gate_pre)
        grad_gate = (grad_swish * up_pre * sigmoid_g * (1.0 + gate_pre * (1.0 - sigmoid_g))).astype(
            jnp.bfloat16
        )
        grad_up = (grad_swish * gate_pre * sigmoid_g).astype(jnp.bfloat16)
        grad_gate_w = jnp.einsum(
            "td,tf->df", normed_mlp, grad_gate, preferred_element_type=jnp.float32
        )
        grad_up_w = jnp.einsum("td,tf->df", normed_mlp, grad_up, preferred_element_type=jnp.float32)
        grad_normed_mlp = jnp.einsum(
            "tf,df->td", grad_gate, gate_w, preferred_element_type=jnp.float32
        ) + jnp.einsum("tf,df->td", grad_up, up_w, preferred_element_type=jnp.float32)
        back_mlp, grad_gain_mlp = norm_back(
            grad_normed_mlp, plain_mlp, inverse_mlp, gain_mlp.astype(jnp.float32)
        )
        grad_flow = grad_flow + back_mlp
        grad_branch = grad_flow.astype(jnp.bfloat16)
        grad_out_w = jnp.einsum(
            "tq,td->qd", attended, grad_branch, preferred_element_type=jnp.float32
        )
        grad_attended = (
            jnp.einsum("td,qd->tq", grad_branch, out_w, preferred_element_type=jnp.float32)
            .astype(jnp.bfloat16)
            .reshape(tok_rows, KV_HEADS, shared, HEAD_DIM)
        )
        query_parts = []
        key_parts = []
        value_parts = []
        for head_index in range(KV_HEADS):
            head_q = queries[:, head_index]
            head_k = keys[:, head_index]
            head_v = values[:, head_index]
            head_do = grad_attended[:, head_index]
            softmax_p = jnp.exp(head_scores(head_q, head_k, allowed) - log_totals[head_index])
            grad_p = jnp.einsum("tgd,sd->gts", head_do, head_v, preferred_element_type=jnp.float32)
            delta_sum = jnp.sum(softmax_p * grad_p, axis=-1, keepdims=True)
            grad_scores = (softmax_p * (grad_p - delta_sum)).astype(jnp.bfloat16)
            query_parts.append(
                jnp.einsum("gts,sd->tgd", grad_scores, head_k, preferred_element_type=jnp.float32)
                * SCORE_SCALE
            )
            key_parts.append(
                jnp.einsum("gts,tgd->sd", grad_scores, head_q, preferred_element_type=jnp.float32)
                * SCORE_SCALE
            )
            value_parts.append(
                jnp.einsum(
                    "gts,tgd->sd",
                    softmax_p.astype(jnp.bfloat16),
                    head_do,
                    preferred_element_type=jnp.float32,
                )
            )
        grad_keys = jnp.stack(key_parts, axis=1).reshape(-1, key_width)
        grad_values = jnp.stack(value_parts, axis=1).reshape(-1, key_width)
        prompt_rows = grad_keys.shape[0] - (tok_rows - 2 * HALF)
        mine_key, mine_value = (
            lax.psum_scatter(
                grad_keys[:prompt_rows].astype(jnp.bfloat16), "ctx", scatter_dimension=0, tiled=True
            ).astype(jnp.float32),
            lax.psum_scatter(
                grad_values[:prompt_rows].astype(jnp.bfloat16),
                "ctx",
                scatter_dimension=0,
                tiled=True,
            ).astype(jnp.float32),
        )
        own_key_grad = jnp.concatenate([mine_key, grad_keys[prompt_rows:]], axis=0).reshape(
            tok_rows, KV_HEADS, HEAD_DIM
        )
        grad_key_pre = (
            rotate_back(own_key_grad, cos_t[:, None], sin_t[:, None])
            .reshape(tok_rows, key_width)
            .astype(jnp.bfloat16)
        )
        grad_value_loc = jnp.concatenate([mine_value, grad_values[prompt_rows:]], axis=0).astype(
            jnp.bfloat16
        )
        grad_query_pre = (
            rotate_back(jnp.stack(query_parts, axis=1), cos_t[:, None, None], sin_t[:, None, None])
            .reshape(tok_rows, query_width)
            .astype(jnp.bfloat16)
        )
        grad_query_w = jnp.einsum(
            "td,tq->dq", normed_attn, grad_query_pre, preferred_element_type=jnp.float32
        )
        grad_key_w = jnp.einsum(
            "td,tq->dq", normed_attn, grad_key_pre, preferred_element_type=jnp.float32
        )
        grad_value_w = jnp.einsum(
            "td,tq->dq", normed_attn, grad_value_loc, preferred_element_type=jnp.float32
        )
        grad_normed_attn = jnp.einsum(
            "tq,dq->td", grad_query_pre, query_w, preferred_element_type=jnp.float32
        )
        grad_normed_attn = grad_normed_attn + jnp.einsum(
            "tq,dq->td", grad_key_pre, key_w, preferred_element_type=jnp.float32
        )
        grad_normed_attn = grad_normed_attn + jnp.einsum(
            "tq,dq->td", grad_value_loc, value_w, preferred_element_type=jnp.float32
        )
        back_attn, grad_gain_attn = norm_back(
            grad_normed_attn, plain_attn, inverse_attn, gain_attn.astype(jnp.float32)
        )
        grad_flow = grad_flow + back_attn
        group_part = (
            lax.psum_scatter(
                grad_gain_attn.astype(jnp.bfloat16), "wt", scatter_dimension=0, tiled=True
            ).astype(jnp.float32),
            lax.psum_scatter(
                grad_query_w.astype(jnp.bfloat16), "wt", scatter_dimension=0, tiled=True
            ).astype(jnp.float32),
            lax.psum_scatter(
                grad_key_w.astype(jnp.bfloat16), "wt", scatter_dimension=0, tiled=True
            ).astype(jnp.float32),
            lax.psum_scatter(
                grad_value_w.astype(jnp.bfloat16), "wt", scatter_dimension=0, tiled=True
            ).astype(jnp.float32),
            lax.psum_scatter(
                grad_out_w.astype(jnp.bfloat16), "wt", scatter_dimension=0, tiled=True
            ).astype(jnp.float32),
            lax.psum_scatter(
                grad_gain_mlp.astype(jnp.bfloat16), "wt", scatter_dimension=0, tiled=True
            ).astype(jnp.float32),
            lax.psum_scatter(
                grad_gate_w.astype(jnp.bfloat16), "wt", scatter_dimension=0, tiled=True
            ).astype(jnp.float32),
            lax.psum_scatter(
                grad_up_w.astype(jnp.bfloat16), "wt", scatter_dimension=0, tiled=True
            ).astype(jnp.float32),
            lax.psum_scatter(
                grad_down_w.astype(jnp.bfloat16), "wt", scatter_dimension=0, tiled=True
            ).astype(jnp.float32),
        )
        shares = (
            lax.psum(group_part[0].astype(jnp.bfloat16), "ctx").astype(jnp.float32),
            lax.psum(group_part[1].astype(jnp.bfloat16), "ctx").astype(jnp.float32),
            lax.psum(group_part[2].astype(jnp.bfloat16), "ctx").astype(jnp.float32),
            lax.psum(group_part[3].astype(jnp.bfloat16), "ctx").astype(jnp.float32),
            lax.psum(group_part[4].astype(jnp.bfloat16), "ctx").astype(jnp.float32),
            lax.psum(group_part[5].astype(jnp.bfloat16), "ctx").astype(jnp.float32),
            lax.psum(group_part[6].astype(jnp.bfloat16), "ctx").astype(jnp.float32),
            lax.psum(group_part[7].astype(jnp.bfloat16), "ctx").astype(jnp.float32),
            lax.psum(group_part[8].astype(jnp.bfloat16), "ctx").astype(jnp.float32),
        )
        layer_shares[layer_index] = shares
    outputs = tuple(
        (jnp.stack([layer_part[member] for layer_part in layer_shares]) for member in range(9))
    )
    return (
        residual[None],
        grad_flow[None],
        outputs[0],
        outputs[1],
        outputs[2],
        outputs[3],
        outputs[4],
        outputs[5],
        outputs[6],
        outputs[7],
        outputs[8],
    )


def solution(mesh):
    return jax.shard_map(
        per_device,
        mesh=mesh,
        in_specs=(
            P("wt", "ctx", None),
            P("wt", None),
            P("wt", "ctx", None),
            P(None, "wt"),
            P(None, "wt", None),
            P(None, "wt", None),
            P(None, "wt", None),
            P(None, "wt", None),
            P(None, "wt"),
            P(None, "wt", None),
            P(None, "wt", None),
            P(None, "wt", None),
        ),
        out_specs=(
            P("wt", "ctx", None),
            P("wt", "ctx", None),
            P(None, "wt"),
            P(None, "wt", None),
            P(None, "wt", None),
            P(None, "wt", None),
            P(None, "wt", None),
            P(None, "wt"),
            P(None, "wt", None),
            P(None, "wt", None),
            P(None, "wt", None),
        ),
        check_vma=False,
    )
```

profile of v0, /device:TPU:0, one launch (start us, length us, event | category | flops | bytes accessed | tf_op | source)
XLA Modules:
  0.0 2619.1 jit_solution(2185649926182511245)
XLA Ops:
  27.2 21.2 all-reduce.11
  48.5 31.9 %all-gather.1 = bf16[1,1152,384]{2,1,0:T(8,128)(2,1)S(1)} all-gather(bf16[1,288,384]{2,1,0:T(8,128)(2,1)S(1)} %get-tuple-element.81), channel_id=3, replica_groups=mesh['ctx'=8,'wt'=4] {'wt'}, dimensions={1}, use_global_device_ids=true | all-gather | bytes 1105920 | tf_op jit(solution)/shard_map/all_gather | solution.py:107
  81.4 20.3 all-gather.2
  106.1 31.6 %all-gather.10 = bf16[1,1152,384]{2,1,0:T(8,128)(2,1)S(1)} all-gather(bf16[1,288,384]{2,1,0:T(8,128)(2,1)S(1)} %get-tuple-element.80), channel_id=12, replica_groups=mesh['ctx'=8,'wt'=4] {'wt'}, dimensions={1}, use_global_device_ids=true | all-gather | bytes 1105920 | tf_op jit(solution)/shard_map/all_gather | solution.py:107
  137.8 30.5 %all-gather.11 = bf16[1,1152,384]{2,1,0:T(8,128)(2,1)} all-gather(bf16[1,288,384]{2,1,0:T(8,128)(2,1)S(1)} %get-tuple-element.82), channel_id=13, replica_groups=mesh['ctx'=8,'wt'=4] {'wt'}, dimensions={1}, use_global_device_ids=true | all-gather | bytes 1105920 | tf_op jit(solution)/shard_map/all_gather | solution.py:106
  223.7 75.1 %all-gather.33.cloned.1.call-done = bf16[1,1152,3072]{2,1,0:T(8,128)(2,1)} async-done(((bf16[1,288,3072]{2,1,0:T(8,128)(2,1)}), bf16[1,1152,3072]{2,1,0:T(8,128)(2,1)}) %all-gather.33.cloned.1.call-update) | async-done | bytes 7077904 | tf_op jit(solution)/shard_map/all_gather | solution.py:110
  306.4 120.9 %all-gather.35.cloned.1.call-done = bf16[1,1152,3072]{2,1,0:T(8,128)(2,1)} async-done(((bf16[1,288,3072]{2,1,0:T(8,128)(2,1)}), bf16[1,1152,3072]{2,1,0:T(8,128)(2,1)}) %all-gather.35.cloned.1.call-update) | async-done | bytes 7077904 | tf_op jit(solution)/shard_map/all_gather | solution.py:111
  436.1 119.1 %all-gather.37.cloned.1.call-done = bf16[1,3072,1152]{2,1,0:T(8,128)(2,1)} async-done(((bf16[1,768,1152]{2,1,0:T(8,128)(2,1)}), bf16[1,3072,1152]{2,1,0:T(8,128)(2,1)}) %all-gather.37.cloned.1.call-update) | async-done | bytes 7077904 | tf_op jit(solution)/shard_map/all_gather | solution.py:112
  586.4 24.5 all-gather.39.cloned.1.call-done
  634.8 32.3 %all-gather.41.cloned.1.call-done = bf16[1,1152,1152]{2,1,0:T(8,128)(2,1)} async-done(((bf16[1,288,1152]{2,1,0:T(8,128)(2,1)}), bf16[1,1152,1152]{2,1,0:T(8,128)(2,1)}) %all-gather.41.cloned.1.call-update) | async-done | bytes 2654224 | tf_op jit(solution)/shard_map/all_gather | solution.py:108
  673.1 123.1 %all-gather.47.cloned.1.call-done = bf16[1,3072,1152]{2,1,0:T(8,128)(2,1)} async-done(((bf16[1,768,1152]{2,1,0:T(8,128)(2,1)}), bf16[1,3072,1152]{2,1,0:T(8,128)(2,1)}) %all-gather.47.cloned.1.call-update) | async-done | bytes 7077904 | tf_op jit(solution)/shard_map/all_gather | solution.py:112
  804.2 120.1 %all-gather.45.cloned.1.call-done = bf16[1,1152,3072]{2,1,0:T(8,128)(2,1)} async-done(((bf16[1,288,3072]{2,1,0:T(8,128)(2,1)}), bf16[1,1152,3072]{2,1,0:T(8,128)(2,1)}) %all-gather.45.cloned.1.call-update) | async-done | bytes 7077904 | tf_op jit(solution)/shard_map/all_gather | solution.py:111
  932.3 120.5 %all-gather.43.cloned.1.call-done = bf16[1,1152,3072]{2,1,0:T(8,128)(2,1)} async-done(((bf16[1,288,3072]{2,1,0:T(8,128)(2,1)}), bf16[1,1152,3072]{2,1,0:T(8,128)(2,1)}) %all-gather.43.cloned.1.call-update) | async-done | bytes 7077904 | tf_op jit(solution)/shard_map/all_gather | solution.py:110
  1052.8 11.2 multiply_convert_fusion.3
  1126.8 16.2 reduce-scatter.55.cloned.1.call-done
  1147.1 32.7 %reduce-scatter.57.cloned.1.call-done = bf16[64,384]{1,0:T(8,128)(2,1)} async-done(((bf16[512,384]{1,0:T(8,128)(2,1)}), bf16[64,384]{1,0:T(8,128)(2,1)}) %reduce-scatter.57.cloned.1.call-update) | async-done | bytes 49168
  1184.3 11.7 multiply_convert_fusion.1
  1276.4 32.8 %reduce-scatter.59.cloned.1.call-done = bf16[64,384]{1,0:T(8,128)(2,1)} async-done(((bf16[512,384]{1,0:T(8,128)(2,1)}), bf16[64,384]{1,0:T(8,128)(2,1)}) %reduce-scatter.59.cloned.1.call-update) | async-done | bytes 49168
  1387.6 25.8 reduce-scatter.31.cloned.1.call-done
  1413.4 54.0 %reduce-scatter.41.cloned.1.call-done = bf16[288,1152]{1,0:T(8,128)(2,1)} async-done(((bf16[1152,1152]{1,0:T(8,128)(2,1)}), bf16[288,1152]{1,0:T(8,128)(2,1)}) %reduce-scatter.41.cloned.1.call-update) | async-done | bytes 663568 | tf_op jit(solution)/shard_map/reduce_scatter | solution.py:343
  1467.4 55.1 %reduce-scatter.29.cloned.1.call-done = bf16[288,1152]{1,0:T(8,128)(2,1)} async-done(((bf16[1152,1152]{1,0:T(8,128)(2,1)}), bf16[288,1152]{1,0:T(8,128)(2,1)}) %reduce-scatter.29.cloned.1.call-update) | async-done | bytes 663568 | tf_op jit(solution)/shard_map/reduce_scatter | solution.py:334
  1522.5 54.7 %reduce-scatter.39.cloned.1.call-done = bf16[288,1152]{1,0:T(8,128)(2,1)} async-done(((bf16[1152,1152]{1,0:T(8,128)(2,1)}), bf16[288,1152]{1,0:T(8,128)(2,1)}) %reduce-scatter.39.cloned.1.call-update) | async-done | bytes 663568 | tf_op jit(solution)/shard_map/reduce_scatter | solution.py:343
  1577.2 55.2 %reduce-scatter.27.cloned.1.call-done = bf16[288,1152]{1,0:T(8,128)(2,1)} async-done(((bf16[1152,1152]{1,0:T(8,128)(2,1)}), bf16[288,1152]{1,0:T(8,128)(2,1)}) %reduce-scatter.27.cloned.1.call-update) | async-done | bytes 663568 | tf_op jit(solution)/shard_map/reduce_scatter | solution.py:334
  1632.4 125.5 %reduce-scatter.53.cloned.1.call-done = bf16[768,1152]{1,0:T(8,128)(2,1)} async-done(((bf16[3072,1152]{1,0:T(8,128)(2,1)}), bf16[768,1152]{1,0:T(8,128)(2,1)}) %reduce-scatter.53.cloned.1.call-update) | async-done | bytes 1769488 | tf_op jit(solution)/shard_map/reduce_scatter | solution.py:355
  1757.9 126.8 %reduce-scatter.45.cloned.1.call-done = bf16[288,3072]{1,0:T(8,128)(2,1)} async-done(((bf16[1152,3072]{1,0:T(8,128)(2,1)}), bf16[288,3072]{1,0:T(8,128)(2,1)}) %reduce-scatter.45.cloned.1.call-update) | async-done | bytes 1769488 | tf_op jit(solution)/shard_map/reduce_scatter | solution.py:349
  1884.7 126.9 %reduce-scatter.49.cloned.1.call-done = bf16[288,3072]{1,0:T(8,128)(2,1)} async-done(((bf16[1152,3072]{1,0:T(8,128)(2,1)}), bf16[288,3072]{1,0:T(8,128)(2,1)}) %reduce-scatter.49.cloned.1.call-update) | async-done | bytes 1769488 | tf_op jit(solution)/shard_map/reduce_scatter | solution.py:352
  2011.6 126.2 %reduce-scatter.51.cloned.1.call-done = bf16[768,1152]{1,0:T(8,128)(2,1)} async-done(((bf16[3072,1152]{1,0:T(8,128)(2,1)}), bf16[768,1152]{1,0:T(8,128)(2,1)}) %reduce-scatter.51.cloned.1.call-update) | async-done | bytes 1769488 | tf_op jit(solution)/shard_map/reduce_scatter | solution.py:355
  2137.8 126.8 %reduce-scatter.43.cloned.1.call-done = bf16[288,3072]{1,0:T(8,128)(2,1)} async-done(((bf16[1152,3072]{1,0:T(8,128)(2,1)}), bf16[288,3072]{1,0:T(8,128)(2,1)}) %reduce-scatter.43.cloned.1.call-update) | async-done | bytes 1769488 | tf_op jit(solution)/shard_map/reduce_scatter | solution.py:349
  2264.6 126.3 %reduce-scatter.47.cloned.1.call-done = bf16[288,3072]{1,0:T(8,128)(2,1)} async-done(((bf16[1152,3072]{1,0:T(8,128)(2,1)}), bf16[288,3072]{1,0:T(8,128)(2,1)}) %reduce-scatter.47.cloned.1.call-update) | async-done | bytes 1769488 | tf_op jit(solution)/shard_map/reduce_scatter | solution.py:352
  2403.8 17.9 all-reduce.10
  2422.1 13.6 all-reduce.8
  2439.8 153.2 %all-reduce.14.cloned.1.call-done = (bf16[1,288,1152]{2,1,0:T(8,128)(2,1)}, bf16[1,288,1152]{2,1,0:T(8,128)(2,1)}, bf16[1,288,384]{2,1,0:T(8,128)(2,1)}, bf16[1,...) async-done(((bf16[1,288,1152]{2,1,0:T(8,128)(2,1)}, ...) | async-done | bytes 14155792 | tf_op jit(solution)/shard_map/psum | solution.py:361
  (740 shorter events, 436.8 us)
Async XLA Ops:
  7.2 184.1 %all-gather.29.cloned.1.call-start = ((), (), s32[]{:S(2)}) async-start(), calls=%async_computation.32 | async-start | bytes 3317760 | tf_op jit(solution)/shard_map/all_gather | solution.py:105
  9.7 210.4 %all-gather.31.cloned.1.call-start = ((), (), s32[]{:S(2)}) async-start(), calls=%async_computation.33 | async-start | bytes 3317760 | tf_op jit(solution)/shard_map/all_gather | solution.py:108
  12.4 286.4 %all-gather.33.cloned.1.call-start = ((), (), s32[]{:S(2)}) async-start(), calls=%async_computation.34 | async-start | bytes 8847360 | tf_op jit(solution)/shard_map/all_gather | solution.py:110
  14.5 412.8 %all-gather.35.cloned.1.call-start = ((), (), s32[]{:S(2)}) async-start(), calls=%async_computation.35 | async-start | bytes 8847360 | tf_op jit(solution)/shard_map/all_gather | solution.py:111
  18.8 536.5 %all-gather.37.cloned.1.call-start = ((), (), s32[]{:S(2)}) async-start(), calls=%async_computation.36 | async-start | bytes 8847360 | tf_op jit(solution)/shard_map/all_gather | solution.py:112
  20.9 590.1 %all-gather.39.cloned.1.call-start = ((), (), s32[]{:S(2)}) async-start(), calls=%async_computation.37 | async-start | bytes 3317760 | tf_op jit(solution)/shard_map/all_gather | solution.py:105
  21.5 645.6 %all-gather.41.cloned.1.call-start = ((), (), s32[]{:S(2)}) async-start(), calls=%async_computation.38 | async-start | bytes 3317760 | tf_op jit(solution)/shard_map/all_gather | solution.py:108
  22.2 774.0 %all-gather.47.cloned.1.call-start = ((), (), s32[]{:S(2)}) async-start(), calls=%async_computation.41 | async-start | bytes 8847360 | tf_op jit(solution)/shard_map/all_gather | solution.py:112
  23.0 901.3 %all-gather.45.cloned.1.call-start = ((), (), s32[]{:S(2)}) async-start(), calls=%async_computation.40 | async-start | bytes 8847360 | tf_op jit(solution)/shard_map/all_gather | solution.py:111
  23.7 1029.0 %all-gather.43.cloned.1.call-start = ((), (), s32[]{:S(2)}) async-start(), calls=%async_computation.39 | async-start | bytes 8847360 | tf_op jit(solution)/shard_map/all_gather | solution.py:110
  24.3 1118.7 %reduce-scatter.55.cloned.1.call-start = ((), (), s32[]{:S(2)}) async-start(), calls=%async_computation.42 | async-start | bytes 442368
  103.6 1040.3 %copy-start.83 = (f32[320,32]{0,1:T(8,128)}, f32[320,32]{0,1:T(8,128)S(1)}, u32[]{:S(2)}) copy-start(f32[320,32]{0,1:T(8,128)S(1)} %get-tuple-element.86) | copy-start | bytes 122884
  103.6 1040.3 %copy-start.86 = (f32[320,32]{0,1:T(8,128)}, f32[320,32]{0,1:T(8,128)S(1)}, u32[]{:S(2)}) copy-start(f32[320,32]{0,1:T(8,128)S(1)} %get-tuple-element.87) | copy-start | bytes 122884
  137.8 425.2 %copy-start.93 = (bf16[1,1152,384]{2,1,0:T(8,128)(2,1)}, bf16[1,1152,384]{2,1,0:T(8,128)(2,1)S(1)}, u32[]{:S(2)}) copy-start(bf16[1,1152,384]{2,1,0:T(8,128)(2,1)S(1)} %all-gather.10) | copy-start | bytes 2654212
  1110.7 69.1 %reduce-scatter.57.cloned.1.call-start = ((), (), s32[]{:S(2)}) async-start(), calls=%async_computation.43 | async-start | bytes 442368
  1122.0 150.4 %reduce-scatter.61.cloned.1.call-start = ((), (), s32[]{:S(2)}) async-start(), calls=%async_computation.45 | async-start | bytes 442368
  1238.4 70.8 %reduce-scatter.59.cloned.1.call-start = ((), (), s32[]{:S(2)}) async-start(), calls=%async_computation.44 | async-start | bytes 442368
  1260.9 124.9 %reduce-scatter.37.cloned.1.call-start = ((), (), s32[]{:S(2)}) async-start(), calls=%async_computation.23 | async-start | bytes 1105920 | tf_op jit(solution)/shard_map/reduce_scatter | solution.py:340
  1262.8 123.0 %reduce-scatter.33.cloned.1.call-start = ((), (), s32[]{:S(2)}) async-start(), calls=%async_computation.21 | async-start | bytes 1105920 | tf_op jit(solution)/shard_map/reduce_scatter | solution.py:337
  1264.6 123.0 %reduce-scatter.35.cloned.1.call-start = ((), (), s32[]{:S(2)}) async-start(), calls=%async_computation.22 | async-start | bytes 1105920 | tf_op jit(solution)/shard_map/reduce_scatter | solution.py:340
  1275.2 138.2 %reduce-scatter.31.cloned.1.call-start = ((), (), s32[]{:S(2)}) async-start(), calls=%async_computation.20 | async-start | bytes 1105920 | tf_op jit(solution)/shard_map/reduce_scatter | solution.py:337
  1313.0 154.4 %reduce-scatter.41.cloned.1.call-start = ((), (), s32[]{:S(2)}) async-start(), calls=%async_computation.25 | async-start | bytes 3317760 | tf_op jit(solution)/shard_map/reduce_scatter | solution.py:343
  1317.4 205.1 %reduce-scatter.29.cloned.1.call-start = ((), (), s32[]{:S(2)}) async-start(), calls=%async_computation.19 | async-start | bytes 3317760 | tf_op jit(solution)/shard_map/reduce_scatter | solution.py:334
  1322.3 254.9 %reduce-scatter.39.cloned.1.call-start = ((), (), s32[]{:S(2)}) async-start(), calls=%async_computation.24 | async-start | bytes 3317760 | tf_op jit(solution)/shard_map/reduce_scatter | solution.py:343
  1326.8 305.6 %reduce-scatter.27.cloned.1.call-start = ((), (), s32[]{:S(2)}) async-start(), calls=%async_computation.18 | async-start | bytes 3317760 | tf_op jit(solution)/shard_map/reduce_scatter | solution.py:334
  1336.6 421.4 %reduce-scatter.53.cloned.1.call-start = ((), (), s32[]{:S(2)}) async-start(), calls=%async_computation.31 | async-start | bytes 8847360 | tf_op jit(solution)/shard_map/reduce_scatter | solution.py:355
  1344.8 539.9 %reduce-scatter.45.cloned.1.call-start = ((), (), s32[]{:S(2)}) async-start(), calls=%async_computation.27 | async-start | bytes 8847360 | tf_op jit(solution)/shard_map/reduce_scatter | solution.py:349
  1353.1 658.5 %reduce-scatter.49.cloned.1.call-start = ((), (), s32[]{:S(2)}) async-start(), calls=%async_computation.29 | async-start | bytes 8847360 | tf_op jit(solution)/shard_map/reduce_scatter | solution.py:352
  1360.5 777.4 %reduce-scatter.51.cloned.1.call-start = ((), (), s32[]{:S(2)}) async-start(), calls=%async_computation.30 | async-start | bytes 8847360 | tf_op jit(solution)/shard_map/reduce_scatter | solution.py:355
  1369.9 894.7 %reduce-scatter.43.cloned.1.call-start = ((), (), s32[]{:S(2)}) async-start(), calls=%async_computation.26 | async-start | bytes 8847360 | tf_op jit(solution)/shard_map/reduce_scatter | solution.py:349
  1378.2 1012.7 %reduce-scatter.47.cloned.1.call-start = ((), (), s32[]{:S(2)}) async-start(), calls=%async_computation.28 | async-start | bytes 8847360 | tf_op jit(solution)/shard_map/reduce_scatter | solution.py:352
  1385.7 1207.2 %all-reduce.14.cloned.1.call-start = ((), (), s32[]{:S(2)}) async-start(), calls=%async_computation.46 | async-start | bytes 28311552 | tf_op jit(solution)/shard_map/psum | solution.py:361
  (197 other events, 2416.0 us)
Sparse Core Ops, SparseCore 0:
  10.2 73.8 all-gather.28
  86.2 83.1 all-gather.30
  171.6 127.1 all-gather.32
  300.8 126.4 all-gather.34
  428.7 126.4 all-gather.36
  557.2 53.7 all-gather.38
  613.1 53.9 all-gather.40
  669.3 126.9 all-gather.46
  797.8 126.4 all-gather.44
  926.3 126.4 all-gather.42
  1110.8 32.1 reduce-scatter.54
  1145.9 33.8 reduce-scatter.56
  1238.5 33.8 reduce-scatter.60
  1275.3 33.8 reduce-scatter.58
  1311.3 24.5 reduce-scatter.36
  1338.1 23.6 reduce-scatter.32
  1363.9 23.6 reduce-scatter.34
  1389.8 23.6 reduce-scatter.30
  1415.7 51.6 reduce-scatter.40
  1470.2 52.3 reduce-scatter.28
  1524.8 52.3 reduce-scatter.38
  1580.1 52.3 reduce-scatter.26
  1634.7 123.1 reduce-scatter.52
  1760.7 123.9 reduce-scatter.44
  1887.6 124.0 reduce-scatter.48
  2013.8 124.0 reduce-scatter.50
  2140.6 123.9 reduce-scatter.42
  2266.9 123.9 reduce-scatter.46
  2397.3 195.6 all-reduce.13
where the time goes:
time: 2630 us; the launch traced here: 2620 us
  waiting for transfers between devices  1990 us (76%)
  matrix products  270 us (10%)
  blocking collectives  205 us (8%)
  local copies, waits for them, and re-layouts  86.4 us (3%)
  other arithmetic  51.2 us (2%)
    reduce_scatter x2, waiting for transfers between devices, per_device(): lax.psum_scatter(grad_gate_w.astype(jnp.bfloat16), 'wt', scatter_dimensio...  254 us
    reduce_scatter x2, waiting for transfers between devices, per_device(): lax.psum_scatter(grad_up_w.astype(jnp.bfloat16), 'wt', scatter_dimension=...  253 us
    reduce_scatter x2, waiting for transfers between devices, per_device(): lax.psum_scatter(grad_down_w.astype(jnp.bfloat16), 'wt', scatter_dimensio...  252 us
    all_gather x2, waiting for transfers between devices, per_device(): lax.all_gather(w_down[layer_index], 'wt', axis=0, tiled=True)  242 us
    all_gather x2, waiting for transfers between devices, per_device(): lax.all_gather(w_up[layer_index], 'wt', axis=0, tiled=True)  241 us
    all_gather x2, waiting for transfers between devices, per_device(): lax.all_gather(w_gate[layer_index], 'wt', axis=0, tiled=True)  196 us
    psum x1, waiting for transfers between devices, per_device(): lax.psum(group_part[1].astype(jnp.bfloat16), 'ctx').astype(jnp.float32)  153 us
    reduce_scatter x2, waiting for transfers between devices, per_device(): lax.psum_scatter(grad_query_w.astype(jnp.bfloat16), 'wt', scatter_dimensi...  110 us
  transfers between devices with their start and end apart: 29, of which 25 were waited for; matrix products, arithmetic and copies ran while one was open for 9% of the time, Pallas kernels for 0%

commit v1 on v0

v1 whole, which is shorter than its diff:
```python
import functools
import math

import jax
import jax.numpy as jnp
from jax import lax
from jax.experimental import pallas as pl
from jax.experimental.pallas import tpu as pltpu
from jax.sharding import PartitionSpec as P

HEADS = 18
KV_HEADS = 6
HEAD_DIM = 64
HALF = 32
CONT = 256
SHARED = HEADS // KV_HEADS
PAIR_KV = KV_HEADS // 2
PAIR_HEADS = HEADS // 2
RUN = 2 * HALF + CONT
ROWS = 2 * RUN
PROMPT = 4 * HALF
TAIL = 2 * CONT

EPSILON = 1e-05
SCORE_SCALE = 0.125
BASE_TWO = SCORE_SCALE * math.log2(math.e)
MASKED = -1e30

BF16 = jnp.bfloat16
F32 = jnp.float32

PAIR, SIDE, ROW = 1, 2, 4


def dot_nn(left, right):
    return lax.dot_general(left, right, (((1,), (0,)), ((), ())), preferred_element_type=F32)


def dot_nt(left, right):
    return lax.dot_general(left, right, (((1,), (1,)), ((), ())), preferred_element_type=F32)


def dot_tn(left, right):
    return lax.dot_general(left, right, (((0,), (0,)), ((), ())), preferred_element_type=F32)


def dot_tt(left, right):
    return lax.dot_general(left, right, (((0,), (1,)), ((), ())), preferred_element_type=F32)


def turned(value):
    return jnp.transpose(value.astype(F32))


def shaped(shape, dtype):
    return jax.ShapeDtypeStruct(shape, dtype)


WHOLE = pl.BlockSpec(memory_space=pltpu.VMEM)
FAR = pl.BlockSpec(memory_space=pl.ANY)
SCALARS = pl.BlockSpec(memory_space=pltpu.SMEM)


def call(kernel, outs, ins, flops, limit, out_specs=None, in_specs=None, **extra):
    moved = sum(math.prod(v.shape) * v.dtype.itemsize for v in (*ins, *outs))
    return pl.pallas_call(
        kernel,
        out_shape=outs,
        in_specs=in_specs or [WHOLE] * len(ins),
        out_specs=out_specs or [WHOLE] * len(outs),
        compiler_params=pltpu.CompilerParams(vmem_limit_bytes=limit << 20),
        cost_estimate=pl.CostEstimate(flops=flops, bytes_accessed=moved, transcendentals=0),
        **extra,
    )(*ins)


def add_norm_kernel(has_parts, *refs):
    if has_parts:
        held, mine, other, gain, total_ref, normed_ref = refs
        total = held[...] + (mine[...].astype(F32) + other[...].astype(F32))
        total_ref[...] = total
    else:
        held, gain, normed_ref = refs
        total = held[...]
    inverse = lax.rsqrt(jnp.mean(total * total, axis=-1, keepdims=True) + EPSILON)
    normed_ref[...] = (total * inverse * gain[...]).astype(BF16)


def add_norm(held, parts, gain):
    rows, width = held.shape
    step = 128
    block = pl.BlockSpec((step, width), lambda i: (i, 0))
    line = pl.BlockSpec((1, width), lambda i: (0, 0))
    ins = (held, *parts, gain)
    outs = ([shaped(held.shape, F32)] if parts else []) + [shaped(held.shape, BF16)]
    result = call(
        functools.partial(add_norm_kernel, bool(parts)),
        outs,
        ins,
        0,
        16,
        in_specs=[block] * (1 + len(parts)) + [line],
        out_specs=[block] * len(outs),
        grid=(rows // step,),
    )
    return result if parts else (held, result[0])


def norm_back_kernel(flow, mine, other, held, gain, flow_ref, low_ref, gain_ref):
    grad = mine[...].astype(F32) + other[...].astype(F32)
    value = held[...]
    inverse = lax.rsqrt(jnp.mean(value * value, axis=-1, keepdims=True) + EPSILON)
    plain = value * inverse
    scaled = grad * gain[...]
    tilt = jnp.mean(scaled * plain, axis=-1, keepdims=True)
    total = flow[...] + inverse * (scaled - plain * tilt)
    flow_ref[...] = total
    low_ref[...] = total.astype(BF16)

    @pl.when(pl.program_id(0) == 0)
    def _():
        gain_ref[...] = jnp.zeros_like(gain_ref)

    gain_ref[...] += jnp.sum(grad * plain, axis=0, keepdims=True)


def norm_back(flow, parts, held, gain):
    rows, width = held.shape
    step = 128
    block = pl.BlockSpec((step, width), lambda i: (i, 0))
    line = pl.BlockSpec((1, width), lambda i: (0, 0))
    return call(
        norm_back_kernel,
        [shaped(held.shape, F32), shaped(held.shape, BF16), shaped((1, width), F32)],
        (flow, *parts, held, gain),
        0,
        16,
        in_specs=[block] * 4 + [line],
        out_specs=[block, block, line],
        grid=(rows // step,),
    )


KEY_HALF = PAIR_KV * HEAD_DIM
QUERY_HALF = PAIR_HEADS * HEAD_DIM
QKV = 2 * KEY_HALF + QUERY_HALF


def rope_kernel(qkv_ref, cos_ref, sin_ref, query_ref, kv_ref, kv_turned_ref):
    cosine, sine = cos_ref[...], sin_ref[...]
    half = HEAD_DIM // 2

    def head(source, target_ref, target):
        low = qkv_ref[source : source + half, :]
        high = qkv_ref[source + half : source + 2 * half, :]
        target_ref[target : target + half, :] = (low * cosine - high * sine).astype(BF16)
        target_ref[target + half : target + 2 * half, :] = (high * cosine + low * sine).astype(
            BF16
        )

    for index in range(PAIR_KV):
        head(index * HEAD_DIM, kv_turned_ref, index * HEAD_DIM)
    kv_turned_ref[KEY_HALF:, :] = qkv_ref[KEY_HALF : 2 * KEY_HALF, :].astype(BF16)
    kv_ref[...] = turned(kv_turned_ref[...]).astype(BF16)
    for index in range(PAIR_HEADS):
        head(2 * KEY_HALF + index * HEAD_DIM, query_ref, index * HEAD_DIM)


def rope(qkv, cosine, sine):
    return call(
        rope_kernel,
        [
            shaped((QUERY_HALF, ROWS), BF16),
            shaped((ROWS, 2 * KEY_HALF), BF16),
            shaped((2 * KEY_HALF, ROWS), BF16),
        ],
        (qkv, cosine, sine),
        0,
        32,
    )


def later_mask():
    key = lax.broadcasted_iota(jnp.int32, (CONT, CONT), 0)
    query = lax.broadcasted_iota(jnp.int32, (CONT, CONT), 1)
    return key <= query


def attend_kernel(
    query_ref, kv_ref, kv_turned_ref, shared_ref, key_pos_ref, row_pos_ref, out_ref, lse_ref
):
    shared_values = turned(shared_ref[:, KEY_HALF:]).astype(BF16)
    for kv_head in range(PAIR_KV):
        low = kv_head * HEAD_DIM
        keys = shared_ref[:, low : low + HEAD_DIM]
        values = shared_values[low : low + HEAD_DIM, :]

        def head(index, carry, kv_head=kv_head, low=low, keys=keys, values=values):
            number = kv_head * SHARED + index
            base = pl.multiple_of(number * HEAD_DIM, HEAD_DIM)
            allowed = key_pos_ref[...] <= row_pos_ref[...]
            query = query_ref[pl.ds(base, HEAD_DIM), TAIL:]
            scores = jnp.where(allowed, dot_nn(keys, query) * BASE_TWO, MASKED)
            top = jnp.max(scores, axis=0, keepdims=True)
            weight = jnp.exp2(scores - top)
            total = jnp.sum(weight, axis=0, keepdims=True)
            out = dot_nn(values, weight.astype(BF16)) / total
            out_ref[pl.ds(base, HEAD_DIM), TAIL:] = out.astype(BF16)
            lse_ref[number, :, TAIL:] = top + jnp.log2(total)
            for run in range(2):
                cols = slice(run * CONT, (run + 1) * CONT)
                query = query_ref[pl.ds(base, HEAD_DIM), cols]
                own_keys = kv_ref[cols, low : low + HEAD_DIM]
                own_values = kv_turned_ref[KEY_HALF + low : KEY_HALF + low + HEAD_DIM, cols]
                first = dot_nn(keys, query) * BASE_TWO
                second = jnp.where(later_mask(), dot_nn(own_keys, query) * BASE_TWO, MASKED)
                top = jnp.maximum(
                    jnp.max(first, axis=0, keepdims=True), jnp.max(second, axis=0, keepdims=True)
                )
                first = jnp.exp2(first - top)
                second = jnp.exp2(second - top)
                total = jnp.sum(first, axis=0, keepdims=True) + jnp.sum(
                    second, axis=0, keepdims=True
                )
                out = dot_nn(values, first.astype(BF16)) + dot_nn(
                    own_values, second.astype(BF16)
                )
                out_ref[pl.ds(base, HEAD_DIM), cols] = (out / total).astype(BF16)
                lse_ref[number, :, cols] = top + jnp.log2(total)
            return carry

        lax.fori_loop(0, SHARED, head, 0)


def attend(query, key_value, key_value_turned, shared, key_pos, row_pos):
    flops = 4 * QUERY_HALF * ROWS * (shared.shape[0] + CONT)
    return call(
        attend_kernel,
        [shaped((QUERY_HALF, ROWS), BF16), shaped((PAIR_HEADS, 1, ROWS), F32)],
        (query, key_value, key_value_turned, shared, key_pos, row_pos),
        flops,
        48,
    )


def attend_back_kernel(
    query_ref,
    grad_ref,
    kv_ref,
    kv_turned_ref,
    shared_ref,
    key_pos_ref,
    row_pos_ref,
    lse_ref,
    cos_ref,
    sin_ref,
    query_grad_ref,
    own_grad_ref,
    shared_grad_ref,
    score_keep,
    weight_keep,
    own_score_keep,
    own_weight_keep,
):
    shared_turned = turned(shared_ref[:, :KEY_HALF]).astype(BF16)
    half = HEAD_DIM // 2
    for kv_head in range(PAIR_KV):
        low = kv_head * HEAD_DIM
        keys = shared_ref[:, low : low + HEAD_DIM]
        values = shared_ref[:, KEY_HALF + low : KEY_HALF + low + HEAD_DIM]
        keys_turned = shared_turned[low : low + HEAD_DIM, :]

        def head(index, carry, kv_head=kv_head, low=low, keys=keys, values=values, keys_turned=keys_turned):
            number = kv_head * SHARED + index
            base = pl.multiple_of(number * HEAD_DIM, HEAD_DIM)

            def put_query_grad(grad, cols):
                cosine, sine = cos_ref[:, cols], sin_ref[:, cols]
                first, second = grad[:half], grad[half:]
                query_grad_ref[pl.ds(base, half), cols] = (
                    (first * cosine + second * sine) * SCORE_SCALE
                ).astype(BF16)
                query_grad_ref[pl.ds(base + half, half), cols] = (
                    (second * cosine - first * sine) * SCORE_SCALE
                ).astype(BF16)

            cols = slice(TAIL, ROWS)
            query = query_ref[pl.ds(base, HEAD_DIM), cols]
            grad = grad_ref[pl.ds(base, HEAD_DIM), cols]
            lse = lse_ref[number, :, cols]
            allowed = key_pos_ref[...] <= row_pos_ref[...]
            scores = jnp.where(allowed, dot_nn(keys, query) * BASE_TWO, MASKED)
            weight = jnp.exp2(scores - lse)
            weight_keep[index, :, cols] = weight.astype(BF16)
            flow = weight * dot_nn(values, grad)
            delta = jnp.sum(flow, axis=0, keepdims=True)
            flow = (flow - weight * delta).astype(BF16)
            score_keep[index, :, cols] = flow
            put_query_grad(dot_nn(keys_turned, flow), cols)
            for run in range(2):
                cols = slice(run * CONT, (run + 1) * CONT)
                query = query_ref[pl.ds(base, HEAD_DIM), cols]
                grad = grad_ref[pl.ds(base, HEAD_DIM), cols]
                lse = lse_ref[number, :, cols]
                own_keys = kv_ref[cols, low : low + HEAD_DIM]
                own_values = kv_ref[cols, KEY_HALF + low : KEY_HALF + low + HEAD_DIM]
                own_turned = kv_turned_ref[low : low + HEAD_DIM, cols]
                first = jnp.exp2(dot_nn(keys, query) * BASE_TWO - lse)
                second = jnp.where(later_mask(), dot_nn(own_keys, query) * BASE_TWO, MASKED)
                second = jnp.exp2(second - lse)
                weight_keep[index, :, cols] = first.astype(BF16)
                own_weight_keep[index, :, cols] = second.astype(BF16)
                first_flow = first * dot_nn(values, grad)
                second_flow = second * dot_nn(own_values, grad)
                delta = jnp.sum(first_flow, axis=0, keepdims=True) + jnp.sum(
                    second_flow, axis=0, keepdims=True
                )
                first_flow = (first_flow - first * delta).astype(BF16)
                second_flow = (second_flow - second * delta).astype(BF16)
                score_keep[index, :, cols] = first_flow
                own_score_keep[index, :, cols] = second_flow
                put_query_grad(
                    dot_nn(keys_turned, first_flow) + dot_nn(own_turned, second_flow), cols
                )
            return carry

        lax.fori_loop(0, SHARED, head, 0)
        key_sum, value_sum = 0.0, 0.0
        own_key_sum, own_value_sum = [0.0, 0.0], [0.0, 0.0]
        for index in range(SHARED):
            base = (kv_head * SHARED + index) * HEAD_DIM
            query = query_ref[base : base + HEAD_DIM, :]
            grad = grad_ref[base : base + HEAD_DIM, :]
            key_sum = key_sum + dot_nt(score_keep[index], query)
            value_sum = value_sum + dot_nt(weight_keep[index], grad)
            for run in range(2):
                cols = slice(run * CONT, (run + 1) * CONT)
                own_key_sum[run] = own_key_sum[run] + dot_nt(
                    own_score_keep[index, :, cols], query[:, cols]
                )
                own_value_sum[run] = own_value_sum[run] + dot_nt(
                    own_weight_keep[index, :, cols], grad[:, cols]
                )
        shared_grad_ref[:, low : low + HEAD_DIM] = key_sum * SCORE_SCALE
        shared_grad_ref[:, KEY_HALF + low : KEY_HALF + low + HEAD_DIM] = value_sum
        for run in range(2):
            cols = slice(run * CONT, (run + 1) * CONT)
            own_grad_ref[cols, low : low + HEAD_DIM] = own_key_sum[run] * SCORE_SCALE
            own_grad_ref[cols, KEY_HALF + low : KEY_HALF + low + HEAD_DIM] = own_value_sum[run]


def attend_back(query, grad, key_value, key_value_turned, shared, key_pos, row_pos, lse, cosine, sine):
    count = shared.shape[0]
    flops = 10 * QUERY_HALF * ROWS * (count + CONT)
    return call(
        attend_back_kernel,
        [
            shaped((QUERY_HALF, ROWS), BF16),
            shaped((TAIL, 2 * KEY_HALF), F32),
            shaped((count, 2 * KEY_HALF), F32),
        ],
        (query, grad, key_value, key_value_turned, shared, key_pos, row_pos, lse, cosine, sine),
        flops,
        56,
        scratch_shapes=[
            pltpu.VMEM((SHARED, count, ROWS), BF16),
            pltpu.VMEM((SHARED, count, ROWS), BF16),
            pltpu.VMEM((SHARED, CONT, TAIL), BF16),
            pltpu.VMEM((SHARED, CONT, TAIL), BF16),
        ],
    )


def merge_kernel(query_grad_ref, own_ref, prompt_ref, cos_ref, sin_ref, out_ref):
    cosine, sine = cos_ref[...], sin_ref[...]
    half = HEAD_DIM // 2
    both = turned(jnp.concatenate([own_ref[...], prompt_ref[...]], axis=0))
    pieces = []
    for index in range(PAIR_KV):
        low = both[index * HEAD_DIM : index * HEAD_DIM + half]
        high = both[index * HEAD_DIM + half : (index + 1) * HEAD_DIM]
        pieces += [low * cosine + high * sine, high * cosine - low * sine]
    both = jnp.concatenate(pieces + [both[KEY_HALF:]], axis=0)
    out_ref[:, : 2 * KEY_HALF] = jnp.transpose(both).astype(BF16)
    out_ref[:, 2 * KEY_HALF :] = turned(query_grad_ref[...]).astype(BF16)


def merge(query_grad, own_grad, prompt_grad, cosine, sine):
    return call(
        merge_kernel,
        [shaped((ROWS, QKV), BF16)],
        (query_grad, own_grad, prompt_grad, cosine, sine),
        0,
        32,
    )[0]


def weight_copies(pieces, target, sems, block, depth):
    if block < 3:
        return [
            pltpu.make_async_copy(
                pieces[block].at[:, : 2 * block_of(target)], target.at[block], sems.at[block]
            )
        ]
    half = depth // 2
    return [
        pltpu.make_async_copy(
            pieces[3 + part].at[:, : 2 * block_of(target)],
            target.at[3, pl.ds(part * half, half)],
            sems.at[3 + part],
        )
        for part in range(2)
    ]


def block_of(target):
    return target.shape[2] // 2


def mlp_kernel(
    quarter_ref, normed_ref, *refs
):
    pieces = refs[:5]
    down_ref, slope_ref, scale_ref, unit_ref, out_ref = refs[5:10]
    held, sems, down_sem = refs[10:]
    rows, depth = normed_ref.shape
    width = depth
    block = block_of(held)
    shard = depth // 4
    lines = block // 4
    wide = width // 3
    quarter = quarter_ref[0]
    copies = [weight_copies(pieces, held, sems, part, depth) for part in range(4)]
    for part in range(4):
        for copy in copies[part]:
            copy.start()
    for place in range(4):
        plane = quarter ^ place
        for part in range(4):
            target_row = pl.multiple_of(place * block + lines * (quarter ^ part), lines)
            for column in range(3):
                target = down_ref.at[
                    pl.ds(target_row, lines), column * wide : (column + 1) * wide
                ]
                taken = slice(2 * block, 2 * block + wide)
                if part < 3:
                    start = pl.multiple_of(shard * plane + lines * column, lines)
                    pltpu.make_async_copy(
                        pieces[part].at[pl.ds(start, lines), taken], target, down_sem
                    ).start()
                else:
                    inner = plane % 2
                    start = pl.multiple_of(shard * inner + lines * column, lines)
                    for half in range(2):

                        @pl.when(plane // 2 == half)
                        def _(half=half, start=start, target=target, taken=taken):
                            pltpu.make_async_copy(
                                pieces[3 + half].at[pl.ds(start, lines), taken], target, down_sem
                            ).start()

    step = rows // 2
    for part in range(4):
        for copy in copies[part]:
            copy.wait()

        def tile(index, carry, part=part):
            at = pl.ds(pl.multiple_of(index * step, step), step)
            normed = normed_ref[at, :]
            gate = dot_nn(normed, held[part, :, :block])
            up = dot_nn(normed, held[part, :, block:])
            sigmoid = 1.0 / (1.0 + jnp.exp(-gate))
            scale = gate * sigmoid
            cols = slice(part * block, (part + 1) * block)
            slope_ref[at, cols] = (up * sigmoid * (1.0 + gate * (1.0 - sigmoid))).astype(BF16)
            scale_ref[at, cols] = scale.astype(BF16)
            unit_ref[at, cols] = (scale * up).astype(BF16)
            return carry

        lax.fori_loop(0, 2, tile, 0)
    pltpu.make_async_copy(down_ref, down_ref, down_sem).wait()

    def finish(index, carry):
        at = pl.ds(pl.multiple_of(index * step, step), step)
        out_ref[at, :] = dot_nn(unit_ref[at, :], down_ref[...]).astype(BF16)
        return carry

    lax.fori_loop(0, 2, finish, 0)


def mlp(quarter, normed, pieces, block):
    rows, depth = normed.shape
    units = 4 * block
    return call(
        mlp_kernel,
        [
            shaped((units, depth), BF16),
            shaped((rows, units), BF16),
            shaped((rows, units), BF16),
            shaped((rows, units), BF16),
            shaped((rows, depth), BF16),
        ],
        (quarter, normed, *pieces),
        6 * rows * depth * units,
        56,
        in_specs=[SCALARS, WHOLE] + [FAR] * 5,
        scratch_shapes=[
            pltpu.VMEM((4, depth, 2 * block), BF16),
            pltpu.SemaphoreType.DMA((5,)),
            pltpu.SemaphoreType.DMA,
        ],
    )


def down_grad_kernel(where_ref, unit_ref, flow_ref, keep_ref, send_ref):
    quarter, row = where_ref[0], where_ref[1]
    block = unit_ref.shape[1] // 4
    half = block // 2
    for place in range(4):
        plane = quarter ^ place
        total = dot_tn(unit_ref[:, place * block : (place + 1) * block], flow_ref[...]).astype(
            BF16
        )
        for index in range(2):
            part = total[index * half : (index + 1) * half]

            @pl.when(row == index)
            def _(part=part, plane=plane):
                keep_ref[plane] = part

            @pl.when(row != index)
            def _(part=part, plane=plane):
                send_ref[plane] = part


def down_grad(where, unit, flow):
    rows, units = unit.shape
    width = flow.shape[1]
    half = units // 8
    return call(
        down_grad_kernel,
        [shaped((4, half, width), BF16)] * 2,
        (where, unit, flow),
        2 * rows * units * width,
        48,
        in_specs=[SCALARS, WHOLE, WHOLE],
    )


def mlp_back_kernel(flow_ref, normed_ref, slope_ref, scale_ref, down_ref, *refs):
    pieces = refs[:5]
    keep_ref, send_ref, out_ref = refs[5:8]
    held, total, unit_grad, sems = refs[8:]
    rows, depth = normed_ref.shape
    block = block_of(held)
    order = (2, 3, 0, 1)
    copies = [weight_copies(pieces, held, sems, part, depth) for part in range(4)]
    for part in order:
        for copy in copies[part]:
            copy.start()
    step = rows // 2
    for part in order:
        cols = slice(part * block, (part + 1) * block)

        def tile(index, carry, cols=cols):
            at = pl.ds(pl.multiple_of(index * step, step), step)
            grad = dot_nt(flow_ref[at, :], down_ref[cols, :])
            unit_grad[at, :block] = (grad * slope_ref[at, cols].astype(F32)).astype(BF16)
            unit_grad[at, block:] = (grad * scale_ref[at, cols].astype(F32)).astype(BF16)
            return carry

        lax.fori_loop(0, 2, tile, 0)
        target = send_ref if part >= 2 else keep_ref
        side = slice((part % 2) * 2 * block, (part % 2 + 1) * 2 * block)
        target[:, side] = dot_tn(normed_ref[...], unit_grad[...]).astype(BF16)
        for copy in copies[part]:
            copy.wait()

        def gather(index, carry, part=part):
            at = pl.ds(pl.multiple_of(index * step, step), step)
            value = dot_nt(unit_grad[at, :], held[part])
            if part == order[0]:
                total[at, :] = value
            elif part == order[-1]:
                out_ref[at, :] = (total[at, :] + value).astype(BF16)
            else:
                total[at, :] += value
            return carry

        lax.fori_loop(0, 2, gather, 0)


def mlp_back(flow, normed, slope, scale, down, pieces):
    rows, depth = normed.shape
    block = down.shape[0] // 4
    return call(
        mlp_back_kernel,
        [
            shaped((depth, 4 * block), BF16),
            shaped((depth, 4 * block), BF16),
            shaped((rows, depth), BF16),
        ],
        (flow, normed, slope, scale, down, *pieces),
        10 * rows * depth * 4 * block,
        60,
        in_specs=[WHOLE] * 5 + [FAR] * 5,
        scratch_shapes=[
            pltpu.VMEM((4, depth, 2 * block), BF16),
            pltpu.VMEM((rows, depth), F32),
            pltpu.VMEM((rows, 2 * block), BF16),
            pltpu.SemaphoreType.DMA((5,)),
        ],
    )


def place_kernel(fresh, where_ref, *refs):
    parts = refs[:6]
    outs = refs[6:] if fresh else refs[13:]
    pair, quarter = where_ref[0], where_ref[1]
    ff_mine, ff_other, down_mine, down_other, attn_mine, attn_other = parts
    query_out, key_out, value_out, out_out, gate_out, up_out, down_out = outs
    block = ff_mine.shape[2] // 4
    side, row = quarter // 2, quarter % 2
    for where_from, owner in ((ff_mine, pair), (ff_other, 1 - pair)):
        for index in range(2):
            for inner in range(2):
                plane = 2 * (side ^ index) + (row ^ inner)
                col = pl.multiple_of((2 * plane + owner) * block, block)
                low = 2 * inner * block
                gate_out[0, :, pl.ds(col, block)] = where_from[
                    index, :, low : low + block
                ].astype(F32)
                up_out[0, :, pl.ds(col, block)] = where_from[
                    index, :, low + block : low + 2 * block
                ].astype(F32)
    down_rows = down_mine.shape[0]
    for where_from, owner in ((down_mine, pair), (down_other, 1 - pair)):
        down_out[0, pl.ds(pl.multiple_of(owner * down_rows, down_rows), down_rows), :] = (
            where_from[...].astype(F32)
        )
    first = jnp.where(pair == 0, attn_mine[...], attn_other[...]).astype(F32)
    second = jnp.where(pair == 0, attn_other[...], attn_mine[...]).astype(F32)
    low = 0
    for out, cols in (
        (key_out, KEY_HALF),
        (value_out, KEY_HALF),
        (query_out, QUERY_HALF),
        (out_out, first.shape[1] - QKV),
    ):
        out[0] = jnp.concatenate([first[:, low : low + cols], second[:, low : low + cols]], axis=1)
        low += cols


def place(layer, where, parts, outs, held):
    ins = (where, *parts, *(held or ()))
    specs = [SCALARS] + [WHOLE] * len(parts) + [FAR] * len(held or ())

    def layer_block(out):
        return pl.BlockSpec((1, *out.shape[1:]), lambda _: (layer, 0, 0))

    aliases = {} if held is None else {1 + len(parts) + i: i for i in range(len(outs))}
    return call(
        functools.partial(place_kernel, held is None),
        outs,
        ins,
        0,
        60,
        in_specs=specs,
        out_specs=[layer_block(out) for out in outs],
        input_output_aliases=aliases,
        grid=(1,),
    )


def positions(deal_row, ctx_count):
    row_ids = jnp.arange(RUN, dtype=jnp.int32)
    block_ids = deal_row[..., None]
    lower_block = block_ids * HALF + row_ids
    upper_block = (2 * ctx_count - 1 - block_ids) * HALF + row_ids - HALF
    continued = 2 * HALF * ctx_count + row_ids - 2 * HALF
    return jnp.where(
        row_ids < HALF, lower_block, jnp.where(row_ids < 2 * HALF, upper_block, continued)
    )


def per_device(
    tokens,
    assign,
    cotangent,
    attn_gain,
    w_query,
    w_key,
    w_value,
    w_out,
    mlp_gain,
    w_gate,
    w_up,
    w_down,
):
    ctx_count = lax.axis_size("ctx")
    wt_count = lax.axis_size("wt")
    ctx_index = lax.axis_index("ctx")
    pair = ctx_index % 2
    side = (ctx_index // SIDE) % 2
    row = (ctx_index // ROW) % 2
    quarter = 2 * side + row
    chip = ctx_index // 2
    chip_count = ctx_count // 2
    outer_bits = [bit for bit in (8, 16, 32, 64, 128) if bit < ctx_count]

    layer_count, depth = attn_gain.shape[0], w_query.shape[1]
    width = w_out.shape[2]
    half_width = width // 2
    ff_block = w_down.shape[1] // 2
    ff_piece = ff_block // 4
    half_depth = depth // 2

    def flip(value, bit, axis="ctx", count=None):
        count = ctx_count if count is None else count
        return lax.ppermute(value, axis, [(i, i ^ bit) for i in range(count)])

    def ordered(bit_value, mine, other):
        first = jnp.where(bit_value == 0, mine, other)
        second = jnp.where(bit_value == 0, other, mine)
        return first, second

    def pair_rows(own):
        first, second = ordered(pair, own, flip(own, PAIR))
        cut = 2 * HALF
        return jnp.concatenate([first[cut:], second[cut:], first[:cut], second[:cut]], axis=0)

    def own_rows(both):
        return jnp.concatenate(
            [
                lax.dynamic_slice(both, (TAIL + 2 * HALF * pair, 0), (2 * HALF, width)),
                lax.dynamic_slice(both, (CONT * pair, 0), (CONT, width)),
            ],
            axis=0,
        )

    every_pos = positions(assign[0], ctx_count).reshape(chip_count, 2, RUN)
    wanted = chip ^ jnp.arange(chip_count, dtype=jnp.int32)
    picked = wanted[:, None] == jnp.arange(chip_count, dtype=jnp.int32)[None, :]
    prompt_pos = jnp.sum(
        jnp.where(picked[:, :, None, None], every_pos[None, :, :, : 2 * HALF], 0), axis=1
    )
    key_pos = prompt_pos.reshape(-1, 1)
    row_pos = prompt_pos[0].reshape(1, -1)
    cont_pos = every_pos[0, 0, 2 * HALF :]
    own_pos = jnp.concatenate([cont_pos, cont_pos, row_pos[0]])
    half_dim = HEAD_DIM // 2
    frequency = jnp.exp(jnp.arange(half_dim, dtype=F32) * (-jnp.log(10000.0) / half_dim))
    phase = frequency[:, None] * own_pos.astype(F32)[None, :]
    cosine, sine = jnp.cos(phase), jnp.sin(phase)

    gain_line = jnp.concatenate([attn_gain, mlp_gain]).reshape(1, -1)
    columns = QKV + half_width

    def attn_piece(layer):
        piece = jnp.concatenate(
            [
                lax.dynamic_slice(
                    weight[layer], (half_depth * row, cols * pair), (half_depth, cols)
                )
                for weight, cols in (
                    (w_key, KEY_HALF),
                    (w_value, KEY_HALF),
                    (w_query, QUERY_HALF),
                    (w_out, half_width),
                )
            ],
            axis=1,
        )
        if layer == 0:
            line = jnp.pad(gain_line, ((0, 15), (0, columns - gain_line.shape[1])))
            piece = jnp.concatenate([piece, line], axis=0)
        return piece

    def attn_weights(mine):
        other = flip(mine, ROW)
        mine, other = mine[:, :half_depth], other[:, :half_depth]
        first, second = ordered(row, mine, other)
        both = jnp.stack([first, second], axis=1).reshape(wt_count * depth, columns)
        qkv_w = both[:, :QKV]
        out_cols = both[:, QKV:]
        keep = lax.dynamic_slice(out_cols, (QUERY_HALF * pair, 0), (QUERY_HALF, half_width))
        send = lax.dynamic_slice(out_cols, (QUERY_HALF * (1 - pair), 0), (QUERY_HALF, half_width))
        out_w = jnp.concatenate(ordered(pair, keep, flip(send, PAIR)), axis=1)
        return qkv_w, out_w

    def mlp_piece(layer):
        col = 2 * ff_block * quarter + ff_block * pair
        low = ff_block * pair + ff_piece * quarter
        down = lax.dynamic_slice(w_down[layer], (low, 0), (ff_piece, width))
        wide = width // 3
        down = jnp.concatenate([down[:, i * wide : (i + 1) * wide] for i in range(3)], axis=0)
        return jnp.concatenate(
            [
                lax.dynamic_slice(w_gate[layer], (0, col), (depth, ff_block)),
                lax.dynamic_slice(w_up[layer], (0, col), (depth, ff_block)),
                down,
            ],
            axis=1,
        )

    def mlp_pieces(mine):
        half_rows = mine.shape[0] // 2
        by_row = flip(mine, ROW)
        by_side = flip(mine, SIDE)
        return (
            mine,
            by_row,
            by_side,
            flip(by_row[:half_rows], SIDE),
            flip(by_side[half_rows:], ROW),
        )

    where = jnp.stack([pair, quarter])
    spot = jnp.stack([quarter, row])
    quarter_id = quarter[None]

    residual = pair_rows(tokens[0]).astype(F32)
    parts = ()
    saved_layers = []
    gains = None
    for layer in range(layer_count):
        gathered = lax.all_gather(attn_piece(layer), "wt", axis=0, tiled=False)
        if layer == 0:
            lines = gathered[:, half_depth, : gain_line.shape[1]].astype(F32)
            gains = (
                lines.reshape(wt_count, 2 * layer_count, depth)
                .transpose(1, 0, 2)
                .reshape(2 * layer_count, 1, wt_count * depth)
            )
        qkv_w, out_w = attn_weights(gathered)
        pieces = mlp_pieces(lax.all_gather(mlp_piece(layer), "wt", axis=0, tiled=True))
        gain_attn, gain_mlp = gains[layer], gains[layer_count + layer]
        residual, normed_attn = add_norm(residual, parts, gain_attn)
        query, key_value, key_value_turned = rope(dot_tt(qkv_w, normed_attn), cosine, sine)
        shared = key_value[TAIL:]
        for bit in [SIDE, ROW] + outer_bits:
            shared = jnp.concatenate([shared, flip(shared, bit)], axis=0)
        attended, lse = attend(query, key_value, key_value_turned, shared, key_pos, row_pos)
        part = dot_tn(attended, out_w).astype(BF16)
        residual_mid, normed_mlp = add_norm(residual, (part, flip(part, PAIR)), gain_mlp)
        down_w, slope, scale, unit, part = mlp(quarter_id, normed_mlp, pieces, ff_block)
        parts = (part, flip(part, PAIR))
        saved_layers.append(
            (
                qkv_w,
                out_w,
                pieces,
                down_w,
                gain_attn,
                gain_mlp,
                residual,
                normed_attn,
                query,
                key_value,
                key_value_turned,
                shared,
                lse,
                attended,
                residual_mid,
                normed_mlp,
                slope,
                scale,
                unit,
            )
        )
        residual = residual_mid
    residual = residual + (parts[0].astype(F32) + parts[1].astype(F32))
    layer_out = own_rows(residual)

    def outer_sum(total):
        for bit in outer_bits:
            total = total.astype(BF16)
            total = total.astype(F32) + flip(total, bit).astype(F32)
        return total.astype(BF16)

    flow = pair_rows(cotangent[0])
    flow, flow_low = flow.astype(F32), flow
    gain_grads = [None] * (2 * layer_count)
    outs = [
        shaped((layer_count, *weight.shape[1:]), F32)
        for weight in (w_query, w_key, w_value, w_out, w_gate, w_up, w_down)
    ]
    held = None
    for layer in reversed(range(layer_count)):
        (
            qkv_w,
            out_w,
            pieces,
            down_w,
            gain_attn,
            gain_mlp,
            residual,
            normed_attn,
            query,
            key_value,
            key_value_turned,
            shared,
            lse,
            attended,
            residual_mid,
            normed_mlp,
            slope,
            scale,
            unit,
        ) = saved_layers[layer]
        keep, send = down_grad(spot, unit, flow_low)
        down_sum = (keep.astype(F32) + flip(send, ROW).astype(F32)).astype(BF16)
        down_share = lax.psum_scatter(down_sum, "wt", scatter_dimension=0, tiled=False)
        keep, send, part = mlp_back(flow_low, normed_mlp, slope, scale, down_w, pieces)
        ff_sum = (keep.astype(F32) + flip(send, SIDE).astype(F32)).astype(BF16)
        ff_share = lax.psum_scatter(ff_sum, "wt", scatter_dimension=0, tiled=True)
        flow, flow_low, gain_grads[layer_count + layer] = norm_back(
            flow, (part, flip(part, PAIR)), residual_mid, gain_mlp
        )
        attended_grad = dot_nt(out_w, flow_low).astype(BF16)
        query_grad, own_grad, shared_grad = attend_back(
            query,
            attended_grad,
            key_value,
            key_value_turned,
            shared,
            key_pos,
            row_pos,
            lse,
            cosine,
            sine,
        )
        for bit in reversed([SIDE, ROW] + outer_bits):
            half = shared_grad.shape[0] // 2
            arrived = flip(shared_grad[half:].astype(BF16), bit)
            shared_grad = shared_grad[:half] + arrived.astype(F32)
        grad_qkv = merge(query_grad, own_grad, shared_grad, cosine, sine)
        part = dot_nt(grad_qkv, qkv_w).astype(BF16)
        flow, flow_low_next, gain_grads[layer] = norm_back(
            flow, (part, flip(part, PAIR)), residual, gain_attn
        )
        qkv_part = dot_tn(normed_attn, grad_qkv).astype(BF16)
        out_part = dot_nn(attended, flow_low).astype(BF16)
        flow_low = flow_low_next
        attn_sums = []
        for whole_part in (qkv_part, out_part):
            split = whole_part.reshape(-1, 2, half_depth, whole_part.shape[1])
            kept = lax.dynamic_index_in_dim(split, row, 1, keepdims=False)
            sent = lax.dynamic_index_in_dim(split, 1 - row, 1, keepdims=False)
            attn_sums.append((kept.astype(F32) + flip(sent, ROW).astype(F32)).astype(BF16))
        qkv_sum, out_sum = attn_sums
        kept = lax.dynamic_slice(
            out_sum, (0, 0, half_width * pair), (wt_count // 2, half_depth, half_width)
        )
        sent = lax.dynamic_slice(
            out_sum, (0, 0, half_width * (1 - pair)), (wt_count // 2, half_depth, half_width)
        )
        out_all = jnp.concatenate(ordered(pair, kept, flip(sent, PAIR)), axis=0)
        attn_share = lax.psum_scatter(
            jnp.concatenate([qkv_sum, out_all], axis=2), "wt", scatter_dimension=0, tiled=False
        )

        swapped = flip(ff_share, ROW)
        cut = 2 * ff_block
        swapped = jnp.concatenate([swapped[:, cut:], swapped[:, :cut]], axis=1)
        ff_total = outer_sum(ff_share.astype(F32) + swapped.astype(F32))
        ff_mine = jnp.stack([ff_total, flip(ff_total, SIDE)])
        ff_other = flip(ff_mine, PAIR)
        placed = [ff_mine, ff_other]
        for share in (down_share, attn_share):
            total = outer_sum(share.astype(F32) + flip(share, SIDE).astype(F32))
            joined = jnp.concatenate(ordered(row, total, flip(total, ROW)), axis=0)
            placed += [joined, flip(joined, PAIR)]
        held = place(layer, where, placed, outs, held)
    token_grad = own_rows(flow)

    gain_total = jnp.concatenate(gain_grads, axis=0)
    for bit in [SIDE, ROW] + outer_bits:
        gain_total = gain_total + flip(gain_total, bit)
    bit = 1
    while bit < wt_count:
        gain_total = gain_total + flip(gain_total, bit, "wt", wt_count)
        bit *= 2
    gain_share = lax.dynamic_slice(
        gain_total, (0, lax.axis_index("wt") * depth), (2 * layer_count, depth)
    )
    query_out, key_out, value_out, out_out, gate_out, up_out, down_out = held
    return (
        layer_out[None],
        token_grad[None],
        gain_share[:layer_count],
        query_out,
        key_out,
        value_out,
        out_out,
        gain_share[layer_count:],
        gate_out,
        up_out,
        down_out,
    )


def solution(mesh):
    weight = P(None, "wt", None)
    return jax.shard_map(
        per_device,
        mesh=mesh,
        in_specs=(
            P("wt", "ctx", None),
            P("wt", None),
            P("wt", "ctx", None),
            P(None, "wt"),
            weight,
            weight,
            weight,
            weight,
            P(None, "wt"),
            weight,
            weight,
            weight,
        ),
        out_specs=(
            P("wt", "ctx", None),
            P("wt", "ctx", None),
            P(None, "wt"),
            weight,
            weight,
            weight,
            weight,
            P(None, "wt"),
            weight,
            weight,
            weight,
        ),
        check_vma=False,
    )
```

time: 2630 us -> 1020 us (0.39)
  waiting for transfers between devices: 1990 us -> 551 us
  matrix products: 270 us -> 31.1 us
  Pallas kernels: 0 us -> 216 us
  blocking collectives: 205 us -> 0 us
  starting transfers between devices: 1.98 us -> 42.8 us
    reduce_scatter x14 -> x6, waiting for transfers between devices: 1010 us -> 0.01 us  [the longest x2 0.01 us: per_device(): lax.psum_scatter(down_sum, 'wt', scatter_dimension=0, tiled=False)]
    all_gather x10 -> x4, waiting for transfers between devices: 736 us -> 80.5 us  [the longest x2 46.7 us: per_device(): lax.all_gather(mlp_piece(layer), 'wt', axis=0, tiled=True)]
    ppermute x0 -> x62, waiting for transfers between devices: none -> 470 us  [flip(): return lax.ppermute(value, axis, [(i, i ^ bit) for i in range(count)])]
    dot_general x114 -> x12, matrix products: 270 us -> 31.1 us  [the longest x4 12.3 us: dot_nt(): lax.dot_general(left, right, (((1,), (1,)), ((), ())), preferred_element_...]
    pallas_call x0 -> x24, Pallas kernels: none -> 216 us  [call(): pl.pallas_call(kernel, out_shape=outs, in_specs=in_specs or [WHOLE] * len...]
    psum x1 -> x0, waiting for transfers between devices: 153 us -> none  [per_device(): lax.psum(group_part[1].astype(jnp.bfloat16), 'ctx').astype(jnp.float32)]
    all_gather x8 -> x0, blocking collectives: 153 us -> none  [the longest x2 63.5 us: per_device(): lax.all_gather(w_value[layer_index], 'wt', axis=0, tiled=True)]
    unnamed x33 -> x10, waiting for transfers between devices: 91.9 us -> 0.16 us
  transfers between devices with their start and end apart: 29 -> 72, of which waited for: 25 -> 34; matrix products, arithmetic and copies ran while one was open for 9% -> 13% of each run, Pallas kernels for 0% -> 16%
where the time goes in v1:
time: 1020 us
  waiting for transfers between devices  551 us (54%)
  Pallas kernels  216 us (21%)
  local copies, waits for them, and re-layouts  99.2 us (10%)
  other arithmetic  61.5 us (6%)
  starting transfers between devices  42.8 us (4%)
  matrix products  31.1 us (3%)
  between operations  16.3 us (2%)
    ppermute x62, waiting for transfers between devices, flip(): return lax.ppermute(value, axis, [(i, i ^ bit) for i in range(count)])  470 us
    pallas_call x24, Pallas kernels, call(): pl.pallas_call(kernel, out_shape=outs, in_specs=in_specs or [WHOLE] * len...  216 us
    unnamed x228, local copies, waits for them, and re-layouts  49.6 us
    all_gather x2, waiting for transfers between devices, per_device(): lax.all_gather(mlp_piece(layer), 'wt', axis=0, tiled=True)  46.7 us
    ppermute x62, starting transfers between devices, flip(): return lax.ppermute(value, axis, [(i, i ^ bit) for i in range(count)])  42 us
    all_gather x2, waiting for transfers between devices, per_device(): gathered = lax.all_gather(attn_piece(layer), 'wt', axis=0, tiled=False)  33.8 us
  transfers between devices with their start and end apart: 72, of which 34 were waited for; matrix products, arithmetic and copies ran while one was open for 13% of the time, Pallas kernels for 16%

profile of v1, /device:TPU:0, one launch (start us, length us, event | category | flops | bytes accessed | tf_op | source)
XLA Modules:
  0.0 1018.2 jit_solution(10610117035868440315)
XLA Ops:
  26.4 33.8 %all-gather.11.cloned.1.call-done = bf16[640,1536]{1,0:T(8,128)(2,1)} async-done(((bf16[160,1536]{1,0:T(8,128)(2,1)}), bf16[640,1536]{1,0:T(8,128)(2,1)}) %all-gather.11.cloned.1.call-update) | async-done | bytes 1966096 | tf_op jit(solution)/shard_map/all_gather | solution.py:827
  69.9 46.6 %all-gather.7.cloned.1.call-done.refs_0_ = bf16[1152,1152]{1,0:T(8,128)(2,1)} async-done(((bf16[288,1152]{1,0:T(8,128)(2,1)}), bf16[1152,1152]{1,0:T(8,128)(2,1)}) %all-gather.7.cloned.1.call-update) | async-done | bytes 2654224 | tf_op jit(solution)/shard_map/all_gather | solution.py:836
  130.2 49.1 %collective-permute-done.2 = bf16[128,384]{1,0:T(8,128)(2,1)S(1)} collective-permute-done((bf16[128,384]{1,0:T(8,128)(2,1)S(1)}, bf16[128,384]{1,0:T(8,128)(2,1)S(1)}, u32[]{:S(2)}, u32[]{:S(2)}) %collective-permute-start.2) | collective-permute-done | bytes 98336 | tf_op jit(solution)/shard_map/ppermute | solution.py:720
  190.4 11.8 %shard_map.205 = (bf16[576,640]{1,0:T(8,128)(2,1)S(1)}, f32[9,1,640]{2,1,0:T(1,128)S(1)}) custom-call(bf16[576,640]{1,0:T(8,128)(2,1)S(1)} %copy-done.57, bf16[640,384]{1,0:T(8,128)(2,1)S(1)} %copy-done.47, bf16[384,640]{1,0:T(8,128)(2,1)S(1)} %copy-done.60, bf16[512,384]{1,0:T(8,128)(2,1)S(1)} %pad_maximum_fusion.15.shared_ref, s32[512,1]{1,0:T(8,128)S(1)} %copy-done.42, ...), custom_call_target="tpu_custom_call" | custom-call | flops 1132462080 | bytes 2876416 | tf_op jit(solution)/shard_map/pallas_call | solution.py:66
  221.8 19.2 %collective-permute-done.8.refs_3_ = bf16[576,1152]{1,0:T(8,128)(2,1)} collective-permute-done((bf16[576,1152]{1,0:T(8,128)(2,1)}, bf16[576,1152]{1,0:T(8,128)(2,1)}, u32[]{:S(2)}, u32[]{:S(2)}) %collective-permute-start.8) | collective-permute-done | bytes 1327136 | tf_op jit(solution)/shard_map/ppermute | solution.py:720
  245.4 18.3 %shard_map.207 = (bf16[1536,1152]{1,0:T(8,128)(2,1)}, bf16[640,1536]{1,0:T(8,128)(2,1)}, bf16[640,1536]{1,0:T(8,128)(2,1)}, bf16[640,1536]{1,0:T(8,128)(2,1)}, bf16[640,1152]{1,0:T(8,128)(2,1)}) custom-call(s32[1]{0:T(128)} %bitcast.12.quarter_ref, bf16[640,1152]{1,0:T(8,128)(2,1)} %copy-done.49, bf16[1152,1152]{1,0:T(8,128)(2,1)} %all-gather.7.cloned.1.call-done.refs_0_, ...), custom_call_target="tpu_custom_call" | custom-call | flops 6794772480 | bytes 23003140 | tf_op jit(solution)/shard_map/pallas_call | solution.py:66
  265.1 18.3 %collective-permute-done.11 = bf16[4,144,1536]{2,1,0:T(8,128)(2,1)} collective-permute-done((bf16[4,144,1536]{2,1,0:T(8,128)(2,1)}, bf16[4,144,1536]{2,1,0:T(8,128)(2,1)}, u32[]{:S(2)}, u32[]{:S(2)}) %collective-permute-start.11) | collective-permute-done | bytes 1769504 | tf_op jit(solution)/shard_map/ppermute | solution.py:720
  301.7 24.8 %collective-permute-done.12 = bf16[128,384]{1,0:T(8,128)(2,1)S(1)} collective-permute-done((bf16[128,384]{1,0:T(8,128)(2,1)S(1)}, bf16[128,384]{1,0:T(8,128)(2,1)S(1)}, u32[]{:S(2)}, u32[]{:S(2)}) %collective-permute-start.12) | collective-permute-done | bytes 98336 | tf_op jit(solution)/shard_map/ppermute | solution.py:720
  329.4 14.2 %collective-permute-done.13 = bf16[256,384]{1,0:T(8,128)(2,1)S(1)} collective-permute-done((bf16[256,384]{1,0:T(8,128)(2,1)S(1)}, bf16[256,384]{1,0:T(8,128)(2,1)S(1)}, u32[]{:S(2)}, u32[]{:S(2)}) %collective-permute-start.13) | collective-permute-done | bytes 196640 | tf_op jit(solution)/shard_map/ppermute | solution.py:720
  343.7 11.9 %shard_map.210 = (bf16[576,640]{1,0:T(8,128)(2,1)S(1)}, f32[9,1,640]{2,1,0:T(1,128)S(1)}) custom-call(bf16[576,640]{1,0:T(8,128)(2,1)S(1)} %get-tuple-element.87.query_ref, bf16[640,384]{1,0:T(8,128)(2,1)S(1)} %get-tuple-element.88.kv_ref, bf16[384,640]{1,0:T(8,128)(2,1)S(1)} %get-tuple-element.89.kv_turned_ref, ...), custom_call_target="tpu_custom_call" | custom-call | flops 1132462080 | bytes 2876416 | tf_op jit(solution)/shard_map/pallas_call | solution.py:66
  375.8 16.9 %collective-permute-done.18.refs_3_ = bf16[576,1152]{1,0:T(8,128)(2,1)} collective-permute-done((bf16[576,1152]{1,0:T(8,128)(2,1)}, bf16[576,1152]{1,0:T(8,128)(2,1)}, u32[]{:S(2)}, u32[]{:S(2)}) %collective-permute-start.18) | collective-permute-done | bytes 1327136 | tf_op jit(solution)/shard_map/ppermute | solution.py:720
  395.6 17.8 %shard_map.212 = (bf16[1536,1152]{1,0:T(8,128)(2,1)}, bf16[640,1536]{1,0:T(8,128)(2,1)}, bf16[640,1536]{1,0:T(8,128)(2,1)}, bf16[640,1536]{1,0:T(8,128)(2,1)}, bf16[640,1152]{1,0:T(8,128)(2,1)}) custom-call(s32[1]{0:T(128)} %bitcast.12.quarter_ref, bf16[640,1152]{1,0:T(8,128)(2,1)} %copy-done.55, bf16[1152,1152]{1,0:T(8,128)(2,1)} %all-gather.9.cloned.1.call-done.refs_0_, ...), custom_call_target="tpu_custom_call" | custom-call | flops 6794772480 | bytes 23003140 | tf_op jit(solution)/shard_map/pallas_call | solution.py:66
  413.3 24.9 %shard_map.213 = (bf16[1152,1536]{1,0:T(8,128)(2,1)}, bf16[1152,1536]{1,0:T(8,128)(2,1)}, bf16[640,1152]{1,0:T(8,128)(2,1)}) custom-call(bf16[640,1152]{1,0:T(8,128)(2,1)} %get-tuple-element.165.flow_ref, bf16[640,1152]{1,0:T(8,128)(2,1)} %copy-done.55, bf16[640,1536]{1,0:T(8,128)(2,1)} %get-tuple-element.94.slope_ref, ...), custom_call_target="tpu_custom_call" | custom-call | flops 11324620800 | bytes 29589504 | tf_op jit(solution)/shard_map/pallas_call | solution.py:66
  439.7 7.1 shard_map.224
  461.8 27.5 %collective-permute-done.52 = bf16[4,192,1152]{2,1,0:T(8,128)(2,1)} collective-permute-done((bf16[4,192,1152]{2,1,0:T(8,128)(2,1)}, bf16[4,192,1152]{2,1,0:T(8,128)(2,1)}, u32[]{:S(2)}, u32[]{:S(2)}) %collective-permute-start.52) | collective-permute-done | bytes 1769504 | tf_op jit(solution)/shard_map/ppermute | solution.py:720
  492.6 22.9 %shard_map.215 = (bf16[576,640]{1,0:T(8,128)(2,1)}, f32[512,384]{1,0:T(8,128)}, f32[512,384]{1,0:T(8,128)}) custom-call(bf16[576,640]{1,0:T(8,128)(2,1)} %copy-done.58, bf16[576,640]{1,0:T(8,128)(2,1)} %convolution_convert_fusion.9.grad_ref, bf16[640,384]{1,0:T(8,128)(2,1)} %copy-done.48, bf16[384,640]{1,0:T(8,128)(2,1)} %copy-done.61, ...), custom_call_target="tpu_custom_call" | custom-call | flops 2831155200 | bytes 5350400 | tf_op jit(solution)/shard_map/pallas_call | solution.py:66
  548.2 18.2 %collective-permute-done.56 = bf16[4,144,960]{2,1,0:T(8,128)(2,1)S(1)} collective-permute-done((bf16[4,144,960]{2,1,0:T(8,128)(2,1)S(1)}, bf16[4,144,960]{2,1,0:T(8,128)(2,1)S(1)}, u32[]{:S(2)}, u32[]{:S(2)}) %collective-permute-start.56) | collective-permute-done | bytes 1105952 | tf_op jit(solution)/shard_map/ppermute | solution.py:720
  578.6 6.7 shard_map.223
  586.5 37.9 %collective-permute-done.38 = bf16[4,192,1152]{2,1,0:T(8,128)(2,1)S(1)} collective-permute-done((bf16[4,192,1152]{2,1,0:T(8,128)(2,1)S(1)}, bf16[4,192,1152]{2,1,0:T(8,128)(2,1)S(1)}, u32[]{:S(2)}, u32[]{:S(2)}) %collective-permute-start.38) | collective-permute-done | bytes 1769504 | tf_op jit(solution)/shard_map/ppermute | solution.py:720
  626.1 36.9 %collective-permute-done.48 = bf16[1152,1536]{1,0:T(8,128)(2,1)} collective-permute-done((bf16[1152,1536]{1,0:T(8,128)(2,1)}, bf16[1152,1536]{1,0:T(8,128)(2,1)}, u32[]{:S(2)}, u32[]{:S(2)}) %collective-permute-start.48) | collective-permute-done | bytes 3538976 | tf_op jit(solution)/shard_map/ppermute | solution.py:720
  669.0 24.5 %shard_map.218 = (bf16[1152,1536]{1,0:T(8,128)(2,1)}, bf16[1152,1536]{1,0:T(8,128)(2,1)}, bf16[640,1152]{1,0:T(8,128)(2,1)}) custom-call(bf16[640,1152]{1,0:T(8,128)(2,1)} %copy-done.52, bf16[640,1152]{1,0:T(8,128)(2,1)} %copy-done.49, bf16[640,1536]{1,0:T(8,128)(2,1)} %get-tuple-element.106.slope_ref, bf16[640,1536]{1,0:T(8,128)(2,1)} %get-tuple-element.107.scale_ref, ...), custom_call_target="tpu_custom_call" | custom-call | flops 11324620800 | bytes 29589504 | tf_op jit(solution)/shard_map/pallas_call | solution.py:66
  693.8 75.9 %collective-permute-done.34 = bf16[1152,1536]{1,0:T(8,128)(2,1)S(1)} collective-permute-done((bf16[1152,1536]{1,0:T(8,128)(2,1)}, bf16[1152,1536]{1,0:T(8,128)(2,1)S(1)}, u32[]{:S(2)}, u32[]{:S(2)}) %collective-permute-start.34) | collective-permute-done | bytes 3538976 | tf_op jit(solution)/shard_map/ppermute | solution.py:720
  786.6 22.9 %shard_map.220 = (bf16[576,640]{1,0:T(8,128)(2,1)}, f32[512,384]{1,0:T(8,128)}, f32[512,384]{1,0:T(8,128)}) custom-call(bf16[576,640]{1,0:T(8,128)(2,1)} %copy-done.56, bf16[576,640]{1,0:T(8,128)(2,1)} %convolution_convert_fusion.8.grad_ref, bf16[640,384]{1,0:T(8,128)(2,1)} %copy-done.46, bf16[384,640]{1,0:T(8,128)(2,1)} %copy-done.59, ...), custom_call_target="tpu_custom_call" | custom-call | flops 2831155200 | bytes 5350400 | tf_op jit(solution)/shard_map/pallas_call | solution.py:66
  847.6 16.0 %collective-permute-done.42 = bf16[4,144,960]{2,1,0:T(8,128)(2,1)} collective-permute-done((bf16[4,144,960]{2,1,0:T(8,128)(2,1)}, bf16[4,144,960]{2,1,0:T(8,128)(2,1)}, u32[]{:S(2)}, u32[]{:S(2)}) %collective-permute-start.42) | collective-permute-done | bytes 1105952 | tf_op jit(solution)/shard_map/ppermute | solution.py:720
  886.1 9.9 collective-permute-done.59
  917.5 11.8 %collective-permute-done.49 = bf16[288,1536]{1,0:T(8,128)(2,1)} collective-permute-done((bf16[288,1536]{1,0:T(8,128)(2,1)}, bf16[288,1536]{1,0:T(8,128)(2,1)}, u32[]{:S(2)}, u32[]{:S(2)}) %collective-permute-start.49) | collective-permute-done | bytes 884768 | tf_op jit(solution)/shard_map/ppermute | solution.py:720
  931.7 16.7 %collective-permute-done.35 = bf16[288,1536]{1,0:T(8,128)(2,1)} collective-permute-done((bf16[288,1536]{1,0:T(8,128)(2,1)}, bf16[288,1536]{1,0:T(8,128)(2,1)}, u32[]{:S(2)}, u32[]{:S(2)}) %collective-permute-start.35) | collective-permute-done | bytes 884768 | tf_op jit(solution)/shard_map/ppermute | solution.py:720
  950.6 6.0 collective-permute-done.40
  960.0 10.9 %collective-permute-done.50 = bf16[288,1536]{1,0:T(8,128)(2,1)S(1)} collective-permute-done((bf16[288,1536]{1,0:T(8,128)(2,1)S(1)}, bf16[288,1536]{1,0:T(8,128)(2,1)S(1)}, u32[]{:S(2)}, u32[]{:S(2)}) %collective-permute-start.50) | collective-permute-done | bytes 884768 | tf_op jit(solution)/shard_map/ppermute | solution.py:720
  971.2 15.5 %collective-permute-done.36 = bf16[288,1536]{1,0:T(8,128)(2,1)S(1)} collective-permute-done((bf16[288,1536]{1,0:T(8,128)(2,1)S(1)}, bf16[288,1536]{1,0:T(8,128)(2,1)S(1)}, u32[]{:S(2)}, u32[]{:S(2)}) %collective-permute-start.36) | collective-permute-done | bytes 884768 | tf_op jit(solution)/shard_map/ppermute | solution.py:720
  994.1 8.5 shard_map.225
  1002.6 8.5 shard_map.226
  (529 shorter events, 309.9 us)
Async XLA Ops:
  7.2 53.0 %all-gather.11.cloned.1.call-start = ((), (), s32[]{:S(2)}) async-start(), calls=%async_computation.14 | async-start | bytes 2457600 | tf_op jit(solution)/shard_map/all_gather | solution.py:827
  13.7 102.8 %all-gather.7.cloned.1.call-start = ((), (), s32[]{:S(2)}) async-start(), calls=%async_computation.6 | async-start | bytes 3317760 | tf_op jit(solution)/shard_map/all_gather | solution.py:836
  20.8 192.9 %all-gather.13.cloned.1.call-start = ((), (), s32[]{:S(2)}) async-start(), calls=%async_computation.15 | async-start | bytes 2211840 | tf_op jit(solution)/shard_map/all_gather | solution.py:827
  23.2 240.6 %all-gather.9.cloned.1.call-start = ((), (), s32[]{:S(2)}) async-start(), calls=%async_computation.7 | async-start | bytes 3317760 | tf_op jit(solution)/shard_map/all_gather | solution.py:836
  23.3 39.6 %collective-permute-start = (bf16[320,1152]{1,0:T(8,128)(2,1)}, bf16[320,1152]{1,0:T(8,128)(2,1)}, u32[]{:S(2)}, u32[]{:S(2)}) collective-permute-start(bf16[320,1152]{1,0:T(8,128)(2,1)} %bitcast.141), channel_id=1, source_target_pairs={{0,4},{4,0},{8,12},{12,8},{16,20},{20,16},{24,28},{28,24},{1,5},{5... | collective-permute-start | bytes 2211848 | tf_op jit(solution)/shard_map/ppermute | solution.py:720
  23.7 39.1 %collective-permute-start.21 = (bf16[320,1152]{1,0:T(8,128)(2,1)}, bf16[320,1152]{1,0:T(8,128)(2,1)}, u32[]{:S(2)}, u32[]{:S(2)}) collective-permute-start(bf16[320,1152]{1,0:T(8,128)(2,1)} %bitcast.140), channel_id=1, source_target_pairs={{0,4},{4,0},{8,12},{12,8},{16,20},{20,16},{24,28},{28,24},{1,5},{5... | collective-permute-start | bytes 2211848 | tf_op jit(solution)/shard_map/ppermute | solution.py:720
  25.8 809.9 %reduce-scatter.15.cloned.1.call-start = ((), (), s32[]{:S(2)}) async-start(), calls=%async_computation.12 | async-start | bytes 2211840 | tf_op jit(solution)/shard_map/reduce_scatter | solution.py:913
  60.2 59.3 %collective-permute-start.1 = (bf16[4,160,1536]{2,1,0:T(8,128)(2,1)}, bf16[4,160,1536]{2,1,0:T(8,128)(2,1)}, u32[]{:S(2)}, u32[]{:S(2)}) collective-permute-start(bf16[4,160,1536]{2,1,0:T(8,128)(2,1)} %bitcast.131), channel_id=1, source_target_pairs={{0,16},{4,20},{8,24},{12,28},{16,0},{20,4},{24,8},{28,12},{1,17},{... | collective-permute-start | bytes 5898248 | tf_op jit(solution)/shard_map/ppermute | solution.py:720
  116.6 90.1 %collective-permute-start.6 = (bf16[1152,1152]{1,0:T(8,128)(2,1)}, bf16[1152,1152]{1,0:T(8,128)(2,1)}, u32[]{:S(2)}, u32[]{:S(2)}) collective-permute-start(bf16[1152,1152]{1,0:T(8,128)(2,1)} %all-gather.7.cloned.1.call-done.refs_0_), channel_id=1, source_target_pairs={{0,16},{4,20},{8,24},{12,28},{16,0},{20,4},{24,8},{28,12},{1,17},{... | collective-permute-start | bytes 7962632 | tf_op jit(solution)/shard_map/ppermute | solution.py:720
  118.0 92.7 %collective-permute-start.7 = (bf16[1152,1152]{1,0:T(8,128)(2,1)}, bf16[1152,1152]{1,0:T(8,128)(2,1)}, u32[]{:S(2)}, u32[]{:S(2)}) collective-permute-start(bf16[1152,1152]{1,0:T(8,128)(2,1)} %all-gather.7.cloned.1.call-done.refs_0_), channel_id=1, source_target_pairs={{0,8},{4,12},{8,0},{12,4},{16,24},{20,28},{24,16},{28,20},{1,9},{5... | collective-permute-start | bytes 7962632 | tf_op jit(solution)/shard_map/ppermute | solution.py:720
  124.1 78.1 %collective-permute-start.4 = (bf16[576,576]{1,0:T(8,128)(2,1)}, bf16[576,576]{1,0:T(8,128)(2,1)}, u32[]{:S(2)}, u32[]{:S(2)}) collective-permute-start(bf16[576,576]{1,0:T(8,128)(2,1)} %constant_dynamic-slice_fusion.9), channel_id=1, source_target_pairs={{0,4},{4,0},{8,12},{12,8},{16,20},{20,16},{24,28},{28,24},{1,5},{5... | collective-permute-start | bytes 1990664 | tf_op jit(solution)/shard_map/ppermute | solution.py:720
  129.7 49.6 %collective-permute-start.2 = (bf16[128,384]{1,0:T(8,128)(2,1)S(1)}, bf16[128,384]{1,0:T(8,128)(2,1)S(1)}, u32[]{:S(2)}, u32[]{:S(2)}) collective-permute-start(bf16[128,384]{1,0:T(8,128)(2,1)S(1)} %slice.210), channel_id=1, source_target_pairs={{0,8},{4,12},{8,0},{12,4},{16,24},{20,28},{24,16},{28,20},{1,9},{5... | collective-permute-start | bytes 294920 | tf_op jit(solution)/shard_map/ppermute | solution.py:720
  213.1 32.3 %collective-permute-start.9 = (bf16[576,1152]{1,0:T(8,128)(2,1)}, bf16[576,1152]{1,0:T(8,128)(2,1)}, u32[]{:S(2)}, u32[]{:S(2)}) collective-permute-start(bf16[576,1152]{1,0:T(8,128)(2,1)} %slice.274), channel_id=1, source_target_pairs={{0,16},{4,20},{8,24},{12,28},{16,0},{20,4},{24,8},{28,12},{1,17},{... | collective-permute-start | bytes 3981320 | tf_op jit(solution)/shard_map/ppermute | solution.py:720
  213.8 69.6 %collective-permute-start.11 = (bf16[4,144,1536]{2,1,0:T(8,128)(2,1)}, bf16[4,144,1536]{2,1,0:T(8,128)(2,1)}, u32[]{:S(2)}, u32[]{:S(2)}) collective-permute-start(bf16[4,144,1536]{2,1,0:T(8,128)(2,1)} %bitcast.129), channel_id=1, source_target_pairs={{0,16},{4,20},{8,24},{12,28},{16,0},{20,4},{24,8},{28,12},{1,17},{... | collective-permute-start | bytes 5308424 | tf_op jit(solution)/shard_map/ppermute | solution.py:720
  263.8 94.5 %collective-permute-start.16 = (bf16[1152,1152]{1,0:T(8,128)(2,1)}, bf16[1152,1152]{1,0:T(8,128)(2,1)}, u32[]{:S(2)}, u32[]{:S(2)}) collective-permute-start(bf16[1152,1152]{1,0:T(8,128)(2,1)} %all-gather.9.cloned.1.call-done.refs_0_), channel_id=1, source_target_pairs={{0,16},{4,20},{8,24},{12,28},{16,0},{20,4},{24,8},{28,12},{1,17},{... | collective-permute-start | bytes 7962632 | tf_op jit(solution)/shard_map/ppermute | solution.py:720
  264.5 96.9 %collective-permute-start.17 = (bf16[1152,1152]{1,0:T(8,128)(2,1)}, bf16[1152,1152]{1,0:T(8,128)(2,1)}, u32[]{:S(2)}, u32[]{:S(2)}) collective-permute-start(bf16[1152,1152]{1,0:T(8,128)(2,1)} %all-gather.9.cloned.1.call-done.refs_0_), channel_id=1, source_target_pairs={{0,8},{4,12},{8,0},{12,4},{16,24},{20,28},{24,16},{28,20},{1,9},{5... | collective-permute-start | bytes 7962632 | tf_op jit(solution)/shard_map/ppermute | solution.py:720
  288.4 39.5 %collective-permute-start.14 = (bf16[576,576]{1,0:T(8,128)(2,1)}, bf16[576,576]{1,0:T(8,128)(2,1)}, u32[]{:S(2)}, u32[]{:S(2)}) collective-permute-start(bf16[576,576]{1,0:T(8,128)(2,1)} %constant_dynamic-slice_fusion.8), channel_id=1, source_target_pairs={{0,4},{4,0},{8,12},{12,8},{16,20},{20,16},{24,28},{28,24},{1,5},{5... | collective-permute-start | bytes 1990664 | tf_op jit(solution)/shard_map/ppermute | solution.py:720
  360.8 31.8 %collective-permute-start.18 = (bf16[576,1152]{1,0:T(8,128)(2,1)}, bf16[576,1152]{1,0:T(8,128)(2,1)}, u32[]{:S(2)}, u32[]{:S(2)}) collective-permute-start(bf16[576,1152]{1,0:T(8,128)(2,1)} %slice.282), channel_id=1, source_target_pairs={{0,8},{4,12},{8,0},{12,4},{16,24},{20,28},{24,16},{28,20},{1,9},{5... | collective-permute-start | bytes 3981320 | tf_op jit(solution)/shard_map/ppermute | solution.py:720
  448.0 41.3 %collective-permute-start.52 = (bf16[4,192,1152]{2,1,0:T(8,128)(2,1)}, bf16[4,192,1152]{2,1,0:T(8,128)(2,1)}, u32[]{:S(2)}, u32[]{:S(2)}) collective-permute-start(bf16[4,192,1152]{2,1,0:T(8,128)(2,1)} %get-tuple-element.130), channel_id=1, source_target_pairs={{0,16},{4,20},{8,24},{12,28},{16,0},{20,4},{24,8},{28,12},{1,17},{... | collective-permute-start | bytes 5308424 | tf_op jit(solution)/shard_map/ppermute | solution.py:720
  492.5 390.7 %reduce-scatter.17.cloned.1.call-start = ((), (), s32[]{:S(2)}) async-start(), calls=%async_computation.13 | async-start | bytes 2211840 | tf_op jit(solution)/shard_map/reduce_scatter | solution.py:959
  568.6 336.1 %reduce-scatter.9.cloned.1.call-start = ((), (), s32[]{:S(2)}) async-start(), calls=%async_computation.9 | async-start | bytes 2211840 | tf_op jit(solution)/shard_map/reduce_scatter | solution.py:913
  585.3 39.1 %collective-permute-start.38 = (bf16[4,192,1152]{2,1,0:T(8,128)(2,1)S(1)}, bf16[4,192,1152]{2,1,0:T(8,128)(2,1)S(1)}, u32[]{:S(2)}, u32[]{:S(2)}) collective-permute-start(bf16[4,192,1152]{2,1,0:T(8,128)(2,1)S(1)} %get-tuple-element.125), channel_id=1, source_target_pairs={{0,16},{4,20},{8,24},{12,28},{16,0},{20,4},{24,8},{28,12},{1,17},{... | collective-permute-start | bytes 5308424 | tf_op jit(solution)/shard_map/ppermute | solution.py:720
  585.9 77.1 %collective-permute-start.48 = (bf16[1152,1536]{1,0:T(8,128)(2,1)}, bf16[1152,1536]{1,0:T(8,128)(2,1)}, u32[]{:S(2)}, u32[]{:S(2)}) collective-permute-start(bf16[1152,1536]{1,0:T(8,128)(2,1)} %get-tuple-element.127), channel_id=1, source_target_pairs={{0,8},{4,12},{8,0},{12,4},{16,24},{20,28},{24,16},{28,20},{1,9},{5... | collective-permute-start | bytes 10616840 | tf_op jit(solution)/shard_map/ppermute | solution.py:720
  626.1 279.6 %reduce-scatter.13.cloned.1.call-start = ((), (), s32[]{:S(2)}) async-start(), calls=%async_computation.11 | async-start | bytes 4423680 | tf_op jit(solution)/shard_map/reduce_scatter | solution.py:916
  668.9 243.5 %reduce-scatter.7.cloned.1.call-start = ((), (), s32[]{:S(2)}) async-start(), calls=%async_computation.8 | async-start | bytes 4423680 | tf_op jit(solution)/shard_map/reduce_scatter | solution.py:916
  693.5 76.2 %collective-permute-start.34 = (bf16[1152,1536]{1,0:T(8,128)(2,1)}, bf16[1152,1536]{1,0:T(8,128)(2,1)S(1)}, u32[]{:S(2)}, u32[]{:S(2)}) collective-permute-start(bf16[1152,1536]{1,0:T(8,128)(2,1)} %get-tuple-element.122), channel_id=1, source_target_pairs={{0,8},{4,12},{8,0},{12,4},{16,24},{20,28},{24,16},{28,20},{1,9},{5... | collective-permute-start | bytes 10616840 | tf_op jit(solution)/shard_map/ppermute | solution.py:720
  693.8 81.8 %collective-permute-start.20 = (bf16[640,1152]{1,0:T(8,128)(2,1)}, bf16[640,1152]{1,0:T(8,128)(2,1)}, u32[]{:S(2)}, u32[]{:S(2)}) collective-permute-start(bf16[640,1152]{1,0:T(8,128)(2,1)} %get-tuple-element.93), channel_id=1, source_target_pairs={{0,4},{4,0},{8,12},{12,8},{16,20},{20,16},{24,28},{28,24},{1,5},{5... | collective-permute-start | bytes 4423688 | tf_op jit(solution)/shard_map/ppermute | solution.py:720
  774.6 143.0 %reduce-scatter.11.cloned.1.call-start = ((), (), s32[]{:S(2)}) async-start(), calls=%async_computation.10 | async-start | bytes 2211840 | tf_op jit(solution)/shard_map/reduce_scatter | solution.py:959
  883.3 107.9 %collective-permute-start.55 = (bf16[384,1152]{1,0:T(8,128)(2,1)}, bf16[384,1152]{1,0:T(8,128)(2,1)}, u32[]{:S(2)}, u32[]{:S(2)}) collective-permute-start(bf16[384,1152]{1,0:T(8,128)(2,1)} %pad_maximum_fusion.9.refs_2_), channel_id=1, source_target_pairs={{0,4},{4,0},{8,12},{12,8},{16,20},{20,16},{24,28},{28,24},{1,5},{5... | collective-permute-start | bytes 2654216 | tf_op jit(solution)/shard_map/ppermute | solution.py:720
  903.2 87.4 %collective-permute-start.33 = (f32[4,1152]{1,0:T(4,128)S(1)}, f32[4,1152]{1,0:T(4,128)S(1)}, u32[]{:S(2)}, u32[]{:S(2)}) collective-permute-start(f32[4,1152]{1,0:T(4,128)S(1)} %add.247), channel_id=1, source_target_pairs={{0,2},{1,3},{2,0},{3,1},{4,6},{5,7},{6,4},{7,5},{8,10},{9,11},{10,... | collective-permute-start | bytes 55304 | tf_op jit(solution)/shard_map/ppermute | solution.py:720
  912.4 35.9 %collective-permute-start.35 = (bf16[288,1536]{1,0:T(8,128)(2,1)}, bf16[288,1536]{1,0:T(8,128)(2,1)}, u32[]{:S(2)}, u32[]{:S(2)}) collective-permute-start(bf16[288,1536]{1,0:T(8,128)(2,1)} %reduce-scatter.7.cloned.1.call-done), channel_id=1, source_target_pairs={{0,16},{4,20},{8,24},{12,28},{16,0},{20,4},{24,8},{28,12},{1,17},{... | collective-permute-start | bytes 2654216 | tf_op jit(solution)/shard_map/ppermute | solution.py:720
  916.9 39.7 %collective-permute-start.40 = (bf16[192,1152]{1,0:T(8,128)(2,1)S(1)}, bf16[192,1152]{1,0:T(8,128)(2,1)}, u32[]{:S(2)}, u32[]{:S(2)}) collective-permute-start(bf16[192,1152]{1,0:T(8,128)(2,1)S(1)} %add_convert_fusion.9), channel_id=1, source_target_pairs={{0,16},{4,20},{8,24},{12,28},{16,0},{20,4},{24,8},{28,12},{1,17},{... | collective-permute-start | bytes 1327112 | tf_op jit(solution)/shard_map/ppermute | solution.py:720
  (154 other events, 2167.1 us)
Sparse Core Ops, SparseCore 0:
  13.9 46.2 all-gather.10
  62.3 54.2 all-gather.6
  118.7 39.0 all-gather.12
  159.8 54.2 all-gather.8
  492.6 36.3 reduce-scatter.14
  568.8 35.7 reduce-scatter.16
  626.2 35.7 reduce-scatter.8
  669.0 64.5 reduce-scatter.12
  774.7 64.5 reduce-scatter.6
  867.2 37.2 reduce-scatter.10

commit v2 on v1

--- a/solution.py
+++ b/solution.py
@@ -61,15 +61,20 @@
 SCALARS = pl.BlockSpec(memory_space=pltpu.SMEM)
 
 
-def call(kernel, outs, ins, flops, limit, out_specs=None, in_specs=None, **extra):
-    moved = sum(math.prod(v.shape) * v.dtype.itemsize for v in (*ins, *outs))
+def call(kernel, outs, ins, flops, limit, out_specs=None, in_specs=None, after=(), **extra):
+    count, waited = len(ins), len(after)
+
+    def body(*refs):
+        kernel(*refs[:count], *refs[count + waited :])
+
+    ins = (*ins, *after)
     return pl.pallas_call(
-        kernel,
+        body,
         out_shape=outs,
-        in_specs=in_specs or [WHOLE] * len(ins),
+        in_specs=(in_specs or [WHOLE] * count) + [FAR] * waited,
         out_specs=out_specs or [WHOLE] * len(outs),
         compiler_params=pltpu.CompilerParams(vmem_limit_bytes=limit << 20),
-        cost_estimate=pl.CostEstimate(flops=flops, bytes_accessed=moved, transcendentals=0),
+        cost_estimate=pl.CostEstimate(flops=1, bytes_accessed=1, transcendentals=0),
         **extra,
     )(*ins)
 
@@ -86,7 +91,7 @@
     normed_ref[...] = (total * inverse * gain[...]).astype(BF16)
 
 
-def add_norm(held, parts, gain):
+def add_norm(held, parts, gain, after=()):
     rows, width = held.shape
     step = 128
     block = pl.BlockSpec((step, width), lambda i: (i, 0))
@@ -102,6 +107,7 @@
         in_specs=[block] * (1 + len(parts)) + [line],
         out_specs=[block] * len(outs),
         grid=(rows // step,),
+        after=after,
     )
     return result if parts else (held, result[0])
 
@@ -124,7 +130,7 @@
     gain_ref[...] += jnp.sum(grad * plain, axis=0, keepdims=True)
 
 
-def norm_back(flow, parts, held, gain):
+def norm_back(flow, parts, held, gain, after=()):
     rows, width = held.shape
     step = 128
     block = pl.BlockSpec((step, width), lambda i: (i, 0))
@@ -138,7 +144,129 @@
         in_specs=[block] * 4 + [line],
         out_specs=[block, block, line],
         grid=(rows // step,),
-    )
+        after=after,
+    )
+
+
+def add_kernel(mine, other, out):
+    out[...] = (mine[...].astype(F32) + other[...].astype(F32)).astype(BF16)
+
+
+def add_two_kernel(first_mine, first_other, second_mine, second_other, *refs):
+    out = refs[-1]
+    if len(refs) == 3:
+        refs[1][...] = refs[0][...]
+    first = first_mine[...].astype(F32) + first_other[...].astype(F32)
+    second = second_mine[...].astype(F32) + second_other[...].astype(F32)
+    axis = len(out.shape) - 1
+    out[...] = jnp.concatenate([first.astype(BF16), second.astype(BF16)], axis=axis)
+
+
+def add_two(first, second, after=(), passed=None):
+    ins = (*first, *second)
+    lead = first[0].shape[:-1]
+    steps = 4
+
+    def block(*shape):
+        shape = (shape[0] // steps, *shape[1:])
+        return pl.BlockSpec(shape, lambda i: (i,) + (0,) * (len(shape) - 1))
+
+    columns = first[0].shape[-1] + second[0].shape[-1]
+    extra = () if passed is None else (passed,)
+    result = call(
+        add_two_kernel,
+        [shaped(part.shape, part.dtype) for part in extra] + [shaped((*lead, columns), BF16)],
+        (*ins, *extra),
+        0,
+        24,
+        in_specs=[block(*part.shape) for part in (*ins, *extra)],
+        out_specs=[block(*part.shape) for part in extra] + [block(*lead, columns)],
+        grid=(steps,),
+        after=after,
+    )
+    return result if extra else result[0]
+
+
+def split_sum_kernel(share, row_other, side_other, row_out, side_out):
+    cut = row_out.shape[1]
+    row_out[...] = (share[:, :cut].astype(F32) + row_other[...].astype(F32)).astype(BF16)
+    side_out[...] = (share[:, cut:].astype(F32) + side_other[...].astype(F32)).astype(BF16)
+
+
+def split_sum(share, row_other, side_other, after=()):
+    return call(
+        split_sum_kernel,
+        [shaped(row_other.shape, BF16), shaped(side_other.shape, BF16)],
+        (share, row_other, side_other),
+        0,
+        16,
+        after=after,
+    )
+
+
+def order_kernel(ids_ref, row_mine, row_other, side_mine, side_other, out):
+    side, row = ids_ref[4], ids_ref[3]
+    half, cut = row_mine.shape
+    for value, mine, other, cols in (
+        (row, row_mine, row_other, slice(0, cut)),
+        (side, side_mine, side_other, slice(cut, None)),
+    ):
+        for index in range(2):
+            chosen = jnp.where(value == index, mine[...], other[...])
+            out[index * half : (index + 1) * half, cols] = chosen
+
+
+def order(ids, parts):
+    half, cut = parts[0].shape
+    return call(
+        order_kernel,
+        [shaped((2 * half, cut + parts[2].shape[1]), BF16)],
+        (ids, *parts),
+        0,
+        16,
+        in_specs=[SCALARS] + [WHOLE] * 4,
+    )[0]
+
+
+def cross_kernel(share, gate_other, up_other, gate_out, up_out):
+    block = gate_out.shape[1] // 2
+    for out, other, low in ((gate_out, gate_other, 0), (up_out, up_other, 2 * block)):
+        for index in range(2):
+            mine = share[:, low + index * block : low + (index + 1) * block]
+            theirs = other[:, (1 - index) * block : (2 - index) * block]
+            out[:, index * block : (index + 1) * block] = (
+                mine.astype(F32) + theirs.astype(F32)
+            ).astype(BF16)
+
+
+def cross(share, gate_other, up_other, after=()):
+    shape = (share.shape[0], share.shape[1] // 2)
+    return call(
+        cross_kernel,
+        [shaped(shape, BF16)] * 2,
+        (share, gate_other, up_other),
+        0,
+        16,
+        after=after,
+    )
+
+
+def add(mine, other, after=(), steps=4):
+    shape = mine.shape
+    block = pl.BlockSpec(
+        (shape[0] // steps, *shape[1:]), lambda i: (i,) + (0,) * (len(shape) - 1)
+    )
+    return call(
+        add_kernel,
+        [shaped(shape, BF16)],
+        (mine, other),
+        0,
+        24,
+        in_specs=[block, block],
+        out_specs=[block],
+        grid=(steps,),
+        after=after,
+    )[0]
 
 
 KEY_HALF = PAIR_KV * HEAD_DIM
@@ -166,7 +294,7 @@
         head(2 * KEY_HALF + index * HEAD_DIM, query_ref, index * HEAD_DIM)
 
 
-def rope(qkv, cosine, sine):
+def rope(qkv, cosine, sine, after=()):
     return call(
         rope_kernel,
         [
@@ -177,6 +305,7 @@
         (qkv, cosine, sine),
         0,
         32,
+        after=after,
     )
 
 
@@ -232,7 +361,7 @@
         lax.fori_loop(0, SHARED, head, 0)
 
 
-def attend(query, key_value, key_value_turned, shared, key_pos, row_pos):
+def attend(query, key_value, key_value_turned, shared, key_pos, row_pos, after=()):
     flops = 4 * QUERY_HALF * ROWS * (shared.shape[0] + CONT)
     return call(
         attend_kernel,
@@ -240,6 +369,7 @@
         (query, key_value, key_value_turned, shared, key_pos, row_pos),
         flops,
         48,
+        after=after,
     )
 
 
@@ -349,7 +479,9 @@
             own_grad_ref[cols, KEY_HALF + low : KEY_HALF + low + HEAD_DIM] = own_value_sum[run]
 
 
-def attend_back(query, grad, key_value, key_value_turned, shared, key_pos, row_pos, lse, cosine, sine):
+def attend_back(
+    query, grad, key_value, key_value_turned, shared, key_pos, row_pos, lse, cosine, sine, after=()
+):
     count = shared.shape[0]
     flops = 10 * QUERY_HALF * ROWS * (count + CONT)
     return call(
@@ -368,6 +500,7 @@
             pltpu.VMEM((SHARED, CONT, TAIL), BF16),
             pltpu.VMEM((SHARED, CONT, TAIL), BF16),
         ],
+        after=after,
     )
 
 
@@ -385,179 +518,265 @@
     out_ref[:, 2 * KEY_HALF :] = turned(query_grad_ref[...]).astype(BF16)
 
 
-def merge(query_grad, own_grad, prompt_grad, cosine, sine):
+def merge(query_grad, own_grad, prompt_grad, cosine, sine, after=()):
     return call(
         merge_kernel,
         [shaped((ROWS, QKV), BF16)],
         (query_grad, own_grad, prompt_grad, cosine, sine),
         0,
         32,
+        after=after,
     )[0]
 
 
-def weight_copies(pieces, target, sems, block, depth):
-    if block < 3:
-        return [
-            pltpu.make_async_copy(
-                pieces[block].at[:, : 2 * block_of(target)], target.at[block], sems.at[block]
-            )
-        ]
-    half = depth // 2
-    return [
-        pltpu.make_async_copy(
-            pieces[3 + part].at[:, : 2 * block_of(target)],
-            target.at[3, pl.ds(part * half, half)],
-            sems.at[3 + part],
-        )
-        for part in range(2)
-    ]
-
-
-def block_of(target):
-    return target.shape[2] // 2
-
-
-def mlp_kernel(
-    quarter_ref, normed_ref, *refs
-):
-    pieces = refs[:5]
-    down_ref, slope_ref, scale_ref, unit_ref, out_ref = refs[5:10]
-    held, sems, down_sem = refs[10:]
+def mlp_kernel(layer, ids_ref, normed_ref, *refs):
+    own = refs[0]
+    from_row, from_side, from_across = refs[1:3], refs[3:5], refs[5:9]
+    gate_ref, up_ref, down_shard = (ref.at[layer] for ref in refs[9:12])
+    weight_ref, down_ref, slope_ref, scale_ref, unit_ref, out_ref = refs[12:18]
+    held, sems, down_sem, keep_sem = refs[18:]
     rows, depth = normed_ref.shape
-    width = depth
-    block = block_of(held)
+    block = held.shape[2] // 2
     shard = depth // 4
     lines = block // 4
-    wide = width // 3
-    quarter = quarter_ref[0]
-    copies = [weight_copies(pieces, held, sems, part, depth) for part in range(4)]
+    wide = depth // 3
+    quarter, plane, pair = ids_ref[0], ids_ref[1], ids_ref[2]
+    slots = line_slots(plane)
+
+    def copy(source, target, sem):
+        pltpu.make_async_copy(source, target, sem).start()
+
+    def at(start, size):
+        return pl.ds(pl.multiple_of(start, 16), size)
+
+    def pieces(part):
+        if part == 0:
+            return [(own.at[owner], 0, shard, owner) for owner in (plane, *slots)]
+        if part < 3:
+            pair_of_slots, last = (from_row, from_side)[part - 1]
+            arrived = (pair_of_slots.at[0], pair_of_slots.at[1], last.at[0])
+            return [(arrived[slot], 0, shard, slots[slot]) for slot in range(3)]
+        half = shard // 2
+        return [
+            (from_across[0], 0, shard, slots[0]),
+            (from_across[1], 0, shard, slots[1]),
+            (from_across[2], 0, half, slots[2]),
+            (from_across[3], half, shard, slots[2]),
+        ]
+
     for part in range(4):
-        for copy in copies[part]:
-            copy.start()
-    for place in range(4):
-        plane = quarter ^ place
-        for part in range(4):
-            target_row = pl.multiple_of(place * block + lines * (quarter ^ part), lines)
-            for column in range(3):
-                target = down_ref.at[
-                    pl.ds(target_row, lines), column * wide : (column + 1) * wide
-                ]
-                taken = slice(2 * block, 2 * block + wide)
-                if part < 3:
-                    start = pl.multiple_of(shard * plane + lines * column, lines)
-                    pltpu.make_async_copy(
-                        pieces[part].at[pl.ds(start, lines), taken], target, down_sem
-                    ).start()
-                else:
-                    inner = plane % 2
-                    start = pl.multiple_of(shard * inner + lines * column, lines)
-                    for half in range(2):
-
-                        @pl.when(plane // 2 == half)
-                        def _(half=half, start=start, target=target, taken=taken):
-                            pltpu.make_async_copy(
-                                pieces[3 + half].at[pl.ds(start, lines), taken], target, down_sem
-                            ).start()
+        for source, low, high, owner in pieces(part):
+            copy(
+                source.at[:, : 2 * block],
+                held.at[part, at(shard * owner + low, high - low)],
+                sems.at[part],
+            )
+        if part == 0:
+            continue
+        col = pl.ds(pl.multiple_of((2 * (quarter ^ part) + pair) * block, block), block)
+        for index, ref in enumerate((gate_ref, up_ref)):
+            copy(
+                ref.at[:, col],
+                held.at[part, at(shard * plane, shard), pl.ds(index * block, block)],
+                sems.at[part],
+            )
+    taken = pl.ds(2 * block, wide)
+
+    def down_copies(source, low, high, place, piece):
+        for column in range(3):
+            first, last = max(low, lines * column), min(high, lines * (column + 1))
+            if first < last:
+                copy(
+                    source.at[at(first - low, last - first), taken],
+                    down_ref.at[
+                        at(
+                            block * place + lines * (quarter ^ piece) + first - lines * column,
+                            last - first,
+                        ),
+                        pl.ds(wide * column, wide),
+                    ],
+                    down_sem,
+                )
+
+    for part in range(4):
+        for source, low, high, owner in pieces(part):
+            down_copies(source, low, high, quarter ^ owner, part)
+        if part == 0:
+            continue
+        copy(
+            down_shard.at[at(block * pair + lines * (quarter ^ part), lines)],
+            down_ref.at[at(block * (quarter ^ plane) + lines * (quarter ^ part), lines)],
+            down_sem,
+        )
 
     step = rows // 2
+    kept = []
     for part in range(4):
-        for copy in copies[part]:
-            copy.wait()
+        pltpu.make_async_copy(held.at[part], held.at[part], sems.at[part]).wait()
+        kept.append(pltpu.make_async_copy(held.at[part], weight_ref.at[part], keep_sem.at[part]))
+        kept[-1].start()
 
         def tile(index, carry, part=part):
-            at = pl.ds(pl.multiple_of(index * step, step), step)
-            normed = normed_ref[at, :]
+            some = pl.ds(pl.multiple_of(index * step, step), step)
+            normed = normed_ref[some, :]
             gate = dot_nn(normed, held[part, :, :block])
             up = dot_nn(normed, held[part, :, block:])
             sigmoid = 1.0 / (1.0 + jnp.exp(-gate))
             scale = gate * sigmoid
             cols = slice(part * block, (part + 1) * block)
-            slope_ref[at, cols] = (up * sigmoid * (1.0 + gate * (1.0 - sigmoid))).astype(BF16)
-            scale_ref[at, cols] = scale.astype(BF16)
-            unit_ref[at, cols] = (scale * up).astype(BF16)
+            slope_ref[some, cols] = (up * sigmoid * (1.0 + gate * (1.0 - sigmoid))).astype(BF16)
+            scale_ref[some, cols] = scale.astype(BF16)
+            unit_ref[some, cols] = (scale * up).astype(BF16)
             return carry
 
         lax.fori_loop(0, 2, tile, 0)
     pltpu.make_async_copy(down_ref, down_ref, down_sem).wait()
 
     def finish(index, carry):
-        at = pl.ds(pl.multiple_of(index * step, step), step)
-        out_ref[at, :] = dot_nn(unit_ref[at, :], down_ref[...]).astype(BF16)
+        some = pl.ds(pl.multiple_of(index * step, step), step)
+        out_ref[some, :] = dot_nn(unit_ref[some, :], down_ref[...]).astype(BF16)
         return carry
 
     lax.fori_loop(0, 2, finish, 0)
-
-
-def mlp(quarter, normed, pieces, block):
+    for part in kept:
+        part.wait()
+
+
+def mlp(layer, ids, normed, pieces, weights, block, after=()):
     rows, depth = normed.shape
     units = 4 * block
-    return call(
-        mlp_kernel,
+    ins = (ids, normed, *pieces, *weights)
+    return call(
+        functools.partial(mlp_kernel, layer),
         [
+            shaped((4, depth, 2 * block), BF16),
             shaped((units, depth), BF16),
             shaped((rows, units), BF16),
             shaped((rows, units), BF16),
             shaped((rows, units), BF16),
             shaped((rows, depth), BF16),
         ],
-        (quarter, normed, *pieces),
+        ins,
         6 * rows * depth * units,
         56,
-        in_specs=[SCALARS, WHOLE] + [FAR] * 5,
+        in_specs=[SCALARS, WHOLE] + [FAR] * (len(ins) - 2),
+        out_specs=[FAR] + [WHOLE] * 5,
         scratch_shapes=[
             pltpu.VMEM((4, depth, 2 * block), BF16),
-            pltpu.SemaphoreType.DMA((5,)),
+            pltpu.SemaphoreType.DMA((4,)),
             pltpu.SemaphoreType.DMA,
+            pltpu.SemaphoreType.DMA((4,)),
         ],
-    )
-
-
-def down_grad_kernel(where_ref, unit_ref, flow_ref, keep_ref, send_ref):
-    quarter, row = where_ref[0], where_ref[1]
+        after=after,
+    )
+
+
+def pack_kernel(layer, ids_ref, gate_ref, up_ref, down_ref, out, sem):
+    quarter, pair = ids_ref[0], ids_ref[2]
+    depth, columns = out.shape
+    wide = columns // 3
+    lines = depth // 3
+    col = pl.ds(pl.multiple_of((2 * quarter + pair) * wide, wide), wide)
+    for index, ref in enumerate((gate_ref, up_ref)):
+        target = out.at[:, pl.ds(index * wide, wide)]
+        pltpu.make_async_copy(ref.at[layer, :, col], target, sem).start()
+    start = pl.multiple_of((4 * pair + quarter) * lines, lines)
+    for index in range(3):
+        pltpu.make_async_copy(
+            down_ref.at[layer, pl.ds(start, lines), pl.ds(index * wide, wide)],
+            out.at[pl.ds(index * lines, lines), pl.ds(2 * wide, wide)],
+            sem,
+        ).start()
+    pltpu.make_async_copy(out, out, sem).wait()
+
+
+def pack(layer, ids, weights, after=()):
+    _, depth, units = weights[0].shape
+    return call(
+        functools.partial(pack_kernel, layer),
+        [shaped((depth, 3 * units // 8), BF16)],
+        (ids, *weights),
+        0,
+        16,
+        in_specs=[SCALARS] + [FAR] * 3,
+        out_specs=[FAR],
+        scratch_shapes=[pltpu.SemaphoreType.DMA],
+        after=after,
+    )[0]
+
+
+def deal(total, row, side, cut, place, row_keep, row_send, side_keep, side_send):
+    half = total.shape[0] // 2
+    for index in range(2):
+        part = total[index * half : (index + 1) * half]
+        for value, keep, send, cols in (
+            (row, row_keep, row_send, slice(0, cut)),
+            (side, side_keep, side_send, slice(cut, None)),
+        ):
+
+            @pl.when(value == index)
+            def _(part=part, keep=keep, cols=cols):
+                keep[place] = part[:, cols]
+
+            @pl.when(value != index)
+            def _(part=part, send=send, cols=cols):
+                send[place] = part[:, cols]
+
+
+def dealt(blocks, half, columns, cut):
+    return [
+        shaped((blocks, half, size), BF16) for size in (cut, cut, columns - cut, columns - cut)
+    ]
+
+
+def down_grad_kernel(cut, ids_ref, unit_ref, flow_ref, *outs):
+    quarter, side, row = ids_ref[0], ids_ref[4], ids_ref[3]
     block = unit_ref.shape[1] // 4
-    half = block // 2
     for place in range(4):
-        plane = quarter ^ place
-        total = dot_tn(unit_ref[:, place * block : (place + 1) * block], flow_ref[...]).astype(
-            BF16
-        )
-        for index in range(2):
-            part = total[index * half : (index + 1) * half]
-
-            @pl.when(row == index)
-            def _(part=part, plane=plane):
-                keep_ref[plane] = part
-
-            @pl.when(row != index)
-            def _(part=part, plane=plane):
-                send_ref[plane] = part
-
-
-def down_grad(where, unit, flow):
+        total = dot_tn(unit_ref[:, place * block : (place + 1) * block], flow_ref[...])
+        deal(total.astype(BF16), row, side, cut, quarter ^ place, *outs)
+
+
+def down_grad(ids, unit, flow, cut, after=()):
     rows, units = unit.shape
     width = flow.shape[1]
-    half = units // 8
-    return call(
-        down_grad_kernel,
-        [shaped((4, half, width), BF16)] * 2,
-        (where, unit, flow),
+    return call(
+        functools.partial(down_grad_kernel, cut),
+        dealt(4, units // 8, width, cut),
+        (ids, unit, flow),
         2 * rows * units * width,
         48,
         in_specs=[SCALARS, WHOLE, WHOLE],
-    )
-
-
-def mlp_back_kernel(flow_ref, normed_ref, slope_ref, scale_ref, down_ref, *refs):
-    pieces = refs[:5]
-    keep_ref, send_ref, out_ref = refs[5:8]
-    held, total, unit_grad, sems = refs[8:]
+        after=after,
+    )
+
+
+def mlp_back_kernel(
+    flow_ref,
+    normed_ref,
+    slope_ref,
+    scale_ref,
+    down_ref,
+    weight_ref,
+    gate_keep,
+    gate_send,
+    up_keep,
+    up_send,
+    out_ref,
+    held,
+    total,
+    unit_grad,
+    sems,
+):
     rows, depth = normed_ref.shape
-    block = block_of(held)
-    order = (2, 3, 0, 1)
-    copies = [weight_copies(pieces, held, sems, part, depth) for part in range(4)]
+    block = held.shape[2] // 2
+    order = (3, 2, 1, 0)
+    copies = {
+        part: pltpu.make_async_copy(weight_ref.at[part], held.at[part], sems.at[part])
+        for part in order
+    }
     for part in order:
-        for copy in copies[part]:
-            copy.start()
+        copies[part].start()
     step = rows // 2
     for part in order:
         cols = slice(part * block, (part + 1) * block)
@@ -570,11 +789,12 @@
             return carry
 
         lax.fori_loop(0, 2, tile, 0)
-        target = send_ref if part >= 2 else keep_ref
-        side = slice((part % 2) * 2 * block, (part % 2 + 1) * 2 * block)
-        target[:, side] = dot_tn(normed_ref[...], unit_grad[...]).astype(BF16)
-        for copy in copies[part]:
-            copy.wait()
+        both = dot_tn(normed_ref[...], unit_grad[...]).astype(BF16)
+        target = gate_send if part >= 2 else gate_keep
+        target[:, (part % 2) * block : (part % 2 + 1) * block] = both[:, :block]
+        target = up_send if part % 2 else up_keep
+        target[:, (part // 2) * block : (part // 2 + 1) * block] = both[:, block:]
+        copies[part].wait()
 
         def gather(index, carry, part=part):
             at = pl.ds(pl.multiple_of(index * step, step), step)
@@ -590,54 +810,202 @@
         lax.fori_loop(0, 2, gather, 0)
 
 
-def mlp_back(flow, normed, slope, scale, down, pieces):
+def mlp_back(flow, normed, slope, scale, down, weights, after=()):
     rows, depth = normed.shape
     block = down.shape[0] // 4
     return call(
         mlp_back_kernel,
-        [
-            shaped((depth, 4 * block), BF16),
-            shaped((depth, 4 * block), BF16),
-            shaped((rows, depth), BF16),
-        ],
-        (flow, normed, slope, scale, down, *pieces),
+        [shaped((depth, 2 * block), BF16)] * 4 + [shaped((rows, depth), BF16)],
+        (flow, normed, slope, scale, down, weights),
         10 * rows * depth * 4 * block,
         60,
-        in_specs=[WHOLE] * 5 + [FAR] * 5,
+        in_specs=[WHOLE] * 5 + [FAR],
         scratch_shapes=[
             pltpu.VMEM((4, depth, 2 * block), BF16),
             pltpu.VMEM((rows, depth), F32),
             pltpu.VMEM((rows, 2 * block), BF16),
-            pltpu.SemaphoreType.DMA((5,)),
+            pltpu.SemaphoreType.DMA((4,)),
         ],
-    )
-
-
-def place_kernel(fresh, where_ref, *refs):
-    parts = refs[:6]
-    outs = refs[6:] if fresh else refs[13:]
+        after=after,
+    )
+
+
+def join_kernel(ids_ref, local, mine, other, out, sem):
+    plane, row = ids_ref[1], ids_ref[3]
+    half = local.shape[0] // 2
+
+    def copy(source, start):
+        target = out.at[pl.ds(pl.multiple_of(start, 16), source.shape[0])]
+        pltpu.make_async_copy(source, target, sem).start()
+
+    copy(local, 2 * half * plane)
+    for slot, owner in enumerate(line_slots(plane)):
+        copy(mine.at[owner, pl.ds(0, half)], half * (2 * owner + row))
+        copy(other.at[slot], half * (2 * owner + 1 - row))
+    pltpu.make_async_copy(out, out, sem).wait()
+
+
+def join(ids, local, mine, other, after=()):
+    shape = (4 * local.shape[0], local.shape[1])
+    return call(
+        join_kernel,
+        [shaped(shape, BF16)],
+        (ids, local, mine, other),
+        0,
+        16,
+        in_specs=[SCALARS] + [FAR] * 3,
+        out_specs=[FAR],
+        scratch_shapes=[pltpu.SemaphoreType.DMA],
+        after=after,
+    )[0]
+
+
+def others_kernel(first, ids_ref, gathered, out, sem):
+    count, rows, _ = out.shape
+    for slot, owner in enumerate(line_slots(ids_ref[1])[first : first + count]):
+        pltpu.make_async_copy(gathered.at[owner, pl.ds(0, rows)], out.at[slot], sem).start()
+    pltpu.make_async_copy(out, out, sem).wait()
+
+
+def others(ids, gathered, rows, first, last, after=()):
+    return call(
+        functools.partial(others_kernel, first),
+        [shaped((last - first, rows, gathered.shape[2]), BF16)],
+        (ids, gathered),
+        0,
+        16,
+        in_specs=[SCALARS, FAR],
+        out_specs=[FAR],
+        scratch_shapes=[pltpu.SemaphoreType.DMA],
+        after=after,
+    )[0]
+
+
+def line_slots(plane):
+    return [plane ^ step for step in (1, 2, 3)]
+
+
+def attn_grad_kernel(cut, ids_ref, normed, grad, attended, flow, *outs):
+    side, row = ids_ref[4], ids_ref[3]
+    blocks, half, _ = outs[0].shape
+    out_cols = flow.shape[1] // 2
+    out = dot_nn(attended[...], flow[...]).astype(BF16)
+    for block in range(blocks):
+        low, col = 2 * (block // 2) * half, (block % 2) * out_cols
+        total = jnp.concatenate(
+            [
+                dot_tn(normed[:, 2 * block * half : 2 * (block + 1) * half], grad[...]).astype(
+                    BF16
+                ),
+                out[low : low + 2 * half, col : col + out_cols],
+            ],
+            axis=1,
+        )
+        deal(total, row, side, cut, block, *outs)
+
+
+def attn_grad(ids, normed, grad, attended, flow, cut, after=()):
+    columns = grad.shape[1] + flow.shape[1] // 2
+    return call(
+        functools.partial(attn_grad_kernel, cut),
+        dealt(4, normed.shape[1] // 8, columns, cut),
+        (ids, normed, grad, attended, flow),
+        0,
+        40,
+        in_specs=[SCALARS] + [WHOLE] * 4,
+        after=after,
+    )
+
+
+def attn_sum_kernel(pair_ref, row_mine, row_other, side_mine, side_other, keep_ref, send_ref):
+    pair = pair_ref[0]
+    total = jnp.concatenate(
+        [
+            (mine[...].astype(F32) + other[...].astype(F32)).astype(BF16)
+            for mine, other in ((row_mine, row_other), (side_mine, side_other))
+        ],
+        axis=2,
+    )
+    keep_ref[:, :, :QKV] = total[:, :, :QKV]
+    for plane in range(4):
+        for owner in range(2):
+
+            @pl.when(pair == owner)
+            def _(plane=plane, owner=owner):
+                if plane // 2 == owner:
+                    keep_ref[plane, :, QKV:] = total[2 * (plane % 2) + owner, :, QKV:]
+                else:
+                    send_ref[plane % 2] = total[2 * (plane % 2) + 1 - owner, :, QKV:]
+                    keep_ref[plane, :, QKV:] = jnp.zeros_like(keep_ref[plane, :, QKV:])
+
+
+def attn_sum(pair, parts, after=()):
+    blocks, half, first = parts[0].shape
+    columns = first + parts[2].shape[2]
+    return call(
+        attn_sum_kernel,
+        [
+            shaped((blocks, half, columns), BF16),
+            shaped((blocks // 2, half, columns - QKV), BF16),
+        ],
+        (pair, *parts),
+        0,
+        32,
+        in_specs=[SCALARS] + [WHOLE] * 4,
+        after=after,
+    )
+
+
+def attn_join_kernel(pair_ref, mine, other, out):
+    pair = pair_ref[0]
+    out[:, :, :QKV] = mine[:, :, :QKV]
+    for plane in range(4):
+        for owner in range(2):
+
+            @pl.when(pair == owner)
+            def _(plane=plane, owner=owner):
+                if plane // 2 == owner:
+                    out[plane, :, QKV:] = mine[plane, :, QKV:]
+                else:
+                    out[plane, :, QKV:] = other[plane % 2]
+
+
+def attn_join(pair, mine, other, after=()):
+    return call(
+        attn_join_kernel,
+        [shaped(mine.shape, BF16)],
+        (pair, mine, other),
+        0,
+        32,
+        in_specs=[SCALARS, WHOLE, WHOLE],
+        after=after,
+    )[0]
+
+
+def place_ff_kernel(where_ref, *refs):
+    gates, ups, downs = refs[0:4], refs[4:8], refs[8:10]
+    gate_out, up_out, down_out = refs[10:]
     pair, quarter = where_ref[0], where_ref[1]
-    ff_mine, ff_other, down_mine, down_other, attn_mine, attn_other = parts
-    query_out, key_out, value_out, out_out, gate_out, up_out, down_out = outs
-    block = ff_mine.shape[2] // 4
-    side, row = quarter // 2, quarter % 2
-    for where_from, owner in ((ff_mine, pair), (ff_other, 1 - pair)):
-        for index in range(2):
-            for inner in range(2):
-                plane = 2 * (side ^ index) + (row ^ inner)
+    block = gates[0].shape[1] // 2
+    for out, pieces, spread, inner in ((gate_out, gates, 2, 1), (up_out, ups, 1, 2)):
+        for number, ref in enumerate(pieces):
+            owner = pair ^ (number // 2)
+            for index in range(2):
+                plane = quarter ^ ((number % 2) * spread + index * inner)
                 col = pl.multiple_of((2 * plane + owner) * block, block)
-                low = 2 * inner * block
-                gate_out[0, :, pl.ds(col, block)] = where_from[
-                    index, :, low : low + block
+                out[0, :, pl.ds(col, block)] = ref[
+                    :, index * block : (index + 1) * block
                 ].astype(F32)
-                up_out[0, :, pl.ds(col, block)] = where_from[
-                    index, :, low + block : low + 2 * block
-                ].astype(F32)
-    down_rows = down_mine.shape[0]
-    for where_from, owner in ((down_mine, pair), (down_other, 1 - pair)):
+    down_rows = downs[0].shape[0]
+    for where_from, owner in ((downs[0], pair), (downs[1], 1 - pair)):
         down_out[0, pl.ds(pl.multiple_of(owner * down_rows, down_rows), down_rows), :] = (
             where_from[...].astype(F32)
         )
+
+
+def place_attn_kernel(where_ref, attn_mine, attn_other, *refs):
+    query_out, key_out, value_out, out_out = refs
+    pair = where_ref[0]
     first = jnp.where(pair == 0, attn_mine[...], attn_other[...]).astype(F32)
     second = jnp.where(pair == 0, attn_other[...], attn_mine[...]).astype(F32)
     low = 0
@@ -651,7 +1019,14 @@
         low += cols
 
 
-def place(layer, where, parts, outs, held):
+def place_kernel(kernel, fresh, parts, outs, *refs):
+    here = refs[: 1 + parts]
+    there = refs[1 + parts :] if fresh else refs[1 + parts + outs :]
+    kernel(*here, *there[:outs])
+    there[outs][...] = jnp.zeros_like(there[outs])
+
+
+def place(kernel, layer, where, parts, outs, held, after=()):
     ins = (where, *parts, *(held or ()))
     specs = [SCALARS] + [WHOLE] * len(parts) + [FAR] * len(held or ())
 
@@ -660,15 +1035,17 @@
 
     aliases = {} if held is None else {1 + len(parts) + i: i for i in range(len(outs))}
     return call(
-        functools.partial(place_kernel, held is None),
-        outs,
+        functools.partial(place_kernel, kernel, held is None, len(parts), len(outs)),
+        [*outs, shaped((8, 128), F32)],
         ins,
         0,
         60,
         in_specs=specs,
-        out_specs=[layer_block(out) for out in outs],
+        out_specs=[layer_block(out) for out in outs]
+        + [pl.BlockSpec((8, 128), lambda _: (0, 0))],
         input_output_aliases=aliases,
         grid=(1,),
+        after=after,
     )
 
 
@@ -739,7 +1116,11 @@
         )
 
     every_pos = positions(assign[0], ctx_count).reshape(chip_count, 2, RUN)
-    wanted = chip ^ jnp.arange(chip_count, dtype=jnp.int32)
+    key_bits = [ROW, SIDE] + outer_bits
+    steps = [0]
+    for bit in key_bits:
+        steps += [step ^ (bit // 2) for step in steps]
+    wanted = chip ^ jnp.array(steps, dtype=jnp.int32)
     picked = wanted[:, None] == jnp.arange(chip_count, dtype=jnp.int32)[None, :]
     prompt_pos = jnp.sum(
         jnp.where(picked[:, :, None, None], every_pos[None, :, :, : 2 * HALF], 0), axis=1
@@ -755,13 +1136,14 @@
 
     gain_line = jnp.concatenate([attn_gain, mlp_gain]).reshape(1, -1)
     columns = QKV + half_width
-
-    def attn_piece(layer):
-        piece = jnp.concatenate(
+    plane = lax.axis_index("wt")
+    ids = jnp.stack([quarter, plane, pair, row, side])
+    ff_weights = (w_gate, w_up, w_down)
+
+    def attn_local(layer):
+        return jnp.concatenate(
             [
-                lax.dynamic_slice(
-                    weight[layer], (half_depth * row, cols * pair), (half_depth, cols)
-                )
+                lax.dynamic_slice(weight[layer], (0, cols * pair), (depth, cols))
                 for weight, cols in (
                     (w_key, KEY_HALF),
                     (w_value, KEY_HALF),
@@ -771,85 +1153,97 @@
             ],
             axis=1,
         )
+
+    def attn_gather(layer):
+        local = attn_local(layer)
+        piece = lax.dynamic_slice(local, (half_depth * row, 0), (half_depth, columns))
         if layer == 0:
             line = jnp.pad(gain_line, ((0, 15), (0, columns - gain_line.shape[1])))
             piece = jnp.concatenate([piece, line], axis=0)
-        return piece
-
-    def attn_weights(mine):
-        other = flip(mine, ROW)
-        mine, other = mine[:, :half_depth], other[:, :half_depth]
-        first, second = ordered(row, mine, other)
-        both = jnp.stack([first, second], axis=1).reshape(wt_count * depth, columns)
-        qkv_w = both[:, :QKV]
-        out_cols = both[:, QKV:]
-        keep = lax.dynamic_slice(out_cols, (QUERY_HALF * pair, 0), (QUERY_HALF, half_width))
-        send = lax.dynamic_slice(out_cols, (QUERY_HALF * (1 - pair), 0), (QUERY_HALF, half_width))
+        return local, lax.all_gather(piece, "wt", axis=0, tiled=False)
+
+    def attn_weights(local, mine, other, after):
+        both = join(ids, local, mine, other, after)
+        keep = lax.dynamic_slice(both, (QUERY_HALF * pair, QKV), (QUERY_HALF, half_width))
+        send = lax.dynamic_slice(both, (QUERY_HALF * (1 - pair), QKV), (QUERY_HALF, half_width))
         out_w = jnp.concatenate(ordered(pair, keep, flip(send, PAIR)), axis=1)
-        return qkv_w, out_w
-
-    def mlp_piece(layer):
-        col = 2 * ff_block * quarter + ff_block * pair
-        low = ff_block * pair + ff_piece * quarter
-        down = lax.dynamic_slice(w_down[layer], (low, 0), (ff_piece, width))
-        wide = width // 3
-        down = jnp.concatenate([down[:, i * wide : (i + 1) * wide] for i in range(3)], axis=0)
-        return jnp.concatenate(
-            [
-                lax.dynamic_slice(w_gate[layer], (0, col), (depth, ff_block)),
-                lax.dynamic_slice(w_up[layer], (0, col), (depth, ff_block)),
-                down,
-            ],
-            axis=1,
-        )
-
-    def mlp_pieces(mine):
-        half_rows = mine.shape[0] // 2
-        by_row = flip(mine, ROW)
-        by_side = flip(mine, SIDE)
-        return (
-            mine,
-            by_row,
-            by_side,
-            flip(by_row[:half_rows], SIDE),
-            flip(by_side[half_rows:], ROW),
-        )
+        return both[:, :QKV], out_w
+
+    def mlp_gather(layer):
+        piece = pack(layer, ids, ff_weights)
+        return lax.all_gather(piece, "wt", axis=0, tiled=False)
+
+    def mlp_spread(line, ahead, bit):
+        first, last = line
+        by_row, by_side = ahead or (flip(first, ROW), flip(first, SIDE))
+        last_by_row, last_by_side = flip(last, ROW), flip(last, SIDE)
+        across = (
+            flip(by_row[0], SIDE),
+            flip(by_row[1], SIDE) if bit == SIDE else flip(by_side[1], ROW),
+            flip(last_by_row[0, :half_depth], SIDE),
+            flip(last_by_side[0, half_depth:], ROW),
+        )
+        return by_row, last_by_row, by_side, last_by_side, *across
 
     where = jnp.stack([pair, quarter])
-    spot = jnp.stack([quarter, row])
-    quarter_id = quarter[None]
 
     residual = pair_rows(tokens[0]).astype(F32)
     parts = ()
     saved_layers = []
-    gains = None
+    attn_sets, ff_sets = [], []
     for layer in range(layer_count):
-        gathered = lax.all_gather(attn_piece(layer), "wt", axis=0, tiled=False)
-        if layer == 0:
-            lines = gathered[:, half_depth, : gain_line.shape[1]].astype(F32)
-            gains = (
-                lines.reshape(wt_count, 2 * layer_count, depth)
-                .transpose(1, 0, 2)
-                .reshape(2 * layer_count, 1, wt_count * depth)
-            )
-        qkv_w, out_w = attn_weights(gathered)
-        pieces = mlp_pieces(lax.all_gather(mlp_piece(layer), "wt", axis=0, tiled=True))
+        attn_sets.append(attn_gather(layer))
+        ff_sets.append(mlp_gather(layer))
+    lines = attn_sets[0][1][:, half_depth, : gain_line.shape[1]].astype(F32)
+    gains = (
+        lines.reshape(wt_count, 2 * layer_count, depth)
+        .transpose(1, 0, 2)
+        .reshape(2 * layer_count, 1, wt_count * depth)
+    )
+    attn_other = flip(others(ids, attn_sets[0][1], half_depth, 0, 3), ROW)
+    for layer in range(layer_count):
+        last = layer + 1 == layer_count
+        local, mine = attn_sets[layer]
+        qkv_w, out_w = attn_weights(local, mine, attn_other, ())
         gain_attn, gain_mlp = gains[layer], gains[layer_count + layer]
         residual, normed_attn = add_norm(residual, parts, gain_attn)
-        query, key_value, key_value_turned = rope(dot_tt(qkv_w, normed_attn), cosine, sine)
+        ahead = tuple(flip(early, bit) for bit in (ROW, SIDE)) if layer else ()
+        query, key_value, key_value_turned = rope(
+            dot_tt(qkv_w, normed_attn), cosine, sine, ahead
+        )
         shared = key_value[TAIL:]
-        for bit in [SIDE, ROW] + outer_bits:
+        for bit in key_bits:
             shared = jnp.concatenate([shared, flip(shared, bit)], axis=0)
-        attended, lse = attend(query, key_value, key_value_turned, shared, key_pos, row_pos)
+        first = early if layer else others(ids, ff_sets[layer], depth, 0, 2, (shared,))
+        line = (first, others(ids, ff_sets[layer], depth, 2, 3, (shared,)))
+        spread = mlp_spread(line, ahead, ROW if layer else SIDE)
+        attended, lse = attend(
+            query, key_value, key_value_turned, shared, key_pos, row_pos, line
+        )
         part = dot_tn(attended, out_w).astype(BF16)
         residual_mid, normed_mlp = add_norm(residual, (part, flip(part, PAIR)), gain_mlp)
-        down_w, slope, scale, unit, part = mlp(quarter_id, normed_mlp, pieces, ff_block)
+        late = ()
+        if layer + 1 < layer_count:
+            next_attn = attn_sets[layer + 1][1]
+            attn_other = flip(others(ids, next_attn, half_depth, 0, 3, (attended,)), ROW)
+            late = (attn_other,)
+        ff_w, down_w, slope, scale, unit, part = mlp(
+            layer,
+            ids,
+            normed_mlp,
+            (ff_sets[layer], *spread),
+            ff_weights,
+            ff_block,
+            late,
+        )
         parts = (part, flip(part, PAIR))
+        if layer + 1 < layer_count:
+            early = others(ids, ff_sets[layer + 1], depth, 0, 2, (part,))
         saved_layers.append(
             (
                 qkv_w,
                 out_w,
-                pieces,
+                ff_w,
                 down_w,
                 gain_attn,
                 gain_mlp,
@@ -874,23 +1268,51 @@
 
     def outer_sum(total):
         for bit in outer_bits:
-            total = total.astype(BF16)
-            total = total.astype(F32) + flip(total, bit).astype(F32)
-        return total.astype(BF16)
+            total = add(total, flip(total, bit), steps=1)
+        return total
+
+    def sum_ff(share, after=()):
+        cut = 2 * ff_block
+        totals = cross(share, flip(share[:, :cut], ROW), flip(share[:, cut:], SIDE), after)
+        return [outer_sum(total) for total in totals]
+
+    def spread_ff(totals):
+        gate, up = totals
+        gates, ups = [gate, flip(gate, SIDE)], [up, flip(up, ROW)]
+        for group in (gates, ups):
+            group += [flip(part, PAIR) for part in group]
+        return gates + ups
+
+    def sum_rows(share, cut, after=()):
+        totals = split_sum(
+            share, flip(share[:, :cut], SIDE), flip(share[:, cut:], ROW), after
+        )
+        return [outer_sum(total) for total in totals]
+
+    def spread_rows(totals):
+        by_row, by_side = totals
+        joined = order(ids, (by_row, flip(by_row, ROW), by_side, flip(by_side, SIDE)))
+        return [joined, flip(joined, PAIR)]
+
+    down_cut, attn_cut = 640, 768
+
+    def scatter(total):
+        return lax.psum_scatter(total, "wt", scatter_dimension=0, tiled=total.ndim == 2)
 
     flow = pair_rows(cotangent[0])
     flow, flow_low = flow.astype(F32), flow
     gain_grads = [None] * (2 * layer_count)
-    outs = [
-        shaped((layer_count, *weight.shape[1:]), F32)
-        for weight in (w_query, w_key, w_value, w_out, w_gate, w_up, w_down)
-    ]
-    held = None
+    ff_outs, attn_outs = (
+        [shaped((layer_count, *weight.shape[1:]), F32) for weight in group]
+        for group in ((w_gate, w_up, w_down), (w_query, w_key, w_value, w_out))
+    )
+    ff_held = attn_held = None
+    shares = {}
     for layer in reversed(range(layer_count)):
         (
             qkv_w,
             out_w,
-            pieces,
+            ff_w,
             down_w,
             gain_attn,
             gain_mlp,
@@ -908,14 +1330,19 @@
             scale,
             unit,
         ) = saved_layers[layer]
-        keep, send = down_grad(spot, unit, flow_low)
-        down_sum = (keep.astype(F32) + flip(send, ROW).astype(F32)).astype(BF16)
-        down_share = lax.psum_scatter(down_sum, "wt", scatter_dimension=0, tiled=False)
-        keep, send, part = mlp_back(flow_low, normed_mlp, slope, scale, down_w, pieces)
-        ff_sum = (keep.astype(F32) + flip(send, SIDE).astype(F32)).astype(BF16)
-        ff_share = lax.psum_scatter(ff_sum, "wt", scatter_dimension=0, tiled=True)
+        older = shares.get(layer + 1)
+        row_keep, row_send, side_keep, side_send = down_grad(ids, unit, flow_low, down_cut)
+        down_parts = (row_keep, flip(row_send, ROW)), (side_keep, flip(side_send, SIDE))
+        done = (row_keep,) if older is None else (row_keep, attn_all)
+        gate_keep, gate_send, up_keep, up_send, part = mlp_back(
+            flow_low, normed_mlp, slope, scale, down_w, ff_w, after=done
+        )
+        gate_got, up_got = flip(gate_send, SIDE), flip(up_send, ROW)
+        done = () if older is None else (older["ff"],)
+        part, down_sum = add_two(*down_parts, done, part)
+        done = (down_sum,)
         flow, flow_low, gain_grads[layer_count + layer] = norm_back(
-            flow, (part, flip(part, PAIR)), residual_mid, gain_mlp
+            flow, (part, flip(part, PAIR)), residual_mid, gain_mlp, after=done
         )
         attended_grad = dot_nt(out_w, flow_low).astype(BF16)
         query_grad, own_grad, shared_grad = attend_back(
@@ -930,50 +1357,43 @@
             cosine,
             sine,
         )
-        for bit in reversed([SIDE, ROW] + outer_bits):
+        for bit in reversed(key_bits):
             half = shared_grad.shape[0] // 2
             arrived = flip(shared_grad[half:].astype(BF16), bit)
             shared_grad = shared_grad[:half] + arrived.astype(F32)
-        grad_qkv = merge(query_grad, own_grad, shared_grad, cosine, sine)
+            if bit == key_bits[-1]:
+                started = shared_grad
+        shares[layer] = {"down": scatter(down_sum)}
+        done = (started, shares[layer]["down"])
+        if older is not None:
+            done = (*done, older["attn"])
+        ff_sum = add_two((gate_keep, gate_got), (up_keep, up_got), done)
+        shares[layer]["ff"] = scatter(ff_sum)
+        down_totals = sum_rows(shares[layer]["down"], down_cut, (ff_sum,))
+        done = (ff_sum, down_totals[0])
+        if older is not None:
+            ff_totals = sum_ff(older["ff"], (ff_sum,))
+            attn_totals = sum_rows(older["attn"], attn_cut, (ff_sum,))
+            done = (*done, ff_totals[0], attn_totals[0])
+        grad_qkv = merge(query_grad, own_grad, shared_grad, cosine, sine, done)
         part = dot_nt(grad_qkv, qkv_w).astype(BF16)
-        flow, flow_low_next, gain_grads[layer] = norm_back(
-            flow, (part, flip(part, PAIR)), residual, gain_attn
-        )
-        qkv_part = dot_tn(normed_attn, grad_qkv).astype(BF16)
-        out_part = dot_nn(attended, flow_low).astype(BF16)
-        flow_low = flow_low_next
-        attn_sums = []
-        for whole_part in (qkv_part, out_part):
-            split = whole_part.reshape(-1, 2, half_depth, whole_part.shape[1])
-            kept = lax.dynamic_index_in_dim(split, row, 1, keepdims=False)
-            sent = lax.dynamic_index_in_dim(split, 1 - row, 1, keepdims=False)
-            attn_sums.append((kept.astype(F32) + flip(sent, ROW).astype(F32)).astype(BF16))
-        qkv_sum, out_sum = attn_sums
-        kept = lax.dynamic_slice(
-            out_sum, (0, 0, half_width * pair), (wt_count // 2, half_depth, half_width)
-        )
-        sent = lax.dynamic_slice(
-            out_sum, (0, 0, half_width * (1 - pair)), (wt_count // 2, half_depth, half_width)
-        )
-        out_all = jnp.concatenate(ordered(pair, kept, flip(sent, PAIR)), axis=0)
-        attn_share = lax.psum_scatter(
-            jnp.concatenate([qkv_sum, out_all], axis=2), "wt", scatter_dimension=0, tiled=False
-        )
-
-        swapped = flip(ff_share, ROW)
-        cut = 2 * ff_block
-        swapped = jnp.concatenate([swapped[:, cut:], swapped[:, :cut]], axis=1)
-        ff_total = outer_sum(ff_share.astype(F32) + swapped.astype(F32))
-        ff_mine = jnp.stack([ff_total, flip(ff_total, SIDE)])
-        ff_other = flip(ff_mine, PAIR)
-        placed = [ff_mine, ff_other]
-        for share in (down_share, attn_share):
-            total = outer_sum(share.astype(F32) + flip(share, SIDE).astype(F32))
-            joined = jnp.concatenate(ordered(row, total, flip(total, ROW)), axis=0)
-            placed += [joined, flip(joined, PAIR)]
-        held = place(layer, where, placed, outs, held)
-    token_grad = own_rows(flow)
-
+        shares[layer]["down"] = spread_rows(down_totals)
+        done = (shares[layer]["down"][0],)
+        if older is not None:
+            older["ff"] = spread_ff(ff_totals)
+            older["attn"] = spread_rows(attn_totals)
+            done = (*done, older["ff"][1], older["ff"][5], older["attn"][0])
+        row_keep, row_send, side_keep, side_send = attn_grad(
+            ids, normed_attn, grad_qkv, attended, flow_low, attn_cut, done
+        )
+        attn_mine, send = attn_sum(
+            pair[None], (row_keep, flip(row_send, ROW), side_keep, flip(side_send, SIDE))
+        )
+        flow, flow_low, gain_grads[layer] = norm_back(
+            flow, (part, flip(part, PAIR)), residual, gain_attn, after=(attn_mine,)
+        )
+        attn_all = attn_join(pair[None], attn_mine, flip(send, PAIR))
+        shares[layer]["attn"] = scatter(attn_all)
     gain_total = jnp.concatenate(gain_grads, axis=0)
     for bit in [SIDE, ROW] + outer_bits:
         gain_total = gain_total + flip(gain_total, bit)
@@ -981,10 +1401,26 @@
     while bit < wt_count:
         gain_total = gain_total + flip(gain_total, bit, "wt", wt_count)
         bit *= 2
+    for layer in reversed(range(layer_count)):
+        share = shares[layer]
+        if layer == 0:
+            share["ff"] = spread_ff(sum_ff(share["ff"], (placed, attn_placed)))
+        *ff_held, placed = place(
+            place_ff_kernel, layer, where, share["ff"] + share["down"], ff_outs, ff_held, (flow_low,)
+        )
+        if layer == 0:
+            totals = sum_rows(share["attn"], attn_cut, (placed, gain_total))
+            share["attn"] = spread_rows(totals)
+        *attn_held, attn_placed = place(
+            place_attn_kernel, layer, where, share["attn"], attn_outs, attn_held, (flow_low,)
+        )
+    query_out, key_out, value_out, out_out = attn_held
+    gate_out, up_out, down_out = ff_held
+    token_grad = own_rows(flow)
+
     gain_share = lax.dynamic_slice(
         gain_total, (0, lax.axis_index("wt") * depth), (2 * layer_count, depth)
     )
-    query_out, key_out, value_out, out_out, gate_out, up_out, down_out = held
     return (
         layer_out[None],
         token_grad[None],

time: 1020 us -> 789 us (0.77)
  waiting for transfers between devices: 551 us -> 229 us
  local copies, waits for them, and re-layouts: 99.2 us -> 162 us
  Pallas kernels: 216 us -> 256 us
  other arithmetic: 61.5 us -> 21.8 us
  starting transfers between devices: 42.8 us -> 76.4 us
  matrix products: 31.1 us -> 20.1 us
    ppermute x62 -> x92, waiting for transfers between devices: 470 us -> 180 us  [flip(): return lax.ppermute(value, axis, [(i, i ^ bit) for i in range(count)])]
    unnamed x228 -> x394, local copies, waits for them, and re-layouts: 49.6 us -> 116 us
    pallas_call x24 -> x56, Pallas kernels: 216 us -> 256 us  [call(): pl.pallas_call(body, out_shape=outs, in_specs=(in_specs or [WHOLE] * coun...]
    ppermute x62 -> x92, starting transfers between devices: 42 us -> 75 us  [flip(): return lax.ppermute(value, axis, [(i, i ^ bit) for i in range(count)])]
    all_gather x4, waiting for transfers between devices: 80.5 us -> 48.9 us  [the longest x2 42.8 us: attn_gather(): return (local, lax.all_gather(piece, 'wt', axis=0, tiled=False))]
    convert_element_type x14 -> x0, other arithmetic: 23.6 us -> none  [the longest x2 10.7 us: per_device(): ff_sum = (keep.astype(F32) + flip(send, SIDE).astype(F32)).astype(BF16)]
    slice x17 -> x12, local copies, waits for them, and re-layouts: 21.5 us -> 7.82 us  [the longest x2 3.23 us: sum_ff(): share[:, cut:]]
  transfers between devices with their start and end apart: 72 -> 102, of which waited for: 34 -> 42; matrix products, arithmetic and copies ran while one was open for 13% -> 10% of each run, Pallas kernels for 16% -> 28%
where the time goes in v2:
time: 789 us; the launch traced here: 782 us
  Pallas kernels  256 us (32%)
  waiting for transfers between devices  229 us (29%)
  local copies, waits for them, and re-layouts  162 us (21%)
  starting transfers between devices  76.4 us (10%)
  other arithmetic  21.8 us (3%)
  matrix products  20.1 us (3%)
  between operations  16.7 us (2%)
    pallas_call x56, Pallas kernels, call(): pl.pallas_call(body, out_shape=outs, in_specs=(in_specs or [WHOLE] * coun...  256 us
    ppermute x92, waiting for transfers between devices, flip(): return lax.ppermute(value, axis, [(i, i ^ bit) for i in range(count)])  180 us
    unnamed x394, local copies, waits for them, and re-layouts  116 us
    ppermute x92, starting transfers between devices, flip(): return lax.ppermute(value, axis, [(i, i ^ bit) for i in range(count)])  75 us
    all_gather x2, waiting for transfers between devices, attn_gather(): return (local, lax.all_gather(piece, 'wt', axis=0, tiled=False))  42.8 us
  transfers between devices with their start and end apart: 102, of which 42 were waited for; matrix products, arithmetic and copies ran while one was open for 10% of the time, Pallas kernels for 28%

profile of v2, /device:TPU:0, one launch (start us, length us, event | category | flops | bytes accessed | tf_op | source)
XLA Modules:
  0.0 782.0 jit_solution(18225640812045184941)
XLA Ops:
  37.3 28.9 %all-gather.9.cloned.1.call-done = bf16[640,1536]{1,0:T(8,128)(2,1)} async-done(((bf16[160,1536]{1,0:T(8,128)(2,1)}), bf16[640,1536]{1,0:T(8,128)(2,1)}) %all-gather.9.cloned.1.call-update) | async-done | bytes 1966096 | tf_op jit(solution)/shard_map/all_gather | solution.py:1163
  75.8 24.8 %collective-permute-done.1.refs_3_ = bf16[3,144,1536]{2,1,0:T(8,128)(2,1)} collective-permute-done((bf16[3,144,1536]{2,1,0:T(8,128)(2,1)}, bf16[3,144,1536]{2,1,0:T(8,128)(2,1)}, u32[]{:S(2)}, u32[]{:S(2)}) %collective-permute-start.1) | collective-permute-done | bytes 1327136 | tf_op jit(solution)/shard_map/ppermute | solution.py:1097
  116.4 6.2 all-gather.11.cloned.1.call-done
  136.7 11.8 %shard_map.219 = (bf16[576,640]{1,0:T(8,128)(2,1)S(1)}, f32[9,1,640]{2,1,0:T(1,128)S(1)}) custom-call(bf16[576,640]{1,0:T(8,128)(2,1)S(1)} %copy-done.80, bf16[640,384]{1,0:T(8,128)(2,1)S(1)} %copy-done.94, bf16[384,640]{1,0:T(8,128)(2,1)S(1)} %copy-done.97, bf16[512,384]{1,0:T(8,128)(2,1)S(1)} %pad_maximum_fusion.7.refs_2_.refs_3_.refs_4_, ...), custom_call_target="tpu_custom_call" | custom-call | flops 1 | bytes 1 | tf_op jit(solution)/shard_map/pallas_call | solution.py:71
  149.9 13.9 %all-gather.13.cloned.1.call-done = bf16[576,1536]{1,0:T(8,128)(2,1)} async-done(((bf16[144,1536]{1,0:T(8,128)(2,1)}), bf16[576,1536]{1,0:T(8,128)(2,1)}) %all-gather.13.cloned.1.call-update) | async-done | bytes 1769488 | tf_op jit(solution)/shard_map/all_gather | solution.py:1163
  179.0 6.1 collective-permute-done.12.refs_9_
  196.7 10.3 %collective-permute-done.13.refs_10_ = bf16[144,1152]{1,0:T(8,128)(2,1)} collective-permute-done((bf16[144,1152]{1,0:T(8,128)(2,1)}, bf16[144,1152]{1,0:T(8,128)(2,1)}, u32[]{:S(2)}, u32[]{:S(2)}) %collective-permute-start.13) | collective-permute-done | bytes 331808 | tf_op jit(solution)/shard_map/ppermute | solution.py:1097
  207.0 6.1 collective-permute-done.11.refs_8_
  213.0 18.9 %shard_map.222 = (bf16[4,1152,768]{2,1,0:T(8,128)(2,1)}, bf16[1536,1152]{1,0:T(8,128)(2,1)}, bf16[640,1536]{1,0:T(8,128)(2,1)}, bf16[640,1536]{1,0:T(8,128)(2,1)...) custom-call(s32[5]{0:T(128)} %copy-done.147, bf16[640,1152]{1,0:T(8,128)(2,1)} %copy-done.47, ...), custom_call_target="tpu_custom_call" | custom-call | flops 1 | bytes 1 | tf_op jit(solution)/shard_map/pallas_call | solution.py:71
  260.3 8.5 %collective-permute-done.16.refs_3_ = bf16[2,288,1152]{2,1,0:T(8,128)(2,1)} collective-permute-done((bf16[2,288,1152]{2,1,0:T(8,128)(2,1)}, bf16[2,288,1152]{2,1,0:T(8,128)(2,1)}, u32[]{:S(2)}, u32[]{:S(2)}) %collective-permute-start.16) | collective-permute-done | bytes 1327136 | tf_op jit(solution)/shard_map/ppermute | solution.py:1097
  284.9 12.2 %shard_map.229 = (bf16[576,640]{1,0:T(8,128)(2,1)S(1)}, f32[9,1,640]{2,1,0:T(1,128)S(1)}) custom-call(bf16[576,640]{1,0:T(8,128)(2,1)S(1)} %get-tuple-element.129.refs_0_, bf16[640,384]{1,0:T(8,128)(2,1)S(1)} %get-tuple-element.130.refs_1_.refs_2_, bf16[384,640]{1,0:T(8,128)(2,1)S(1)} %get-tuple-element.131.refs_2_.refs_3_, ...), custom_call_target="tpu_custom_call" | custom-call | flops 1 | bytes 1 | tf_op jit(solution)/shard_map/pallas_call | solution.py:71
  304.0 7.6 collective-permute-done.23.refs_6_
  326.6 18.7 %shard_map.231 = (bf16[4,1152,768]{2,1,0:T(8,128)(2,1)}, bf16[1536,1152]{1,0:T(8,128)(2,1)}, bf16[640,1536]{1,0:T(8,128)(2,1)}, bf16[640,1536]{1,0:T(8,128)(2,1)...) custom-call(s32[5]{0:T(128)} %copy-done.147, bf16[640,1152]{1,0:T(8,128)(2,1)} %copy-done.53, ...), custom_call_target="tpu_custom_call" | custom-call | flops 1 | bytes 1 | tf_op jit(solution)/shard_map/pallas_call | solution.py:71
  345.3 7.2 shard_map.232
  356.2 24.6 %shard_map.233 = (bf16[1152,768]{1,0:T(8,128)(2,1)}, bf16[1152,768]{1,0:T(8,128)(2,1)}, bf16[1152,768]{1,0:T(8,128)(2,1)}, bf16[1152,768]{1,0:T(8,128)(2,1)}, bf16[640,1152]{1,0:T(8,128)(2,1)}) custom-call(bf16[640,1152]{1,0:T(8,128)(2,1)} %get-tuple-element.235.refs_2_.refs_0_, bf16[640,1152]{1,0:T(8,128)(2,1)} %copy-done.53, ...), custom_call_target="tpu_custom_call" | custom-call | flops 1 | bytes 1 | tf_op jit(solution)/shard_map/pallas_call | solution.py:71
  406.0 22.6 %shard_map.236 = (bf16[576,640]{1,0:T(8,128)(2,1)}, f32[512,384]{1,0:T(8,128)}, f32[512,384]{1,0:T(8,128)}) custom-call(bf16[576,640]{1,0:T(8,128)(2,1)} %copy-done.81, bf16[576,640]{1,0:T(8,128)(2,1)} %convolution_convert_fusion.5.refs_1_, bf16[640,384]{1,0:T(8,128)(2,1)} %copy-done.95, bf16[384,640]{1,0:T(8,128)(2,1)} %copy-done.98, ...), custom_call_target="tpu_custom_call" | custom-call | flops 1 | bytes 1 | tf_op jit(solution)/shard_map/pallas_call | solution.py:71
  430.1 6.6 collective-permute-done.33
  466.3 5.3 shard_map.241
  474.1 16.6 %collective-permute-done.42.refs_2_ = bf16[4,144,768]{2,1,0:T(8,128)(2,1)S(1)} collective-permute-done((bf16[4,144,768]{2,1,0:T(8,128)(2,1)S(1)}, bf16[4,144,768]{2,1,0:T(8,128)(2,1)S(1)}, u32[]{:S(2)}, u32[]{:S(2)}) %collective-permute-start.42) | collective-permute-done | bytes 884768 | tf_op jit(solution)/shard_map/ppermute | solution.py:1097
  507.8 7.4 shard_map.244
  520.2 24.9 %shard_map.246 = (bf16[1152,768]{1,0:T(8,128)(2,1)}, bf16[1152,768]{1,0:T(8,128)(2,1)}, bf16[1152,768]{1,0:T(8,128)(2,1)}, bf16[1152,768]{1,0:T(8,128)(2,1)}, bf16[640,1152]{1,0:T(8,128)(2,1)}) custom-call(bf16[640,1152]{1,0:T(8,128)(2,1)} %copy-done.50, bf16[640,1152]{1,0:T(8,128)(2,1)} %copy-done.47, bf16[640,1536]{1,0:T(8,128)(2,1)} %get-tuple-element.172.refs_2_, ...), custom_call_target="tpu_custom_call" | custom-call | flops 1 | bytes 1 | tf_op jit(solution)/shard_map/pallas_call | solution.py:71
  571.5 22.6 %shard_map.249 = (bf16[576,640]{1,0:T(8,128)(2,1)}, f32[512,384]{1,0:T(8,128)}, f32[512,384]{1,0:T(8,128)}) custom-call(bf16[576,640]{1,0:T(8,128)(2,1)} %copy-done.79, bf16[576,640]{1,0:T(8,128)(2,1)} %convolution_convert_fusion.4.refs_1_, bf16[640,384]{1,0:T(8,128)(2,1)} %copy-done.93, bf16[384,640]{1,0:T(8,128)(2,1)} %copy-done.96, ...), custom_call_target="tpu_custom_call" | custom-call | flops 1 | bytes 1 | tf_op jit(solution)/shard_map/pallas_call | solution.py:71
  596.0 6.1 collective-permute-done.48
  623.6 11.5 %collective-permute-done.56.refs_1_ = bf16[144,768]{1,0:T(8,128)(2,1)S(1)} collective-permute-done((bf16[144,768]{1,0:T(8,128)(2,1)S(1)}, bf16[144,768]{1,0:T(8,128)(2,1)S(1)}, u32[]{:S(2)}, u32[]{:S(2)}) %collective-permute-start.56) | collective-permute-done | bytes 221216 | tf_op jit(solution)/shard_map/ppermute | solution.py:1097
  644.9 11.3 %collective-permute-done.49 = bf16[128,384]{1,0:T(8,128)(2,1)S(1)} collective-permute-done((bf16[128,384]{1,0:T(8,128)(2,1)S(1)}, bf16[128,384]{1,0:T(8,128)(2,1)S(1)}, u32[]{:S(2)}, u32[]{:S(2)}) %collective-permute-start.49) | collective-permute-done | bytes 98336 | tf_op jit(solution)/shard_map/ppermute | solution.py:1097
  665.6 5.3 shard_map.257
  676.1 12.4 %collective-permute-done.65.refs_2_ = bf16[4,144,768]{2,1,0:T(8,128)(2,1)S(1)} collective-permute-done((bf16[4,144,768]{2,1,0:T(8,128)(2,1)S(1)}, bf16[4,144,768]{2,1,0:T(8,128)(2,1)S(1)}, u32[]{:S(2)}, u32[]{:S(2)}) %collective-permute-start.65) | collective-permute-done | bytes 884768 | tf_op jit(solution)/shard_map/ppermute | solution.py:1097
  699.2 4.4 shard_map.259
  715.8 4.8 add_add_fusion
  723.9 7.3 shard_map.261
  738.7 5.3 collective-permute-done.82.refs_2_
  751.0 7.3 shard_map.264
  (743 shorter events, 377.9 us)
Async XLA Ops:
  7.2 59.0 %all-gather.9.cloned.1.call-start = ((), (), s32[]{:S(2)}) async-start(), calls=%async_computation.12 | async-start | bytes 2457600 | tf_op jit(solution)/shard_map/all_gather | solution.py:1163
  19.8 102.8 %all-gather.11.cloned.1.call-start = ((), (), s32[]{:S(2)}) async-start(), calls=%async_computation.13 | async-start | bytes 3317760 | tf_op jit(solution)/shard_map/all_gather | solution.py:1174
  25.5 138.3 %all-gather.13.cloned.1.call-start = ((), (), s32[]{:S(2)}) async-start(), calls=%async_computation.14 | async-start | bytes 2211840 | tf_op jit(solution)/shard_map/all_gather | solution.py:1163
  29.7 202.9 %all-gather.15.cloned.1.call-start = ((), (), s32[]{:S(2)}) async-start(), calls=%async_computation.15 | async-start | bytes 3317760 | tf_op jit(solution)/shard_map/all_gather | solution.py:1174
  29.7 41.6 %collective-permute-start = (bf16[320,1152]{1,0:T(8,128)(2,1)}, bf16[320,1152]{1,0:T(8,128)(2,1)}, u32[]{:S(2)}, u32[]{:S(2)}) collective-permute-start(bf16[320,1152]{1,0:T(8,128)(2,1)} %bitcast.91), channel_id=1, source_target_pairs={{0,4},{4,0},{8,12},{12,8},{16,20},{20,16},{24,28},{28,24},{1,5},{5... | collective-permute-start | bytes 2211848 | tf_op jit(solution)/shard_map/ppermute | solution.py:1097
  36.0 404.3 %reduce-scatter.7.cloned.1.call-start = ((), (), s32[]{:S(2)}) async-start(), calls=%async_computation.6 | async-start | bytes 2211840 | tf_op jit(solution)/shard_map/reduce_scatter | solution.py:1300
  69.4 31.2 %collective-permute-start.1 = (bf16[3,144,1536]{2,1,0:T(8,128)(2,1)}, bf16[3,144,1536]{2,1,0:T(8,128)(2,1)}, u32[]{:S(2)}, u32[]{:S(2)}) collective-permute-start(bf16[3,144,1536]{2,1,0:T(8,128)(2,1)} %shard_map.212), channel_id=1, source_target_pairs={{0,16},{4,20},{8,24},{12,28},{16,0},{20,4},{24,8},{28,12},{1,17},{... | collective-permute-start | bytes 3981320 | tf_op jit(solution)/shard_map/ppermute | solution.py:1097
  108.7 59.3 %collective-permute-start.4 = (bf16[576,576]{1,0:T(8,128)(2,1)}, bf16[576,576]{1,0:T(8,128)(2,1)}, u32[]{:S(2)}, u32[]{:S(2)}) collective-permute-start(bf16[576,576]{1,0:T(8,128)(2,1)} %constant_dynamic-slice_fusion.8), channel_id=1, source_target_pairs={{0,4},{4,0},{8,12},{12,8},{16,20},{20,16},{24,28},{28,24},{1,5},{5... | collective-permute-start | bytes 1990664 | tf_op jit(solution)/shard_map/ppermute | solution.py:1097
  126.0 48.5 %collective-permute-start.6 = (bf16[2,288,1152]{2,1,0:T(8,128)(2,1)}, bf16[2,288,1152]{2,1,0:T(8,128)(2,1)}, u32[]{:S(2)}, u32[]{:S(2)}) collective-permute-start(bf16[2,288,1152]{2,1,0:T(8,128)(2,1)} %shard_map.217.refs_6_), channel_id=1, source_target_pairs={{0,16},{4,20},{8,24},{12,28},{16,0},{20,4},{24,8},{28,12},{1,17},{... | collective-permute-start | bytes 3981320 | tf_op jit(solution)/shard_map/ppermute | solution.py:1097
  128.9 44.1 %collective-permute-start.7 = (bf16[1,288,1152]{2,1,0:T(8,128)(2,1)}, bf16[1,288,1152]{2,1,0:T(8,128)(2,1)}, u32[]{:S(2)}, u32[]{:S(2)}) collective-permute-start(bf16[1,288,1152]{2,1,0:T(8,128)(2,1)} %shard_map.218.refs_7_), channel_id=1, source_target_pairs={{0,16},{4,20},{8,24},{12,28},{16,0},{20,4},{24,8},{28,12},{1,17},{... | collective-permute-start | bytes 1990664 | tf_op jit(solution)/shard_map/ppermute | solution.py:1097
  130.5 47.9 %collective-permute-start.9 = (bf16[1,288,1152]{2,1,0:T(8,128)(2,1)}, bf16[1,288,1152]{2,1,0:T(8,128)(2,1)}, u32[]{:S(2)}, u32[]{:S(2)}) collective-permute-start(bf16[1,288,1152]{2,1,0:T(8,128)(2,1)} %shard_map.218.refs_7_), channel_id=1, source_target_pairs={{0,8},{4,12},{8,0},{12,4},{16,24},{20,28},{24,16},{28,20},{1,9},{5... | collective-permute-start | bytes 1990664 | tf_op jit(solution)/shard_map/ppermute | solution.py:1097
  132.0 75.0 %collective-permute-start.8 = (bf16[2,288,1152]{2,1,0:T(8,128)(2,1)}, bf16[2,288,1152]{2,1,0:T(8,128)(2,1)}, u32[]{:S(2)}, u32[]{:S(2)}) collective-permute-start(bf16[2,288,1152]{2,1,0:T(8,128)(2,1)} %shard_map.217.refs_6_), channel_id=1, source_target_pairs={{0,8},{4,12},{8,0},{12,4},{16,24},{20,28},{24,16},{28,20},{1,9},{5... | collective-permute-start | bytes 3981320 | tf_op jit(solution)/shard_map/ppermute | solution.py:1097
  168.1 38.9 %collective-permute-start.14 = (bf16[3,144,1536]{2,1,0:T(8,128)(2,1)}, bf16[3,144,1536]{2,1,0:T(8,128)(2,1)}, u32[]{:S(2)}, u32[]{:S(2)}) collective-permute-start(bf16[3,144,1536]{2,1,0:T(8,128)(2,1)} %shard_map.221), channel_id=1, source_target_pairs={{0,16},{4,20},{8,24},{12,28},{16,0},{20,4},{24,8},{28,12},{1,17},{... | collective-permute-start | bytes 3981320 | tf_op jit(solution)/shard_map/ppermute | solution.py:1097
  178.5 28.5 %collective-permute-start.10 = (bf16[288,1152]{1,0:T(8,128)(2,1)}, bf16[288,1152]{1,0:T(8,128)(2,1)}, u32[]{:S(2)}, u32[]{:S(2)}) collective-permute-start(bf16[288,1152]{1,0:T(8,128)(2,1)} %get-tuple-element.246), channel_id=1, source_target_pairs={{0,8},{4,12},{8,0},{12,4},{16,24},{20,28},{24,16},{28,20},{1,9},{5... | collective-permute-start | bytes 1990664 | tf_op jit(solution)/shard_map/ppermute | solution.py:1097
  185.2 27.9 %collective-permute-start.11 = (bf16[288,1152]{1,0:T(8,128)(2,1)}, bf16[288,1152]{1,0:T(8,128)(2,1)}, u32[]{:S(2)}, u32[]{:S(2)}) collective-permute-start(bf16[288,1152]{1,0:T(8,128)(2,1)} %get-tuple-element.245), channel_id=1, source_target_pairs={{0,8},{4,12},{8,0},{12,4},{16,24},{20,28},{24,16},{28,20},{1,9},{5... | collective-permute-start | bytes 1990664 | tf_op jit(solution)/shard_map/ppermute | solution.py:1097
  237.3 31.5 %collective-permute-start.16 = (bf16[2,288,1152]{2,1,0:T(8,128)(2,1)}, bf16[2,288,1152]{2,1,0:T(8,128)(2,1)}, u32[]{:S(2)}, u32[]{:S(2)}) collective-permute-start(bf16[2,288,1152]{2,1,0:T(8,128)(2,1)} %shard_map.226.refs_6_), channel_id=1, source_target_pairs={{0,16},{4,20},{8,24},{12,28},{16,0},{20,4},{24,8},{28,12},{1,17},{... | collective-permute-start | bytes 3981320 | tf_op jit(solution)/shard_map/ppermute | solution.py:1097
  237.9 31.1 %collective-permute-start.17 = (bf16[2,288,1152]{2,1,0:T(8,128)(2,1)}, bf16[2,288,1152]{2,1,0:T(8,128)(2,1)}, u32[]{:S(2)}, u32[]{:S(2)}) collective-permute-start(bf16[2,288,1152]{2,1,0:T(8,128)(2,1)} %shard_map.226.refs_6_), channel_id=1, source_target_pairs={{0,8},{4,12},{8,0},{12,4},{16,24},{20,28},{24,16},{28,20},{1,9},{5... | collective-permute-start | bytes 3981320 | tf_op jit(solution)/shard_map/ppermute | solution.py:1097
  280.4 44.3 %collective-permute-start.24 = (bf16[288,1152]{1,0:T(8,128)(2,1)}, bf16[288,1152]{1,0:T(8,128)(2,1)}, u32[]{:S(2)}, u32[]{:S(2)}) collective-permute-start(bf16[288,1152]{1,0:T(8,128)(2,1)} %slice_bitcast_fusion.1), channel_id=1, source_target_pairs={{0,8},{4,12},{8,0},{12,4},{16,24},{20,28},{24,16},{28,20},{1,9},{5... | collective-permute-start | bytes 1990664 | tf_op jit(solution)/shard_map/ppermute | solution.py:1097
  284.3 27.2 %collective-permute-start.23 = (bf16[1,288,1152]{2,1,0:T(8,128)(2,1)S(1)}, bf16[1,288,1152]{2,1,0:T(8,128)(2,1)S(1)}, u32[]{:S(2)}, u32[]{:S(2)}) collective-permute-start(bf16[1,288,1152]{2,1,0:T(8,128)(2,1)S(1)} %shard_map.228.refs_7_), channel_id=1, source_target_pairs={{0,8},{4,12},{8,0},{12,4},{16,24},{20,28},{24,16},{28,20},{1,9},{5... | collective-permute-start | bytes 1990664 | tf_op jit(solution)/shard_map/ppermute | solution.py:1097
  354.3 26.6 %collective-permute-start.30 = (bf16[4,192,640]{2,1,0:T(8,128)(2,1)}, bf16[4,192,640]{2,1,0:T(8,128)(2,1)}, u32[]{:S(2)}, u32[]{:S(2)}) collective-permute-start(bf16[4,192,640]{2,1,0:T(8,128)(2,1)} %get-tuple-element.138), channel_id=1, source_target_pairs={{0,16},{4,20},{8,24},{12,28},{16,0},{20,4},{24,8},{28,12},{1,17},{... | collective-permute-start | bytes 2949128 | tf_op jit(solution)/shard_map/ppermute | solution.py:1097
  389.6 155.6 %reduce-scatter.9.cloned.1.call-start = ((), (), s32[]{:S(2)}) async-start(), calls=%async_computation.7 | async-start | bytes 4423680 | tf_op jit(solution)/shard_map/reduce_scatter | solution.py:1300
  389.7 48.1 %collective-permute-start.35 = (bf16[1152,768]{1,0:T(8,128)(2,1)}, bf16[1152,768]{1,0:T(8,128)(2,1)S(1)}, u32[]{:S(2)}, u32[]{:S(2)}) collective-permute-start(bf16[1152,768]{1,0:T(8,128)(2,1)} %get-tuple-element.155), channel_id=1, source_target_pairs={{0,8},{4,12},{8,0},{12,4},{16,24},{20,28},{24,16},{28,20},{1,9},{5... | collective-permute-start | bytes 5308424 | tf_op jit(solution)/shard_map/ppermute | solution.py:1097
  390.4 48.7 %collective-permute-start.36 = (bf16[1152,768]{1,0:T(8,128)(2,1)}, bf16[1152,768]{1,0:T(8,128)(2,1)S(1)}, u32[]{:S(2)}, u32[]{:S(2)}) collective-permute-start(bf16[1152,768]{1,0:T(8,128)(2,1)} %get-tuple-element.157), channel_id=1, source_target_pairs={{0,16},{4,20},{8,24},{12,28},{16,0},{20,4},{24,8},{28,12},{1,17},{... | collective-permute-start | bytes 5308424 | tf_op jit(solution)/shard_map/ppermute | solution.py:1097
  449.8 155.9 %reduce-scatter.13.cloned.1.call-start = ((), (), s32[]{:S(2)}) async-start(), calls=%async_computation.9 | async-start | bytes 2211840 | tf_op jit(solution)/shard_map/reduce_scatter | solution.py:1300
  496.7 109.0 %reduce-scatter.11.cloned.1.call-start = ((), (), s32[]{:S(2)}) async-start(), calls=%async_computation.8 | async-start | bytes 2211840 | tf_op jit(solution)/shard_map/reduce_scatter | solution.py:1300
  518.1 27.0 %collective-permute-start.44 = (bf16[4,192,640]{2,1,0:T(8,128)(2,1)}, bf16[4,192,640]{2,1,0:T(8,128)(2,1)}, u32[]{:S(2)}, u32[]{:S(2)}) collective-permute-start(bf16[4,192,640]{2,1,0:T(8,128)(2,1)} %get-tuple-element.169), channel_id=1, source_target_pairs={{0,16},{4,20},{8,24},{12,28},{16,0},{20,4},{24,8},{28,12},{1,17},{... | collective-permute-start | bytes 2949128 | tf_op jit(solution)/shard_map/ppermute | solution.py:1097
  555.1 155.2 %reduce-scatter.17.cloned.1.call-start = ((), (), s32[]{:S(2)}) async-start(), calls=%async_computation.11 | async-start | bytes 4423680 | tf_op jit(solution)/shard_map/reduce_scatter | solution.py:1300
  555.4 47.8 %collective-permute-start.50 = (bf16[1152,768]{1,0:T(8,128)(2,1)}, bf16[1152,768]{1,0:T(8,128)(2,1)S(1)}, u32[]{:S(2)}, u32[]{:S(2)}) collective-permute-start(bf16[1152,768]{1,0:T(8,128)(2,1)} %get-tuple-element.187), channel_id=1, source_target_pairs={{0,8},{4,12},{8,0},{12,4},{16,24},{20,28},{24,16},{28,20},{1,9},{5... | collective-permute-start | bytes 5308424 | tf_op jit(solution)/shard_map/ppermute | solution.py:1097
  556.6 47.9 %collective-permute-start.51 = (bf16[1152,768]{1,0:T(8,128)(2,1)}, bf16[1152,768]{1,0:T(8,128)(2,1)S(1)}, u32[]{:S(2)}, u32[]{:S(2)}) collective-permute-start(bf16[1152,768]{1,0:T(8,128)(2,1)} %get-tuple-element.189), channel_id=1, source_target_pairs={{0,16},{4,20},{8,24},{12,28},{16,0},{20,4},{24,8},{28,12},{1,17},{... | collective-permute-start | bytes 5308424 | tf_op jit(solution)/shard_map/ppermute | solution.py:1097
  616.1 128.8 %reduce-scatter.15.cloned.1.call-start = ((), (), s32[]{:S(2)}) async-start(), calls=%async_computation.10 | async-start | bytes 2211840 | tf_op jit(solution)/shard_map/reduce_scatter | solution.py:1300
  637.6 27.7 %collective-permute-start.61 = (bf16[288,768]{1,0:T(8,128)(2,1)S(1)}, bf16[288,768]{1,0:T(8,128)(2,1)S(1)}, u32[]{:S(2)}, u32[]{:S(2)}) collective-permute-start(bf16[288,768]{1,0:T(8,128)(2,1)S(1)} %get-tuple-element.191.refs_7_.refs_1_), channel_id=1, source_target_pairs={{0,8},{4,12},{8,0},{12,4},{16,24},{20,28},{24,16},{28,20},{1,9},{5... | collective-permute-start | bytes 1327112 | tf_op jit(solution)/shard_map/ppermute | solution.py:1097
  638.3 27.1 %collective-permute-start.62 = (bf16[288,768]{1,0:T(8,128)(2,1)S(1)}, bf16[288,768]{1,0:T(8,128)(2,1)S(1)}, u32[]{:S(2)}, u32[]{:S(2)}) collective-permute-start(bf16[288,768]{1,0:T(8,128)(2,1)S(1)} %get-tuple-element.194.refs_5_), channel_id=1, source_target_pairs={{0,16},{4,20},{8,24},{12,28},{16,0},{20,4},{24,8},{28,12},{1,17},{... | collective-permute-start | bytes 1327112 | tf_op jit(solution)/shard_map/ppermute | solution.py:1097
  (267 other events, 2642.6 us)
Sparse Core Ops, SparseCore 0:
  19.9 46.2 all-gather.8
  68.3 54.1 all-gather.10
  124.7 39.0 all-gather.12
  165.8 54.2 all-gather.14
  389.7 36.4 reduce-scatter.6
  449.9 64.3 reduce-scatter.8
  516.8 38.6 reduce-scatter.12
  558.4 37.4 reduce-scatter.10
  616.3 63.6 reduce-scatter.16
  695.1 35.2 reduce-scatter.14

commit v3 on v2

--- a/solution.py
+++ b/solution.py
@@ -61,13 +61,22 @@
 SCALARS = pl.BlockSpec(memory_space=pltpu.SMEM)
 
 
-def call(kernel, outs, ins, flops, limit, out_specs=None, in_specs=None, after=(), **extra):
+def call(
+    kernel, outs, ins, limit, out_specs=None, in_specs=None, after=(), far_in=0, far_out=0, **extra
+):
     count, waited = len(ins), len(after)
 
     def body(*refs):
         kernel(*refs[:count], *refs[count + waited :])
 
-    ins = (*ins, *after)
+    ins = [
+        pltpu.with_memory_space_constraint(value, pltpu.HBM) if index < far_in else value
+        for index, value in enumerate(ins)
+    ]
+    outs = [
+        pltpu.HBM(out.shape, out.dtype) if index < far_out else out
+        for index, out in enumerate(outs)
+    ]
     return pl.pallas_call(
         body,
         out_shape=outs,
@@ -76,7 +85,7 @@
         compiler_params=pltpu.CompilerParams(vmem_limit_bytes=limit << 20),
         cost_estimate=pl.CostEstimate(flops=1, bytes_accessed=1, transcendentals=0),
         **extra,
-    )(*ins)
+    )(*ins, *after)
 
 
 def add_norm_kernel(has_parts, *refs):
@@ -102,8 +111,7 @@
         functools.partial(add_norm_kernel, bool(parts)),
         outs,
         ins,
-        0,
-        16,
+        10,
         in_specs=[block] * (1 + len(parts)) + [line],
         out_specs=[block] * len(outs),
         grid=(rows // step,),
@@ -130,7 +138,7 @@
     gain_ref[...] += jnp.sum(grad * plain, axis=0, keepdims=True)
 
 
-def norm_back(flow, parts, held, gain, after=()):
+def norm_back(flow, parts, held, gain, after=(), pinned=False):
     rows, width = held.shape
     step = 128
     block = pl.BlockSpec((step, width), lambda i: (i, 0))
@@ -139,12 +147,12 @@
         norm_back_kernel,
         [shaped(held.shape, F32), shaped(held.shape, BF16), shaped((1, width), F32)],
         (flow, *parts, held, gain),
-        0,
-        16,
+        12,
         in_specs=[block] * 4 + [line],
         out_specs=[block, block, line],
         grid=(rows // step,),
         after=after,
+        far_in=4 if pinned else 0,
     )
 
 
@@ -177,12 +185,12 @@
         add_two_kernel,
         [shaped(part.shape, part.dtype) for part in extra] + [shaped((*lead, columns), BF16)],
         (*ins, *extra),
-        0,
-        24,
+        12,
         in_specs=[block(*part.shape) for part in (*ins, *extra)],
         out_specs=[block(*part.shape) for part in extra] + [block(*lead, columns)],
         grid=(steps,),
         after=after,
+        far_in=4,
     )
     return result if extra else result[0]
 
@@ -198,8 +206,7 @@
         split_sum_kernel,
         [shaped(row_other.shape, BF16), shaped(side_other.shape, BF16)],
         (share, row_other, side_other),
-        0,
-        16,
+        8,
         after=after,
     )
 
@@ -222,8 +229,7 @@
         order_kernel,
         [shaped((2 * half, cut + parts[2].shape[1]), BF16)],
         (ids, *parts),
-        0,
-        16,
+        8,
         in_specs=[SCALARS] + [WHOLE] * 4,
     )[0]
 
@@ -245,8 +251,7 @@
         cross_kernel,
         [shaped(shape, BF16)] * 2,
         (share, gate_other, up_other),
-        0,
-        16,
+        8,
         after=after,
     )
 
@@ -260,8 +265,7 @@
         add_kernel,
         [shaped(shape, BF16)],
         (mine, other),
-        0,
-        24,
+        12,
         in_specs=[block, block],
         out_specs=[block],
         grid=(steps,),
@@ -303,8 +307,7 @@
             shaped((2 * KEY_HALF, ROWS), BF16),
         ],
         (qkv, cosine, sine),
-        0,
-        32,
+        14,
         after=after,
     )
 
@@ -362,13 +365,11 @@
 
 
 def attend(query, key_value, key_value_turned, shared, key_pos, row_pos, after=()):
-    flops = 4 * QUERY_HALF * ROWS * (shared.shape[0] + CONT)
     return call(
         attend_kernel,
         [shaped((QUERY_HALF, ROWS), BF16), shaped((PAIR_HEADS, 1, ROWS), F32)],
         (query, key_value, key_value_turned, shared, key_pos, row_pos),
-        flops,
-        48,
+        16 + shared.shape[0] // 64,
         after=after,
     )
 
@@ -483,7 +484,6 @@
     query, grad, key_value, key_value_turned, shared, key_pos, row_pos, lse, cosine, sine, after=()
 ):
     count = shared.shape[0]
-    flops = 10 * QUERY_HALF * ROWS * (count + CONT)
     return call(
         attend_back_kernel,
         [
@@ -492,8 +492,7 @@
             shaped((count, 2 * KEY_HALF), F32),
         ],
         (query, grad, key_value, key_value_turned, shared, key_pos, row_pos, lse, cosine, sine),
-        flops,
-        56,
+        22 + count // 64,
         scratch_shapes=[
             pltpu.VMEM((SHARED, count, ROWS), BF16),
             pltpu.VMEM((SHARED, count, ROWS), BF16),
@@ -523,8 +522,7 @@
         merge_kernel,
         [shaped((ROWS, QKV), BF16)],
         (query_grad, own_grad, prompt_grad, cosine, sine),
-        0,
-        32,
+        16,
         after=after,
     )[0]
 
@@ -657,8 +655,7 @@
             shaped((rows, depth), BF16),
         ],
         ins,
-        6 * rows * depth * units,
-        56,
+        32,
         in_specs=[SCALARS, WHOLE] + [FAR] * (len(ins) - 2),
         out_specs=[FAR] + [WHOLE] * 5,
         scratch_shapes=[
@@ -696,10 +693,8 @@
         functools.partial(pack_kernel, layer),
         [shaped((depth, 3 * units // 8), BF16)],
         (ids, *weights),
-        0,
         16,
         in_specs=[SCALARS] + [FAR] * 3,
-        out_specs=[FAR],
         scratch_shapes=[pltpu.SemaphoreType.DMA],
         after=after,
     )[0]
@@ -744,8 +739,7 @@
         functools.partial(down_grad_kernel, cut),
         dealt(4, units // 8, width, cut),
         (ids, unit, flow),
-        2 * rows * units * width,
-        48,
+        16,
         in_specs=[SCALARS, WHOLE, WHOLE],
         after=after,
     )
@@ -817,8 +811,7 @@
         mlp_back_kernel,
         [shaped((depth, 2 * block), BF16)] * 4 + [shaped((rows, depth), BF16)],
         (flow, normed, slope, scale, down, weights),
-        10 * rows * depth * 4 * block,
-        60,
+        40,
         in_specs=[WHOLE] * 5 + [FAR],
         scratch_shapes=[
             pltpu.VMEM((4, depth, 2 * block), BF16),
@@ -827,6 +820,7 @@
             pltpu.SemaphoreType.DMA((4,)),
         ],
         after=after,
+        far_out=4,
     )
 
 
@@ -851,10 +845,8 @@
         join_kernel,
         [shaped(shape, BF16)],
         (ids, local, mine, other),
-        0,
         16,
         in_specs=[SCALARS] + [FAR] * 3,
-        out_specs=[FAR],
         scratch_shapes=[pltpu.SemaphoreType.DMA],
         after=after,
     )[0]
@@ -872,10 +864,8 @@
         functools.partial(others_kernel, first),
         [shaped((last - first, rows, gathered.shape[2]), BF16)],
         (ids, gathered),
-        0,
         16,
         in_specs=[SCALARS, FAR],
-        out_specs=[FAR],
         scratch_shapes=[pltpu.SemaphoreType.DMA],
         after=after,
     )[0]
@@ -910,8 +900,7 @@
         functools.partial(attn_grad_kernel, cut),
         dealt(4, normed.shape[1] // 8, columns, cut),
         (ids, normed, grad, attended, flow),
-        0,
-        40,
+        20,
         in_specs=[SCALARS] + [WHOLE] * 4,
         after=after,
     )
@@ -949,8 +938,7 @@
             shaped((blocks // 2, half, columns - QKV), BF16),
         ],
         (pair, *parts),
-        0,
-        32,
+        16,
         in_specs=[SCALARS] + [WHOLE] * 4,
         after=after,
     )
@@ -975,8 +963,7 @@
         attn_join_kernel,
         [shaped(mine.shape, BF16)],
         (pair, mine, other),
-        0,
-        32,
+        12,
         in_specs=[SCALARS, WHOLE, WHOLE],
         after=after,
     )[0]
@@ -1038,8 +1025,7 @@
         functools.partial(place_kernel, kernel, held is None, len(parts), len(outs)),
         [*outs, shaped((8, 128), F32)],
         ins,
-        0,
-        60,
+        48,
         in_specs=specs,
         out_specs=[layer_block(out) for out in outs]
         + [pl.BlockSpec((8, 128), lambda _: (0, 0))],
@@ -1342,7 +1328,7 @@
         part, down_sum = add_two(*down_parts, done, part)
         done = (down_sum,)
         flow, flow_low, gain_grads[layer_count + layer] = norm_back(
-            flow, (part, flip(part, PAIR)), residual_mid, gain_mlp, after=done
+            flow, (part, flip(part, PAIR)), residual_mid, gain_mlp, after=done, pinned=True
         )
         attended_grad = dot_nt(out_w, flow_low).astype(BF16)
         query_grad, own_grad, shared_grad = attend_back(

time: 789 us -> 749 us (0.949)
  local copies, waits for them, and re-layouts: 162 us -> 131 us
  Pallas kernels: 256 us -> 243 us
    unnamed x394 -> x386, local copies, waits for them, and re-layouts: 116 us -> 87.7 us
    pallas_call x56, Pallas kernels: 256 us -> 243 us  [call(): pl.pallas_call(body, out_shape=outs, in_specs=(in_specs or [WHOLE] * coun...]
  transfers between devices with their start and end apart: 102 -> 102, of which waited for: 42 -> 43; matrix products, arithmetic and copies ran while one was open for 10% -> 10% of each run, Pallas kernels for 28% -> 28%
where the time goes in v3:
time: 749 us; the launch traced here: 744 us
  Pallas kernels  243 us (32%)
  waiting for transfers between devices  234 us (31%)
  local copies, waits for them, and re-layouts  131 us (17%)
  starting transfers between devices  80.2 us (11%)
  other arithmetic  20.3 us (3%)
  matrix products  18.3 us (2%)
  between operations  16.8 us (2%)
    pallas_call x56, Pallas kernels, call(): pl.pallas_call(body, out_shape=outs, in_specs=(in_specs or [WHOLE] * coun...  243 us
    ppermute x92, waiting for transfers between devices, flip(): return lax.ppermute(value, axis, [(i, i ^ bit) for i in range(count)])  186 us
    unnamed x386, local copies, waits for them, and re-layouts  87.7 us
    ppermute x92, starting transfers between devices, flip(): return lax.ppermute(value, axis, [(i, i ^ bit) for i in range(count)])  78.7 us
    all_gather x2, waiting for transfers between devices, attn_gather(): return (local, lax.all_gather(piece, 'wt', axis=0, tiled=False))  42.6 us
  transfers between devices with their start and end apart: 102, of which 43 were waited for; matrix products, arithmetic and copies ran while one was open for 10% of the time, Pallas kernels for 28%

profile of v3, /device:TPU:0, one launch (start us, length us, event | category | flops | bytes accessed | tf_op | source)
XLA Modules:
  0.0 743.9 jit_solution(17417719343474655085)
XLA Ops:
  36.9 29.3 %all-gather.9.cloned.1.call-done = bf16[640,1536]{1,0:T(8,128)(2,1)} async-done(((bf16[160,1536]{1,0:T(8,128)(2,1)}), bf16[640,1536]{1,0:T(8,128)(2,1)}) %all-gather.9.cloned.1.call-update) | async-done | bytes 1966096 | tf_op jit(solution)/shard_map/all_gather | solution.py:1149
  76.5 25.0 %collective-permute-done.1.refs_3_ = bf16[3,144,1536]{2,1,0:T(8,128)(2,1)} collective-permute-done((bf16[3,144,1536]{2,1,0:T(8,128)(2,1)}, bf16[3,144,1536]{2,1,0:T(8,128)(2,1)}, u32[]{:S(2)}, u32[]{:S(2)}) %collective-permute-start.1) | collective-permute-done | bytes 1327136 | tf_op jit(solution)/shard_map/ppermute | solution.py:1083
  117.3 5.3 all-gather.11.cloned.1.call-done
  137.3 11.8 %shard_map.219 = (bf16[576,640]{1,0:T(8,128)(2,1)S(1)}, f32[9,1,640]{2,1,0:T(1,128)S(1)}) custom-call(bf16[576,640]{1,0:T(8,128)(2,1)S(1)} %copy-done.73, bf16[640,384]{1,0:T(8,128)(2,1)S(1)} %copy-done.88, bf16[384,640]{1,0:T(8,128)(2,1)S(1)} %copy-done.101, bf16[512,384]{1,0:T(8,128)(2,1)S(1)} %pad_maximum_fusion.7.refs_2_.refs_3_.refs_4_, ...), custom_call_target="tpu_custom_call" | custom-call | flops 1 | bytes 1 | tf_op jit(solution)/shard_map/pallas_call | solution.py:80
  150.6 13.3 %all-gather.13.cloned.1.call-done = bf16[576,1536]{1,0:T(8,128)(2,1)} async-done(((bf16[144,1536]{1,0:T(8,128)(2,1)}), bf16[576,1536]{1,0:T(8,128)(2,1)}) %all-gather.13.cloned.1.call-update) | async-done | bytes 1769488 | tf_op jit(solution)/shard_map/all_gather | solution.py:1149
  179.9 6.1 collective-permute-done.12.refs_9_
  196.3 11.0 %collective-permute-done.13.refs_10_ = bf16[144,1152]{1,0:T(8,128)(2,1)} collective-permute-done((bf16[144,1152]{1,0:T(8,128)(2,1)}, bf16[144,1152]{1,0:T(8,128)(2,1)}, u32[]{:S(2)}, u32[]{:S(2)}) %collective-permute-start.13) | collective-permute-done | bytes 331808 | tf_op jit(solution)/shard_map/ppermute | solution.py:1083
  207.4 6.5 collective-permute-done.11.refs_8_
  213.9 13.3 %shard_map.222 = (bf16[4,1152,768]{2,1,0:T(8,128)(2,1)}, bf16[1536,1152]{1,0:T(8,128)(2,1)S(1)}, bf16[640,1536]{1,0:T(8,128)(2,1)S(1)}, bf16[640,1536]{1,0:T(8,1...) custom-call(s32[5]{0:T(128)S(1)} %stack.28.refs_0_, ...), custom_call_target="tpu_custom_call" | custom-call | flops 1 | bytes 1 | tf_op jit(solution)/shard_map/pallas_call | solution.py:80
  259.0 9.6 %collective-permute-done.16.refs_3_ = bf16[2,288,1152]{2,1,0:T(8,128)(2,1)} collective-permute-done((bf16[2,288,1152]{2,1,0:T(8,128)(2,1)}, bf16[2,288,1152]{2,1,0:T(8,128)(2,1)}, u32[]{:S(2)}, u32[]{:S(2)}) %collective-permute-start.16) | collective-permute-done | bytes 1327136 | tf_op jit(solution)/shard_map/ppermute | solution.py:1083
  284.8 12.2 %shard_map.229 = (bf16[576,640]{1,0:T(8,128)(2,1)S(1)}, f32[9,1,640]{2,1,0:T(1,128)S(1)}) custom-call(bf16[576,640]{1,0:T(8,128)(2,1)S(1)} %get-tuple-element.129.refs_0_, bf16[640,384]{1,0:T(8,128)(2,1)S(1)} %get-tuple-element.130.refs_1_.refs_2_, bf16[384,640]{1,0:T(8,128)(2,1)S(1)} %get-tuple-element.131.refs_2_.refs_3_, ...), custom_call_target="tpu_custom_call" | custom-call | flops 1 | bytes 1 | tf_op jit(solution)/shard_map/pallas_call | solution.py:80
  304.5 5.8 collective-permute-done.23.refs_6_
  326.5 13.3 %shard_map.231 = (bf16[4,1152,768]{2,1,0:T(8,128)(2,1)}, bf16[1536,1152]{1,0:T(8,128)(2,1)S(1)}, bf16[640,1536]{1,0:T(8,128)(2,1)S(1)}, bf16[640,1536]{1,0:T(8,1...) custom-call(s32[5]{0:T(128)S(1)} %stack.28.refs_0_, ...), custom_call_target="tpu_custom_call" | custom-call | flops 1 | bytes 1 | tf_op jit(solution)/shard_map/pallas_call | solution.py:80
  348.0 20.2 %shard_map.233 = (bf16[1152,768]{1,0:T(8,128)(2,1)}, bf16[1152,768]{1,0:T(8,128)(2,1)}, bf16[1152,768]{1,0:T(8,128)(2,1)}, bf16[1152,768]{1,0:T(8,128)(2,1)}, bf16[640,1152]{1,0:T(8,128)(2,1)S(1)}) custom-call(bf16[640,1152]{1,0:T(8,128)(2,1)S(1)} %copy-done.15, bf16[640,1152]{1,0:T(8,128)(2,1)S(1)} %get-tuple-element.134.refs_1_, ...), custom_call_target="tpu_custom_call" | custom-call | flops 1 | bytes 1 | tf_op jit(solution)/shard_map/pallas_call | solution.py:80
  382.0 5.9 shard_map.235
  391.7 19.6 %shard_map.236 = (bf16[576,640]{1,0:T(8,128)(2,1)S(1)}, f32[512,384]{1,0:T(8,128)S(1)}, f32[512,384]{1,0:T(8,128)S(1)}) custom-call(bf16[576,640]{1,0:T(8,128)(2,1)S(1)} %copy-done.76, bf16[576,640]{1,0:T(8,128)(2,1)S(1)} %convolution_convert_fusion.5.refs_1_, bf16[640,384]{1,0:T(8,128)(2,1)S(1)} %copy-done.91, bf16[384,640]{1,0:T(8,128)(2,1)S(1)} %copy-done.104, ...), custom_call_target="tpu_custom_call" | custom-call | flops 1 | bytes 1 | tf_op jit(solution)/shard_map/pallas_call | solution.py:80
  414.6 6.8 collective-permute-done.33
  424.2 5.4 shard_map.237.refs_3_.refs_5_
  448.8 5.3 shard_map.241
  456.3 16.2 %collective-permute-done.42.refs_2_ = bf16[4,144,768]{2,1,0:T(8,128)(2,1)S(1)} collective-permute-done((bf16[4,144,768]{2,1,0:T(8,128)(2,1)S(1)}, bf16[4,144,768]{2,1,0:T(8,128)(2,1)S(1)}, u32[]{:S(2)}, u32[]{:S(2)}) %collective-permute-start.42) | collective-permute-done | bytes 884768 | tf_op jit(solution)/shard_map/ppermute | solution.py:1083
  488.6 5.1 shard_map.244
  496.8 22.0 %shard_map.246 = (bf16[1152,768]{1,0:T(8,128)(2,1)}, bf16[1152,768]{1,0:T(8,128)(2,1)}, bf16[1152,768]{1,0:T(8,128)(2,1)}, bf16[1152,768]{1,0:T(8,128)(2,1)}, bf16[640,1152]{1,0:T(8,128)(2,1)S(1)}) custom-call(bf16[640,1152]{1,0:T(8,128)(2,1)S(1)} %get-tuple-element.167.refs_2_.refs_0_, bf16[640,1152]{1,0:T(8,128)(2,1)S(1)} %copy-done.54, ...), custom_call_target="tpu_custom_call" | custom-call | flops 1 | bytes 1 | tf_op jit(solution)/shard_map/pallas_call | solution.py:80
  535.2 5.7 shard_map.248
  544.6 19.6 %shard_map.249 = (bf16[576,640]{1,0:T(8,128)(2,1)S(1)}, f32[512,384]{1,0:T(8,128)S(1)}, f32[512,384]{1,0:T(8,128)S(1)}) custom-call(bf16[576,640]{1,0:T(8,128)(2,1)S(1)} %copy-done.74, bf16[576,640]{1,0:T(8,128)(2,1)S(1)} %convolution_convert_fusion.4.refs_1_, bf16[640,384]{1,0:T(8,128)(2,1)S(1)} %copy-done.89, bf16[384,640]{1,0:T(8,128)(2,1)S(1)} %copy-done.102, ...), custom_call_target="tpu_custom_call" | custom-call | flops 1 | bytes 1 | tf_op jit(solution)/shard_map/pallas_call | solution.py:80
  567.5 7.1 collective-permute-done.48
  577.6 5.4 shard_map.250.refs_3_.refs_5_
  590.6 11.9 %collective-permute-done.56.refs_1_ = bf16[144,768]{1,0:T(8,128)(2,1)S(1)} collective-permute-done((bf16[144,768]{1,0:T(8,128)(2,1)S(1)}, bf16[144,768]{1,0:T(8,128)(2,1)S(1)}, u32[]{:S(2)}, u32[]{:S(2)}) %collective-permute-start.56) | collective-permute-done | bytes 221216 | tf_op jit(solution)/shard_map/ppermute | solution.py:1083
  612.1 12.0 %collective-permute-done.49 = bf16[128,384]{1,0:T(8,128)(2,1)S(1)} collective-permute-done((bf16[128,384]{1,0:T(8,128)(2,1)S(1)}, bf16[128,384]{1,0:T(8,128)(2,1)S(1)}, u32[]{:S(2)}, u32[]{:S(2)}) %collective-permute-start.49) | collective-permute-done | bytes 98336 | tf_op jit(solution)/shard_map/ppermute | solution.py:1083
  633.1 5.4 shard_map.257
  644.7 11.7 %collective-permute-done.65.refs_2_ = bf16[4,144,768]{2,1,0:T(8,128)(2,1)S(1)} collective-permute-done((bf16[4,144,768]{2,1,0:T(8,128)(2,1)S(1)}, bf16[4,144,768]{2,1,0:T(8,128)(2,1)S(1)}, u32[]{:S(2)}, u32[]{:S(2)}) %collective-permute-start.65) | collective-permute-done | bytes 884768 | tf_op jit(solution)/shard_map/ppermute | solution.py:1083
  692.7 6.2 shard_map.261
  716.2 6.2 shard_map.264
  (735 shorter events, 366.9 us)
Async XLA Ops:
  7.2 59.0 %all-gather.9.cloned.1.call-start = ((), (), s32[]{:S(2)}) async-start(), calls=%async_computation.12 | async-start | bytes 2457600 | tf_op jit(solution)/shard_map/all_gather | solution.py:1149
  19.8 102.8 %all-gather.11.cloned.1.call-start = ((), (), s32[]{:S(2)}) async-start(), calls=%async_computation.13 | async-start | bytes 3317760 | tf_op jit(solution)/shard_map/all_gather | solution.py:1160
  25.5 138.3 %all-gather.13.cloned.1.call-start = ((), (), s32[]{:S(2)}) async-start(), calls=%async_computation.14 | async-start | bytes 2211840 | tf_op jit(solution)/shard_map/all_gather | solution.py:1149
  29.7 203.7 %all-gather.15.cloned.1.call-start = ((), (), s32[]{:S(2)}) async-start(), calls=%async_computation.15 | async-start | bytes 3317760 | tf_op jit(solution)/shard_map/all_gather | solution.py:1160
  29.7 42.5 %collective-permute-start = (bf16[320,1152]{1,0:T(8,128)(2,1)}, bf16[320,1152]{1,0:T(8,128)(2,1)}, u32[]{:S(2)}, u32[]{:S(2)}) collective-permute-start(bf16[320,1152]{1,0:T(8,128)(2,1)} %bitcast.91), channel_id=1, source_target_pairs={{0,4},{4,0},{8,12},{12,8},{16,20},{20,16},{24,28},{28,24},{1,5},{5... | collective-permute-start | bytes 2211848 | tf_op jit(solution)/shard_map/ppermute | solution.py:1083
  36.0 386.2 %reduce-scatter.7.cloned.1.call-start = ((), (), s32[]{:S(2)}) async-start(), calls=%async_computation.6 | async-start | bytes 2211840 | tf_op jit(solution)/shard_map/reduce_scatter | solution.py:1286
  70.3 31.2 %collective-permute-start.1 = (bf16[3,144,1536]{2,1,0:T(8,128)(2,1)}, bf16[3,144,1536]{2,1,0:T(8,128)(2,1)}, u32[]{:S(2)}, u32[]{:S(2)}) collective-permute-start(bf16[3,144,1536]{2,1,0:T(8,128)(2,1)} %shard_map.212), channel_id=1, source_target_pairs={{0,16},{4,20},{8,24},{12,28},{16,0},{20,4},{24,8},{28,12},{1,17},{... | collective-permute-start | bytes 3981320 | tf_op jit(solution)/shard_map/ppermute | solution.py:1083
  109.6 59.2 %collective-permute-start.4 = (bf16[576,576]{1,0:T(8,128)(2,1)}, bf16[576,576]{1,0:T(8,128)(2,1)}, u32[]{:S(2)}, u32[]{:S(2)}) collective-permute-start(bf16[576,576]{1,0:T(8,128)(2,1)} %constant_dynamic-slice_fusion.8), channel_id=1, source_target_pairs={{0,4},{4,0},{8,12},{12,8},{16,20},{20,16},{24,28},{28,24},{1,5},{5... | collective-permute-start | bytes 1990664 | tf_op jit(solution)/shard_map/ppermute | solution.py:1083
  126.4 48.9 %collective-permute-start.6 = (bf16[2,288,1152]{2,1,0:T(8,128)(2,1)}, bf16[2,288,1152]{2,1,0:T(8,128)(2,1)}, u32[]{:S(2)}, u32[]{:S(2)}) collective-permute-start(bf16[2,288,1152]{2,1,0:T(8,128)(2,1)} %shard_map.217.refs_6_), channel_id=1, source_target_pairs={{0,16},{4,20},{8,24},{12,28},{16,0},{20,4},{24,8},{28,12},{1,17},{... | collective-permute-start | bytes 3981320 | tf_op jit(solution)/shard_map/ppermute | solution.py:1083
  129.6 44.4 %collective-permute-start.7 = (bf16[1,288,1152]{2,1,0:T(8,128)(2,1)}, bf16[1,288,1152]{2,1,0:T(8,128)(2,1)}, u32[]{:S(2)}, u32[]{:S(2)}) collective-permute-start(bf16[1,288,1152]{2,1,0:T(8,128)(2,1)} %shard_map.218.refs_7_), channel_id=1, source_target_pairs={{0,16},{4,20},{8,24},{12,28},{16,0},{20,4},{24,8},{28,12},{1,17},{... | collective-permute-start | bytes 1990664 | tf_op jit(solution)/shard_map/ppermute | solution.py:1083
  131.2 48.1 %collective-permute-start.9 = (bf16[1,288,1152]{2,1,0:T(8,128)(2,1)}, bf16[1,288,1152]{2,1,0:T(8,128)(2,1)}, u32[]{:S(2)}, u32[]{:S(2)}) collective-permute-start(bf16[1,288,1152]{2,1,0:T(8,128)(2,1)} %shard_map.218.refs_7_), channel_id=1, source_target_pairs={{0,8},{4,12},{8,0},{12,4},{16,24},{20,28},{24,16},{28,20},{1,9},{5... | collective-permute-start | bytes 1990664 | tf_op jit(solution)/shard_map/ppermute | solution.py:1083
  132.6 74.7 %collective-permute-start.8 = (bf16[2,288,1152]{2,1,0:T(8,128)(2,1)}, bf16[2,288,1152]{2,1,0:T(8,128)(2,1)}, u32[]{:S(2)}, u32[]{:S(2)}) collective-permute-start(bf16[2,288,1152]{2,1,0:T(8,128)(2,1)} %shard_map.217.refs_6_), channel_id=1, source_target_pairs={{0,8},{4,12},{8,0},{12,4},{16,24},{20,28},{24,16},{28,20},{1,9},{5... | collective-permute-start | bytes 3981320 | tf_op jit(solution)/shard_map/ppermute | solution.py:1083
  168.8 38.6 %collective-permute-start.14 = (bf16[3,144,1536]{2,1,0:T(8,128)(2,1)}, bf16[3,144,1536]{2,1,0:T(8,128)(2,1)}, u32[]{:S(2)}, u32[]{:S(2)}) collective-permute-start(bf16[3,144,1536]{2,1,0:T(8,128)(2,1)} %shard_map.221), channel_id=1, source_target_pairs={{0,16},{4,20},{8,24},{12,28},{16,0},{20,4},{24,8},{28,12},{1,17},{... | collective-permute-start | bytes 3981320 | tf_op jit(solution)/shard_map/ppermute | solution.py:1083
  179.3 28.1 %collective-permute-start.10 = (bf16[288,1152]{1,0:T(8,128)(2,1)}, bf16[288,1152]{1,0:T(8,128)(2,1)}, u32[]{:S(2)}, u32[]{:S(2)}) collective-permute-start(bf16[288,1152]{1,0:T(8,128)(2,1)} %get-tuple-element.246), channel_id=1, source_target_pairs={{0,8},{4,12},{8,0},{12,4},{16,24},{20,28},{24,16},{28,20},{1,9},{5... | collective-permute-start | bytes 1990664 | tf_op jit(solution)/shard_map/ppermute | solution.py:1083
  186.0 27.9 %collective-permute-start.11 = (bf16[288,1152]{1,0:T(8,128)(2,1)}, bf16[288,1152]{1,0:T(8,128)(2,1)}, u32[]{:S(2)}, u32[]{:S(2)}) collective-permute-start(bf16[288,1152]{1,0:T(8,128)(2,1)} %get-tuple-element.245), channel_id=1, source_target_pairs={{0,8},{4,12},{8,0},{12,4},{16,24},{20,28},{24,16},{28,20},{1,9},{5... | collective-permute-start | bytes 1990664 | tf_op jit(solution)/shard_map/ppermute | solution.py:1083
  237.2 31.4 %collective-permute-start.16 = (bf16[2,288,1152]{2,1,0:T(8,128)(2,1)}, bf16[2,288,1152]{2,1,0:T(8,128)(2,1)}, u32[]{:S(2)}, u32[]{:S(2)}) collective-permute-start(bf16[2,288,1152]{2,1,0:T(8,128)(2,1)} %shard_map.226.refs_6_), channel_id=1, source_target_pairs={{0,16},{4,20},{8,24},{12,28},{16,0},{20,4},{24,8},{28,12},{1,17},{... | collective-permute-start | bytes 3981320 | tf_op jit(solution)/shard_map/ppermute | solution.py:1083
  237.7 31.1 %collective-permute-start.17 = (bf16[2,288,1152]{2,1,0:T(8,128)(2,1)}, bf16[2,288,1152]{2,1,0:T(8,128)(2,1)}, u32[]{:S(2)}, u32[]{:S(2)}) collective-permute-start(bf16[2,288,1152]{2,1,0:T(8,128)(2,1)} %shard_map.226.refs_6_), channel_id=1, source_target_pairs={{0,8},{4,12},{8,0},{12,4},{16,24},{20,28},{24,16},{28,20},{1,9},{5... | collective-permute-start | bytes 3981320 | tf_op jit(solution)/shard_map/ppermute | solution.py:1083
  244.8 26.1 %collective-permute-start.20 = (bf16[576,576]{1,0:T(8,128)(2,1)}, bf16[576,576]{1,0:T(8,128)(2,1)}, u32[]{:S(2)}, u32[]{:S(2)}) collective-permute-start(bf16[576,576]{1,0:T(8,128)(2,1)} %constant_dynamic-slice_fusion.7), channel_id=1, source_target_pairs={{0,4},{4,0},{8,12},{12,8},{16,20},{20,16},{24,28},{28,24},{1,5},{5... | collective-permute-start | bytes 1990664 | tf_op jit(solution)/shard_map/ppermute | solution.py:1083
  280.1 42.5 %collective-permute-start.24 = (bf16[288,1152]{1,0:T(8,128)(2,1)}, bf16[288,1152]{1,0:T(8,128)(2,1)}, u32[]{:S(2)}, u32[]{:S(2)}) collective-permute-start(bf16[288,1152]{1,0:T(8,128)(2,1)} %slice_bitcast_fusion.1), channel_id=1, source_target_pairs={{0,8},{4,12},{8,0},{12,4},{16,24},{20,28},{24,16},{28,20},{1,9},{5... | collective-permute-start | bytes 1990664 | tf_op jit(solution)/shard_map/ppermute | solution.py:1083
  284.2 26.2 %collective-permute-start.23 = (bf16[1,288,1152]{2,1,0:T(8,128)(2,1)S(1)}, bf16[1,288,1152]{2,1,0:T(8,128)(2,1)S(1)}, u32[]{:S(2)}, u32[]{:S(2)}) collective-permute-start(bf16[1,288,1152]{2,1,0:T(8,128)(2,1)S(1)} %shard_map.228.refs_7_), channel_id=1, source_target_pairs={{0,8},{4,12},{8,0},{12,4},{16,24},{20,28},{24,16},{28,20},{1,9},{5... | collective-permute-start | bytes 1990664 | tf_op jit(solution)/shard_map/ppermute | solution.py:1083
  375.8 145.1 %reduce-scatter.9.cloned.1.call-start = ((), (), s32[]{:S(2)}) async-start(), calls=%async_computation.7 | async-start | bytes 4423680 | tf_op jit(solution)/shard_map/reduce_scatter | solution.py:1286
  375.9 46.3 %collective-permute-start.35 = (bf16[1152,768]{1,0:T(8,128)(2,1)}, bf16[1152,768]{1,0:T(8,128)(2,1)}, u32[]{:S(2)}, u32[]{:S(2)}) collective-permute-start(bf16[1152,768]{1,0:T(8,128)(2,1)} %get-tuple-element.155), channel_id=1, source_target_pairs={{0,8},{4,12},{8,0},{12,4},{16,24},{20,28},{24,16},{28,20},{1,9},{5... | collective-permute-start | bytes 5308424 | tf_op jit(solution)/shard_map/ppermute | solution.py:1083
  377.4 44.8 %collective-permute-start.36 = (bf16[1152,768]{1,0:T(8,128)(2,1)}, bf16[1152,768]{1,0:T(8,128)(2,1)}, u32[]{:S(2)}, u32[]{:S(2)}) collective-permute-start(bf16[1152,768]{1,0:T(8,128)(2,1)} %get-tuple-element.157), channel_id=1, source_target_pairs={{0,16},{4,20},{8,24},{12,28},{16,0},{20,4},{24,8},{28,12},{1,17},{... | collective-permute-start | bytes 5308424 | tf_op jit(solution)/shard_map/ppermute | solution.py:1083
  429.6 145.1 %reduce-scatter.13.cloned.1.call-start = ((), (), s32[]{:S(2)}) async-start(), calls=%async_computation.9 | async-start | bytes 2211840 | tf_op jit(solution)/shard_map/reduce_scatter | solution.py:1286
  478.9 96.6 %reduce-scatter.11.cloned.1.call-start = ((), (), s32[]{:S(2)}) async-start(), calls=%async_computation.8 | async-start | bytes 2211840 | tf_op jit(solution)/shard_map/reduce_scatter | solution.py:1286
  493.8 27.1 %collective-permute-start.44 = (bf16[4,192,640]{2,1,0:T(8,128)(2,1)S(1)}, bf16[4,192,640]{2,1,0:T(8,128)(2,1)}, u32[]{:S(2)}, u32[]{:S(2)}) collective-permute-start(bf16[4,192,640]{2,1,0:T(8,128)(2,1)S(1)} %get-tuple-element.169), channel_id=1, source_target_pairs={{0,16},{4,20},{8,24},{12,28},{16,0},{20,4},{24,8},{28,12},{1,17},{... | collective-permute-start | bytes 2949128 | tf_op jit(solution)/shard_map/ppermute | solution.py:1083
  528.8 150.2 %reduce-scatter.17.cloned.1.call-start = ((), (), s32[]{:S(2)}) async-start(), calls=%async_computation.11 | async-start | bytes 4423680 | tf_op jit(solution)/shard_map/reduce_scatter | solution.py:1286
  529.1 45.5 %collective-permute-start.50 = (bf16[1152,768]{1,0:T(8,128)(2,1)}, bf16[1152,768]{1,0:T(8,128)(2,1)}, u32[]{:S(2)}, u32[]{:S(2)}) collective-permute-start(bf16[1152,768]{1,0:T(8,128)(2,1)} %get-tuple-element.187), channel_id=1, source_target_pairs={{0,8},{4,12},{8,0},{12,4},{16,24},{20,28},{24,16},{28,20},{1,9},{5... | collective-permute-start | bytes 5308424 | tf_op jit(solution)/shard_map/ppermute | solution.py:1083
  530.7 44.0 %collective-permute-start.51 = (bf16[1152,768]{1,0:T(8,128)(2,1)}, bf16[1152,768]{1,0:T(8,128)(2,1)}, u32[]{:S(2)}, u32[]{:S(2)}) collective-permute-start(bf16[1152,768]{1,0:T(8,128)(2,1)} %get-tuple-element.189), channel_id=1, source_target_pairs={{0,16},{4,20},{8,24},{12,28},{16,0},{20,4},{24,8},{28,12},{1,17},{... | collective-permute-start | bytes 5308424 | tf_op jit(solution)/shard_map/ppermute | solution.py:1083
  583.0 128.4 %reduce-scatter.15.cloned.1.call-start = ((), (), s32[]{:S(2)}) async-start(), calls=%async_computation.10 | async-start | bytes 2211840 | tf_op jit(solution)/shard_map/reduce_scatter | solution.py:1286
  604.9 27.8 %collective-permute-start.61 = (bf16[288,768]{1,0:T(8,128)(2,1)S(1)}, bf16[288,768]{1,0:T(8,128)(2,1)S(1)}, u32[]{:S(2)}, u32[]{:S(2)}) collective-permute-start(bf16[288,768]{1,0:T(8,128)(2,1)S(1)} %get-tuple-element.191.refs_7_.refs_1_), channel_id=1, source_target_pairs={{0,8},{4,12},{8,0},{12,4},{16,24},{20,28},{24,16},{28,20},{1,9},{5... | collective-permute-start | bytes 1327112 | tf_op jit(solution)/shard_map/ppermute | solution.py:1083
  606.1 26.7 %collective-permute-start.62 = (bf16[288,768]{1,0:T(8,128)(2,1)S(1)}, bf16[288,768]{1,0:T(8,128)(2,1)S(1)}, u32[]{:S(2)}, u32[]{:S(2)}) collective-permute-start(bf16[288,768]{1,0:T(8,128)(2,1)S(1)} %get-tuple-element.194.refs_5_), channel_id=1, source_target_pairs={{0,16},{4,20},{8,24},{12,28},{16,0},{20,4},{24,8},{28,12},{1,17},{... | collective-permute-start | bytes 1327112 | tf_op jit(solution)/shard_map/ppermute | solution.py:1083
  (263 other events, 2367.2 us)
Sparse Core Ops, SparseCore 0:
  19.9 46.2 all-gather.8
  68.3 54.1 all-gather.10
  124.7 39.0 all-gather.12
  165.8 54.2 all-gather.14
  375.9 36.2 reduce-scatter.6
  429.7 64.2 reduce-scatter.8
  496.4 38.6 reduce-scatter.12
  538.0 37.4 reduce-scatter.10
  583.1 65.4 reduce-scatter.16
  663.6 37.5 reduce-scatter.14

commit v4 on v3

--- a/solution.py
+++ b/solution.py
@@ -361,7 +361,7 @@
                 lse_ref[number, :, cols] = top + jnp.log2(total)
             return carry
 
-        lax.fori_loop(0, SHARED, head, 0)
+        lax.fori_loop(0, SHARED, head, 0, unroll=True)
 
 
 def attend(query, key_value, key_value_turned, shared, key_pos, row_pos, after=()):
@@ -455,7 +455,7 @@
                 )
             return carry
 
-        lax.fori_loop(0, SHARED, head, 0)
+        lax.fori_loop(0, SHARED, head, 0, unroll=True)
         key_sum, value_sum = 0.0, 0.0
         own_key_sum, own_value_sum = [0.0, 0.0], [0.0, 0.0]
         for index in range(SHARED):
@@ -627,7 +627,7 @@
             unit_ref[some, cols] = (scale * up).astype(BF16)
             return carry
 
-        lax.fori_loop(0, 2, tile, 0)
+        lax.fori_loop(0, 2, tile, 0, unroll=True)
     pltpu.make_async_copy(down_ref, down_ref, down_sem).wait()
 
     def finish(index, carry):
@@ -635,12 +635,12 @@
         out_ref[some, :] = dot_nn(unit_ref[some, :], down_ref[...]).astype(BF16)
         return carry
 
-    lax.fori_loop(0, 2, finish, 0)
+    lax.fori_loop(0, 2, finish, 0, unroll=True)
     for part in kept:
         part.wait()
 
 
-def mlp(layer, ids, normed, pieces, weights, block, after=()):
+def mlp(layer, ids, normed, pieces, weights, block, after=(), far_out=0):
     rows, depth = normed.shape
     units = 4 * block
     ins = (ids, normed, *pieces, *weights)
@@ -665,6 +665,7 @@
             pltpu.SemaphoreType.DMA((4,)),
         ],
         after=after,
+        far_out=far_out,
     )
 
 
@@ -782,7 +783,7 @@
             unit_grad[at, block:] = (grad * scale_ref[at, cols].astype(F32)).astype(BF16)
             return carry
 
-        lax.fori_loop(0, 2, tile, 0)
+        lax.fori_loop(0, 2, tile, 0, unroll=True)
         both = dot_tn(normed_ref[...], unit_grad[...]).astype(BF16)
         target = gate_send if part >= 2 else gate_keep
         target[:, (part % 2) * block : (part % 2 + 1) * block] = both[:, :block]
@@ -801,7 +802,7 @@
                 total[at, :] += value
             return carry
 
-        lax.fori_loop(0, 2, gather, 0)
+        lax.fori_loop(0, 2, gather, 0, unroll=True)
 
 
 def mlp_back(flow, normed, slope, scale, down, weights, after=()):
@@ -1221,6 +1222,7 @@
             ff_weights,
             ff_block,
             late,
+            0 if layer + 1 == layer_count else 5,
         )
         parts = (part, flip(part, PAIR))
         if layer + 1 < layer_count:
@@ -1372,14 +1374,34 @@
         row_keep, row_send, side_keep, side_send = attn_grad(
             ids, normed_attn, grad_qkv, attended, flow_low, attn_cut, done
         )
+        if older is None:
+            done = (layer_out,)
+        else:
+            *ff_held, placed = place(
+                place_ff_kernel,
+                layer + 1,
+                where,
+                older["ff"] + older["down"],
+                ff_outs,
+                ff_held,
+                (row_keep,),
+            )
+            *attn_held, attn_placed = place(
+                place_attn_kernel, layer + 1, where, older["attn"], attn_outs, attn_held, (row_keep,)
+            )
+            done = (placed, attn_placed)
         attn_mine, send = attn_sum(
-            pair[None], (row_keep, flip(row_send, ROW), side_keep, flip(side_send, SIDE))
-        )
+            pair[None],
+            (row_keep, flip(row_send, ROW), side_keep, flip(side_send, SIDE)),
+            done,
+        )
+        done = (attn_mine,)
         flow, flow_low, gain_grads[layer] = norm_back(
-            flow, (part, flip(part, PAIR)), residual, gain_attn, after=(attn_mine,)
+            flow, (part, flip(part, PAIR)), residual, gain_attn, after=done
         )
         attn_all = attn_join(pair[None], attn_mine, flip(send, PAIR))
         shares[layer]["attn"] = scatter(attn_all)
+    ff_totals = sum_ff(shares[0]["ff"], (attn_all,))
     gain_total = jnp.concatenate(gain_grads, axis=0)
     for bit in [SIDE, ROW] + outer_bits:
         gain_total = gain_total + flip(gain_total, bit)
@@ -1387,19 +1409,14 @@
     while bit < wt_count:
         gain_total = gain_total + flip(gain_total, bit, "wt", wt_count)
         bit *= 2
-    for layer in reversed(range(layer_count)):
-        share = shares[layer]
-        if layer == 0:
-            share["ff"] = spread_ff(sum_ff(share["ff"], (placed, attn_placed)))
-        *ff_held, placed = place(
-            place_ff_kernel, layer, where, share["ff"] + share["down"], ff_outs, ff_held, (flow_low,)
-        )
-        if layer == 0:
-            totals = sum_rows(share["attn"], attn_cut, (placed, gain_total))
-            share["attn"] = spread_rows(totals)
-        *attn_held, attn_placed = place(
-            place_attn_kernel, layer, where, share["attn"], attn_outs, attn_held, (flow_low,)
-        )
+    ff = spread_ff(ff_totals)
+    *ff_held, placed = place(
+        place_ff_kernel, 0, where, ff + shares[0]["down"], ff_outs, ff_held, (gain_total,)
+    )
+    attn_totals = sum_rows(shares[0]["attn"], attn_cut, (placed,))
+    *attn_held, _ = place(
+        place_attn_kernel, 0, where, spread_rows(attn_totals), attn_outs, attn_held
+    )
     query_out, key_out, value_out, out_out = attn_held
     gate_out, up_out, down_out = ff_held
     token_grad = own_rows(flow)

time: 749 us -> 743 us (level)
  Pallas kernels: 243 us -> 233 us
    pallas_call x56, Pallas kernels: 243 us -> 233 us  [call(): pl.pallas_call(body, out_shape=outs, in_specs=(in_specs or [WHOLE] * coun...]
    unnamed x386 -> x356, local copies, waits for them, and re-layouts: 87.7 us -> 86 us
  transfers between devices with their start and end apart: 102 -> 102, of which waited for: 43 -> 44; matrix products, arithmetic and copies ran while one was open for 10% -> 11% of each run, Pallas kernels for 28% -> 27%
where the time goes in v4:
time: 743 us; the launch traced here: 734 us
  Pallas kernels  233 us (31%)
  waiting for transfers between devices  232 us (31%)
  local copies, waits for them, and re-layouts  134 us (18%)
  starting transfers between devices  74.2 us (10%)
  other arithmetic  25.6 us (3%)
  matrix products  19.2 us (3%)
  between operations  16.5 us (2%)
    pallas_call x56, Pallas kernels, call(): pl.pallas_call(body, out_shape=outs, in_specs=(in_specs or [WHOLE] * coun...  233 us
    ppermute x92, waiting for transfers between devices, flip(): return lax.ppermute(value, axis, [(i, i ^ bit) for i in range(count)])  190 us
    unnamed x356, local copies, waits for them, and re-layouts  86 us
    ppermute x92, starting transfers between devices, flip(): return lax.ppermute(value, axis, [(i, i ^ bit) for i in range(count)])  73.8 us
    all_gather x2, waiting for transfers between devices, attn_gather(): return (local, lax.all_gather(piece, 'wt', axis=0, tiled=False))  37.2 us
  transfers between devices with their start and end apart: 102, of which 44 were waited for; matrix products, arithmetic and copies ran while one was open for 11% of the time, Pallas kernels for 27%

profile of v4, /device:TPU:0, one launch (start us, length us, event | category | flops | bytes accessed | tf_op | source)
XLA Modules:
  0.0 734.1 jit_solution(1375154710709739833)
XLA Ops:
  42.2 24.0 %all-gather.9.cloned.1.call-done = bf16[640,1536]{1,0:T(8,128)(2,1)} async-done(((bf16[160,1536]{1,0:T(8,128)(2,1)}), bf16[640,1536]{1,0:T(8,128)(2,1)}) %all-gather.9.cloned.1.call-update) | async-done | bytes 1966096 | tf_op jit(solution)/shard_map/all_gather | solution.py:1150
  84.0 17.3 %collective-permute-done.1.refs_3_ = bf16[3,144,1536]{2,1,0:T(8,128)(2,1)} collective-permute-done((bf16[3,144,1536]{2,1,0:T(8,128)(2,1)}, bf16[3,144,1536]{2,1,0:T(8,128)(2,1)}, u32[]{:S(2)}, u32[]{:S(2)}) %collective-permute-start.1) | collective-permute-done | bytes 1327136 | tf_op jit(solution)/shard_map/ppermute | solution.py:1084
  140.8 8.3 %shard_map.219 = (bf16[576,640]{1,0:T(8,128)(2,1)S(1)}, f32[9,1,640]{2,1,0:T(1,128)S(1)}) custom-call(bf16[576,640]{1,0:T(8,128)(2,1)S(1)} %copy-done.57, bf16[640,384]{1,0:T(8,128)(2,1)S(1)} %copy-done.72, bf16[384,640]{1,0:T(8,128)(2,1)S(1)} %copy-done.82, bf16[512,384]{1,0:T(8,128)(2,1)S(1)} %copy-done.22, s32[512,1]{1,0:T(8,128)S(1)} %copy-done.33, ...), custom_call_target="tpu_custom_call" | custom-call | flops 1 | bytes 1 | tf_op jit(solution)/shard_map/pallas_call | solution.py:80
  150.7 13.2 %all-gather.13.cloned.1.call-done = bf16[576,1536]{1,0:T(8,128)(2,1)} async-done(((bf16[144,1536]{1,0:T(8,128)(2,1)}), bf16[576,1536]{1,0:T(8,128)(2,1)}) %all-gather.13.cloned.1.call-update) | async-done | bytes 1769488 | tf_op jit(solution)/shard_map/all_gather | solution.py:1150
  179.8 6.1 collective-permute-done.12.refs_9_
  200.9 7.5 %collective-permute-done.13.refs_10_ = bf16[144,1152]{1,0:T(8,128)(2,1)} collective-permute-done((bf16[144,1152]{1,0:T(8,128)(2,1)}, bf16[144,1152]{1,0:T(8,128)(2,1)}, u32[]{:S(2)}, u32[]{:S(2)}) %collective-permute-start.13) | collective-permute-done | bytes 331808 | tf_op jit(solution)/shard_map/ppermute | solution.py:1084
  208.4 5.7 collective-permute-done.11.refs_8_
  215.8 15.7 %shard_map.222 = (bf16[4,1152,768]{2,1,0:T(8,128)(2,1)}, bf16[1536,1152]{1,0:T(8,128)(2,1)}, bf16[640,1536]{1,0:T(8,128)(2,1)}, bf16[640,1536]{1,0:T(8,128)(2,1)...) custom-call(s32[5]{0:T(128)S(1)} %stack.28.refs_0_, bf16[640,1152]{1,0:T(8,128)(2,1)S(1)} %get-tuple-element.124.refs_1_, ...), custom_call_target="tpu_custom_call" | custom-call | flops 1 | bytes 1 | tf_op jit(solution)/shard_map/pallas_call | solution.py:80
  256.7 10.7 %collective-permute-done.16.refs_3_ = bf16[2,288,1152]{2,1,0:T(8,128)(2,1)} collective-permute-done((bf16[2,288,1152]{2,1,0:T(8,128)(2,1)}, bf16[2,288,1152]{2,1,0:T(8,128)(2,1)}, u32[]{:S(2)}, u32[]{:S(2)}) %collective-permute-start.16) | collective-permute-done | bytes 1327136 | tf_op jit(solution)/shard_map/ppermute | solution.py:1084
  283.8 8.3 %shard_map.229 = (bf16[576,640]{1,0:T(8,128)(2,1)S(1)}, f32[9,1,640]{2,1,0:T(1,128)S(1)}) custom-call(bf16[576,640]{1,0:T(8,128)(2,1)S(1)} %get-tuple-element.128.refs_0_, bf16[640,384]{1,0:T(8,128)(2,1)S(1)} %get-tuple-element.129.refs_1_.refs_2_, bf16[384,640]{1,0:T(8,128)(2,1)S(1)} %get-tuple-element.130.refs_2_.refs_3_, ...), custom_call_target="tpu_custom_call" | custom-call | flops 1 | bytes 1 | tf_op jit(solution)/shard_map/pallas_call | solution.py:80
  300.8 10.7 %collective-permute-done.23.refs_6_ = bf16[1,288,1152]{2,1,0:T(8,128)(2,1)S(1)} collective-permute-done((bf16[1,288,1152]{2,1,0:T(8,128)(2,1)S(1)}, bf16[1,288,1152]{2,1,0:T(8,128)(2,1)S(1)}, u32[]{:S(2)}, u32[]{:S(2)}) %collective-permute-start.23) | collective-permute-done | bytes 663584 | tf_op jit(solution)/shard_map/ppermute | solution.py:1084
  322.8 12.6 %shard_map.231 = (bf16[4,1152,768]{2,1,0:T(8,128)(2,1)}, bf16[1536,1152]{1,0:T(8,128)(2,1)S(1)}, bf16[640,1536]{1,0:T(8,128)(2,1)S(1)}, bf16[640,1536]{1,0:T(8,1...) custom-call(s32[5]{0:T(128)S(1)} %stack.28.refs_0_, ...), custom_call_target="tpu_custom_call" | custom-call | flops 1 | bytes 1 | tf_op jit(solution)/shard_map/pallas_call | solution.py:80
  336.7 5.4 shard_map.232
  345.9 19.2 %shard_map.233 = (bf16[1152,768]{1,0:T(8,128)(2,1)}, bf16[1152,768]{1,0:T(8,128)(2,1)}, bf16[1152,768]{1,0:T(8,128)(2,1)}, bf16[1152,768]{1,0:T(8,128)(2,1)}, bf16[640,1152]{1,0:T(8,128)(2,1)S(1)}) custom-call(bf16[640,1152]{1,0:T(8,128)(2,1)S(1)} %copy-done.13, bf16[640,1152]{1,0:T(8,128)(2,1)S(1)} %get-tuple-element.133.refs_1_, ...), custom_call_target="tpu_custom_call" | custom-call | flops 1 | bytes 1 | tf_op jit(solution)/shard_map/pallas_call | solution.py:80
  375.0 5.7 shard_map.235
  384.4 17.3 %shard_map.236 = (bf16[576,640]{1,0:T(8,128)(2,1)S(1)}, f32[512,384]{1,0:T(8,128)S(1)}, f32[512,384]{1,0:T(8,128)S(1)}) custom-call(bf16[576,640]{1,0:T(8,128)(2,1)S(1)} %copy-done.60, bf16[576,640]{1,0:T(8,128)(2,1)S(1)} %convolution_convert_fusion.5.refs_1_, bf16[640,384]{1,0:T(8,128)(2,1)S(1)} %copy-done.75, bf16[384,640]{1,0:T(8,128)(2,1)S(1)} %copy-done.85, ...), custom_call_target="tpu_custom_call" | custom-call | flops 1 | bytes 1 | tf_op jit(solution)/shard_map/pallas_call | solution.py:80
  404.5 11.7 %collective-permute-done.33 = bf16[256,384]{1,0:T(8,128)(2,1)S(1)} collective-permute-done((bf16[256,384]{1,0:T(8,128)(2,1)S(1)}, bf16[256,384]{1,0:T(8,128)(2,1)S(1)}, u32[]{:S(2)}, u32[]{:S(2)}) %collective-permute-start.33) | collective-permute-done | bytes 196640 | tf_op jit(solution)/shard_map/ppermute | solution.py:1084
  417.3 5.4 shard_map.237.refs_3_.refs_5_
  446.5 5.3 shard_map.241
  457.1 12.8 %collective-permute-done.42.refs_2_ = bf16[4,144,768]{2,1,0:T(8,128)(2,1)S(1)} collective-permute-done((bf16[4,144,768]{2,1,0:T(8,128)(2,1)S(1)}, bf16[4,144,768]{2,1,0:T(8,128)(2,1)S(1)}, u32[]{:S(2)}, u32[]{:S(2)}) %collective-permute-start.42) | collective-permute-done | bytes 884768 | tf_op jit(solution)/shard_map/ppermute | solution.py:1084
  493.0 21.5 %shard_map.246 = (bf16[1152,768]{1,0:T(8,128)(2,1)}, bf16[1152,768]{1,0:T(8,128)(2,1)}, bf16[1152,768]{1,0:T(8,128)(2,1)}, bf16[1152,768]{1,0:T(8,128)(2,1)}, bf16[640,1152]{1,0:T(8,128)(2,1)S(1)}) custom-call(bf16[640,1152]{1,0:T(8,128)(2,1)S(1)} %get-tuple-element.166.refs_2_.refs_0_, bf16[640,1152]{1,0:T(8,128)(2,1)S(1)} %copy-done.36, ...), custom_call_target="tpu_custom_call" | custom-call | flops 1 | bytes 1 | tf_op jit(solution)/shard_map/pallas_call | solution.py:80
  527.8 5.7 shard_map.248
  537.4 17.0 %shard_map.249 = (bf16[576,640]{1,0:T(8,128)(2,1)S(1)}, f32[512,384]{1,0:T(8,128)S(1)}, f32[512,384]{1,0:T(8,128)S(1)}) custom-call(bf16[576,640]{1,0:T(8,128)(2,1)S(1)} %copy-done.58, bf16[576,640]{1,0:T(8,128)(2,1)S(1)} %convolution_convert_fusion.4.refs_1_, bf16[640,384]{1,0:T(8,128)(2,1)S(1)} %copy-done.73, bf16[384,640]{1,0:T(8,128)(2,1)S(1)} %copy-done.83, ...), custom_call_target="tpu_custom_call" | custom-call | flops 1 | bytes 1 | tf_op jit(solution)/shard_map/pallas_call | solution.py:80
  556.6 12.3 %collective-permute-done.48 = bf16[256,384]{1,0:T(8,128)(2,1)S(1)} collective-permute-done((bf16[256,384]{1,0:T(8,128)(2,1)S(1)}, bf16[256,384]{1,0:T(8,128)(2,1)S(1)}, u32[]{:S(2)}, u32[]{:S(2)}) %collective-permute-start.48) | collective-permute-done | bytes 196640 | tf_op jit(solution)/shard_map/ppermute | solution.py:1084
  571.2 5.4 shard_map.250.refs_3_.refs_5_
  582.1 13.5 %collective-permute-done.56.refs_1_ = bf16[144,768]{1,0:T(8,128)(2,1)S(1)} collective-permute-done((bf16[144,768]{1,0:T(8,128)(2,1)S(1)}, bf16[144,768]{1,0:T(8,128)(2,1)S(1)}, u32[]{:S(2)}, u32[]{:S(2)}) %collective-permute-start.56) | collective-permute-done | bytes 221216 | tf_op jit(solution)/shard_map/ppermute | solution.py:1084
  600.0 7.1 collective-permute-done.49
  617.4 5.4 collective-permute-done.60.refs_4_
  625.1 6.5 shard_map.257
  647.4 6.0 collective-permute-done.65.refs_2_
  676.9 8.5 %collective-permute-done.80.refs_1_ = bf16[288,768]{1,0:T(8,128)(2,1)S(1)} collective-permute-done((bf16[288,768]{1,0:T(8,128)(2,1)S(1)}, bf16[288,768]{1,0:T(8,128)(2,1)S(1)}, u32[]{:S(2)}, u32[]{:S(2)}) %collective-permute-start.80) | collective-permute-done | bytes 442400 | tf_op jit(solution)/shard_map/ppermute | solution.py:1084
  703.8 6.2 shard_map.264
  (705 shorter events, 379.8 us)
Async XLA Ops:
  7.2 59.0 %all-gather.9.cloned.1.call-start = ((), (), s32[]{:S(2)}) async-start(), calls=%async_computation.12 | async-start | bytes 2457600 | tf_op jit(solution)/shard_map/all_gather | solution.py:1150
  19.8 102.8 %all-gather.11.cloned.1.call-start = ((), (), s32[]{:S(2)}) async-start(), calls=%async_computation.13 | async-start | bytes 3317760 | tf_op jit(solution)/shard_map/all_gather | solution.py:1161
  25.5 138.3 %all-gather.13.cloned.1.call-start = ((), (), s32[]{:S(2)}) async-start(), calls=%async_computation.14 | async-start | bytes 2211840 | tf_op jit(solution)/shard_map/all_gather | solution.py:1150
  29.7 202.4 %all-gather.15.cloned.1.call-start = ((), (), s32[]{:S(2)}) async-start(), calls=%async_computation.15 | async-start | bytes 3317760 | tf_op jit(solution)/shard_map/all_gather | solution.py:1161
  29.7 43.0 %collective-permute-start = (bf16[320,1152]{1,0:T(8,128)(2,1)}, bf16[320,1152]{1,0:T(8,128)(2,1)}, u32[]{:S(2)}, u32[]{:S(2)}) collective-permute-start(bf16[320,1152]{1,0:T(8,128)(2,1)} %bitcast.91), channel_id=1, source_target_pairs={{0,4},{4,0},{8,12},{12,8},{16,20},{20,16},{24,28},{28,24},{1,5},{5... | collective-permute-start | bytes 2211848 | tf_op jit(solution)/shard_map/ppermute | solution.py:1084
  36.0 380.3 %reduce-scatter.7.cloned.1.call-start = ((), (), s32[]{:S(2)}) async-start(), calls=%async_computation.6 | async-start | bytes 2211840 | tf_op jit(solution)/shard_map/reduce_scatter | solution.py:1288
  70.1 31.2 %collective-permute-start.1 = (bf16[3,144,1536]{2,1,0:T(8,128)(2,1)}, bf16[3,144,1536]{2,1,0:T(8,128)(2,1)}, u32[]{:S(2)}, u32[]{:S(2)}) collective-permute-start(bf16[3,144,1536]{2,1,0:T(8,128)(2,1)} %shard_map.212), channel_id=1, source_target_pairs={{0,16},{4,20},{8,24},{12,28},{16,0},{20,4},{24,8},{28,12},{1,17},{... | collective-permute-start | bytes 3981320 | tf_op jit(solution)/shard_map/ppermute | solution.py:1084
  110.2 58.6 %collective-permute-start.4 = (bf16[576,576]{1,0:T(8,128)(2,1)}, bf16[576,576]{1,0:T(8,128)(2,1)}, u32[]{:S(2)}, u32[]{:S(2)}) collective-permute-start(bf16[576,576]{1,0:T(8,128)(2,1)} %constant_dynamic-slice_fusion.8), channel_id=1, source_target_pairs={{0,4},{4,0},{8,12},{12,8},{16,20},{20,16},{24,28},{28,24},{1,5},{5... | collective-permute-start | bytes 1990664 | tf_op jit(solution)/shard_map/ppermute | solution.py:1084
  127.4 47.9 %collective-permute-start.6 = (bf16[2,288,1152]{2,1,0:T(8,128)(2,1)}, bf16[2,288,1152]{2,1,0:T(8,128)(2,1)}, u32[]{:S(2)}, u32[]{:S(2)}) collective-permute-start(bf16[2,288,1152]{2,1,0:T(8,128)(2,1)} %shard_map.217.refs_6_), channel_id=1, source_target_pairs={{0,16},{4,20},{8,24},{12,28},{16,0},{20,4},{24,8},{28,12},{1,17},{... | collective-permute-start | bytes 3981320 | tf_op jit(solution)/shard_map/ppermute | solution.py:1084
  130.7 43.3 %collective-permute-start.7 = (bf16[1,288,1152]{2,1,0:T(8,128)(2,1)}, bf16[1,288,1152]{2,1,0:T(8,128)(2,1)}, u32[]{:S(2)}, u32[]{:S(2)}) collective-permute-start(bf16[1,288,1152]{2,1,0:T(8,128)(2,1)} %shard_map.218.refs_7_), channel_id=1, source_target_pairs={{0,16},{4,20},{8,24},{12,28},{16,0},{20,4},{24,8},{28,12},{1,17},{... | collective-permute-start | bytes 1990664 | tf_op jit(solution)/shard_map/ppermute | solution.py:1084
  133.7 45.6 %collective-permute-start.9 = (bf16[1,288,1152]{2,1,0:T(8,128)(2,1)}, bf16[1,288,1152]{2,1,0:T(8,128)(2,1)}, u32[]{:S(2)}, u32[]{:S(2)}) collective-permute-start(bf16[1,288,1152]{2,1,0:T(8,128)(2,1)} %shard_map.218.refs_7_), channel_id=1, source_target_pairs={{0,8},{4,12},{8,0},{12,4},{16,24},{20,28},{24,16},{28,20},{1,9},{5... | collective-permute-start | bytes 1990664 | tf_op jit(solution)/shard_map/ppermute | solution.py:1084
  135.2 73.2 %collective-permute-start.8 = (bf16[2,288,1152]{2,1,0:T(8,128)(2,1)}, bf16[2,288,1152]{2,1,0:T(8,128)(2,1)}, u32[]{:S(2)}, u32[]{:S(2)}) collective-permute-start(bf16[2,288,1152]{2,1,0:T(8,128)(2,1)} %shard_map.217.refs_6_), channel_id=1, source_target_pairs={{0,8},{4,12},{8,0},{12,4},{16,24},{20,28},{24,16},{28,20},{1,9},{5... | collective-permute-start | bytes 3981320 | tf_op jit(solution)/shard_map/ppermute | solution.py:1084
  168.8 39.5 %collective-permute-start.14 = (bf16[3,144,1536]{2,1,0:T(8,128)(2,1)}, bf16[3,144,1536]{2,1,0:T(8,128)(2,1)}, u32[]{:S(2)}, u32[]{:S(2)}) collective-permute-start(bf16[3,144,1536]{2,1,0:T(8,128)(2,1)} %shard_map.221), channel_id=1, source_target_pairs={{0,16},{4,20},{8,24},{12,28},{16,0},{20,4},{24,8},{28,12},{1,17},{... | collective-permute-start | bytes 3981320 | tf_op jit(solution)/shard_map/ppermute | solution.py:1084
  179.3 29.1 %collective-permute-start.10 = (bf16[288,1152]{1,0:T(8,128)(2,1)}, bf16[288,1152]{1,0:T(8,128)(2,1)}, u32[]{:S(2)}, u32[]{:S(2)}) collective-permute-start(bf16[288,1152]{1,0:T(8,128)(2,1)} %get-tuple-element.246), channel_id=1, source_target_pairs={{0,8},{4,12},{8,0},{12,4},{16,24},{20,28},{24,16},{28,20},{1,9},{5... | collective-permute-start | bytes 1990664 | tf_op jit(solution)/shard_map/ppermute | solution.py:1084
  186.0 28.0 %collective-permute-start.11 = (bf16[288,1152]{1,0:T(8,128)(2,1)}, bf16[288,1152]{1,0:T(8,128)(2,1)}, u32[]{:S(2)}, u32[]{:S(2)}) collective-permute-start(bf16[288,1152]{1,0:T(8,128)(2,1)} %get-tuple-element.245), channel_id=1, source_target_pairs={{0,8},{4,12},{8,0},{12,4},{16,24},{20,28},{24,16},{28,20},{1,9},{5... | collective-permute-start | bytes 1990664 | tf_op jit(solution)/shard_map/ppermute | solution.py:1084
  235.9 31.5 %collective-permute-start.16 = (bf16[2,288,1152]{2,1,0:T(8,128)(2,1)}, bf16[2,288,1152]{2,1,0:T(8,128)(2,1)}, u32[]{:S(2)}, u32[]{:S(2)}) collective-permute-start(bf16[2,288,1152]{2,1,0:T(8,128)(2,1)} %shard_map.226.refs_6_), channel_id=1, source_target_pairs={{0,16},{4,20},{8,24},{12,28},{16,0},{20,4},{24,8},{28,12},{1,17},{... | collective-permute-start | bytes 3981320 | tf_op jit(solution)/shard_map/ppermute | solution.py:1084
  237.4 31.1 %collective-permute-start.17 = (bf16[2,288,1152]{2,1,0:T(8,128)(2,1)}, bf16[2,288,1152]{2,1,0:T(8,128)(2,1)}, u32[]{:S(2)}, u32[]{:S(2)}) collective-permute-start(bf16[2,288,1152]{2,1,0:T(8,128)(2,1)} %shard_map.226.refs_6_), channel_id=1, source_target_pairs={{0,8},{4,12},{8,0},{12,4},{16,24},{20,28},{24,16},{28,20},{1,9},{5... | collective-permute-start | bytes 3981320 | tf_op jit(solution)/shard_map/ppermute | solution.py:1084
  280.0 42.8 %collective-permute-start.24 = (bf16[288,1152]{1,0:T(8,128)(2,1)}, bf16[288,1152]{1,0:T(8,128)(2,1)}, u32[]{:S(2)}, u32[]{:S(2)}) collective-permute-start(bf16[288,1152]{1,0:T(8,128)(2,1)} %slice_bitcast_fusion.1), channel_id=1, source_target_pairs={{0,8},{4,12},{8,0},{12,4},{16,24},{20,28},{24,16},{28,20},{1,9},{5... | collective-permute-start | bytes 1990664 | tf_op jit(solution)/shard_map/ppermute | solution.py:1084
  283.2 28.3 %collective-permute-start.23 = (bf16[1,288,1152]{2,1,0:T(8,128)(2,1)S(1)}, bf16[1,288,1152]{2,1,0:T(8,128)(2,1)S(1)}, u32[]{:S(2)}, u32[]{:S(2)}) collective-permute-start(bf16[1,288,1152]{2,1,0:T(8,128)(2,1)S(1)} %shard_map.228.refs_7_), channel_id=1, source_target_pairs={{0,8},{4,12},{8,0},{12,4},{16,24},{20,28},{24,16},{28,20},{1,9},{5... | collective-permute-start | bytes 1990664 | tf_op jit(solution)/shard_map/ppermute | solution.py:1084
  297.0 25.8 %collective-permute-start.25 = (bf16[288,1152]{1,0:T(8,128)(2,1)}, bf16[288,1152]{1,0:T(8,128)(2,1)}, u32[]{:S(2)}, u32[]{:S(2)}) collective-permute-start(bf16[288,1152]{1,0:T(8,128)(2,1)} %slice_bitcast_fusion), channel_id=1, source_target_pairs={{0,16},{4,20},{8,24},{12,28},{16,0},{20,4},{24,8},{28,12},{1,17},{... | collective-permute-start | bytes 1990664 | tf_op jit(solution)/shard_map/ppermute | solution.py:1084
  370.6 145.9 %reduce-scatter.9.cloned.1.call-start = ((), (), s32[]{:S(2)}) async-start(), calls=%async_computation.7 | async-start | bytes 4423680 | tf_op jit(solution)/shard_map/reduce_scatter | solution.py:1288
  370.7 45.5 %collective-permute-start.35 = (bf16[1152,768]{1,0:T(8,128)(2,1)}, bf16[1152,768]{1,0:T(8,128)(2,1)}, u32[]{:S(2)}, u32[]{:S(2)}) collective-permute-start(bf16[1152,768]{1,0:T(8,128)(2,1)} %get-tuple-element.154), channel_id=1, source_target_pairs={{0,8},{4,12},{8,0},{12,4},{16,24},{20,28},{24,16},{28,20},{1,9},{5... | collective-permute-start | bytes 5308424 | tf_op jit(solution)/shard_map/ppermute | solution.py:1084
  371.5 44.7 %collective-permute-start.36 = (bf16[1152,768]{1,0:T(8,128)(2,1)}, bf16[1152,768]{1,0:T(8,128)(2,1)}, u32[]{:S(2)}, u32[]{:S(2)}) collective-permute-start(bf16[1152,768]{1,0:T(8,128)(2,1)} %get-tuple-element.156), channel_id=1, source_target_pairs={{0,16},{4,20},{8,24},{12,28},{16,0},{20,4},{24,8},{28,12},{1,17},{... | collective-permute-start | bytes 5308424 | tf_op jit(solution)/shard_map/ppermute | solution.py:1084
  422.7 146.3 %reduce-scatter.13.cloned.1.call-start = ((), (), s32[]{:S(2)}) async-start(), calls=%async_computation.9 | async-start | bytes 2211840 | tf_op jit(solution)/shard_map/reduce_scatter | solution.py:1288
  422.7 30.7 %collective-permute-start.28 = (bf16[640,1152]{1,0:T(8,128)(2,1)}, bf16[640,1152]{1,0:T(8,128)(2,1)}, u32[]{:S(2)}, u32[]{:S(2)}) collective-permute-start(bf16[640,1152]{1,0:T(8,128)(2,1)} %get-tuple-element.134), channel_id=1, source_target_pairs={{0,4},{4,0},{8,12},{12,8},{16,20},{20,16},{24,28},{28,24},{1,5},{5... | collective-permute-start | bytes 4423688 | tf_op jit(solution)/shard_map/ppermute | solution.py:1084
  475.6 93.7 %reduce-scatter.11.cloned.1.call-start = ((), (), s32[]{:S(2)}) async-start(), calls=%async_computation.8 | async-start | bytes 2211840 | tf_op jit(solution)/shard_map/reduce_scatter | solution.py:1288
  523.3 148.6 %reduce-scatter.17.cloned.1.call-start = ((), (), s32[]{:S(2)}) async-start(), calls=%async_computation.11 | async-start | bytes 4423680 | tf_op jit(solution)/shard_map/reduce_scatter | solution.py:1288
  523.4 45.5 %collective-permute-start.50 = (bf16[1152,768]{1,0:T(8,128)(2,1)}, bf16[1152,768]{1,0:T(8,128)(2,1)}, u32[]{:S(2)}, u32[]{:S(2)}) collective-permute-start(bf16[1152,768]{1,0:T(8,128)(2,1)} %get-tuple-element.186), channel_id=1, source_target_pairs={{0,8},{4,12},{8,0},{12,4},{16,24},{20,28},{24,16},{28,20},{1,9},{5... | collective-permute-start | bytes 5308424 | tf_op jit(solution)/shard_map/ppermute | solution.py:1084
  524.0 44.9 %collective-permute-start.51 = (bf16[1152,768]{1,0:T(8,128)(2,1)}, bf16[1152,768]{1,0:T(8,128)(2,1)}, u32[]{:S(2)}, u32[]{:S(2)}) collective-permute-start(bf16[1152,768]{1,0:T(8,128)(2,1)} %get-tuple-element.188), channel_id=1, source_target_pairs={{0,16},{4,20},{8,24},{12,28},{16,0},{20,4},{24,8},{28,12},{1,17},{... | collective-permute-start | bytes 5308424 | tf_op jit(solution)/shard_map/ppermute | solution.py:1084
  576.7 124.1 %reduce-scatter.15.cloned.1.call-start = ((), (), s32[]{:S(2)}) async-start(), calls=%async_computation.10 | async-start | bytes 2211840 | tf_op jit(solution)/shard_map/reduce_scatter | solution.py:1288
  581.5 50.6 %collective-permute-start.71 = (bf16[384,1152]{1,0:T(8,128)(2,1)S(1)}, bf16[384,1152]{1,0:T(8,128)(2,1)S(1)}, u32[]{:S(2)}, u32[]{:S(2)}) collective-permute-start(bf16[384,1152]{1,0:T(8,128)(2,1)S(1)} %shard_map.240.refs_5_.refs_9_), channel_id=1, source_target_pairs={{0,4},{4,0},{8,12},{12,8},{16,20},{20,16},{24,28},{28,24},{1,5},{5... | collective-permute-start | bytes 2654216 | tf_op jit(solution)/shard_map/ppermute | solution.py:1084
  662.8 33.5 %collective-permute-start.88 = (bf16[384,1152]{1,0:T(8,128)(2,1)S(1)}, bf16[384,1152]{1,0:T(8,128)(2,1)S(1)}, u32[]{:S(2)}, u32[]{:S(2)}) collective-permute-start(bf16[384,1152]{1,0:T(8,128)(2,1)S(1)} %shard_map.255.refs_5_.refs_9_), channel_id=1, source_target_pairs={{0,4},{4,0},{8,12},{12,8},{16,20},{20,16},{24,28},{28,24},{1,5},{5... | collective-permute-start | bytes 2654216 | tf_op jit(solution)/shard_map/ppermute | solution.py:1084
  (248 other events, 1801.3 us)
Sparse Core Ops, SparseCore 0:
  19.9 46.2 all-gather.8
  68.3 54.1 all-gather.10
  124.7 39.0 all-gather.12
  165.8 54.2 all-gather.14
  370.7 36.8 reduce-scatter.6
  422.8 64.7 reduce-scatter.8
  490.1 38.6 reduce-scatter.12
  531.7 37.4 reduce-scatter.10
  576.8 65.4 reduce-scatter.16
  658.6 37.4 reduce-scatter.14

commit v5 on v4

--- a/solution.py
+++ b/solution.py
@@ -825,6 +825,50 @@
     )
 
 
+def local_kernel(ids_ref, gain_ref, key_ref, value_ref, query_ref, out_ref, local, piece):
+    row, pair = ids_ref[3], ids_ref[2]
+    half = local.shape[0] // 2
+    low = 0
+    for ref in (key_ref, value_ref, query_ref, out_ref):
+        cols = ref.shape[2] // 2
+        for index in range(2):
+
+            @pl.when(pair == index)
+            def _(ref=ref, low=low, cols=cols, index=index):
+                local[:, low : low + cols] = ref[0, :, index * cols : (index + 1) * cols]
+
+        low += cols
+    for index in range(2):
+
+        @pl.when(row == index)
+        def _(index=index):
+            piece[:half, :] = local[index * half : (index + 1) * half, :]
+
+    if piece.shape[0] > half:
+        piece[half:, :] = jnp.broadcast_to(gain_ref[...], (piece.shape[0] - half, low))
+
+
+def local_weights(layer, ids, gains, weights):
+    depth = weights[0].shape[1]
+    columns = sum(weight.shape[2] for weight in weights) // 2
+    rows = depth // 2 + (0 if layer else 16)
+    return call(
+        local_kernel,
+        [shaped((depth, columns), BF16), shaped((rows, columns), BF16)],
+        (ids, gains, *weights),
+        16,
+        in_specs=[SCALARS, pl.BlockSpec(gains.shape, lambda _: (0, 0))]
+        + [
+            pl.BlockSpec((1, *weight.shape[1:]), lambda _: (layer, 0, 0)) for weight in weights
+        ],
+        out_specs=[
+            pl.BlockSpec((depth, columns), lambda _: (0, 0)),
+            pl.BlockSpec((rows, columns), lambda _: (0, 0)),
+        ],
+        grid=(1,),
+    )
+
+
 def join_kernel(ids_ref, local, mine, other, out, sem):
     plane, row = ids_ref[1], ids_ref[3]
     half = local.shape[0] // 2
@@ -1127,26 +1171,10 @@
     ids = jnp.stack([quarter, plane, pair, row, side])
     ff_weights = (w_gate, w_up, w_down)
 
-    def attn_local(layer):
-        return jnp.concatenate(
-            [
-                lax.dynamic_slice(weight[layer], (0, cols * pair), (depth, cols))
-                for weight, cols in (
-                    (w_key, KEY_HALF),
-                    (w_value, KEY_HALF),
-                    (w_query, QUERY_HALF),
-                    (w_out, half_width),
-                )
-            ],
-            axis=1,
-        )
+    gain_row = jnp.pad(gain_line, ((0, 0), (0, columns - gain_line.shape[1])))
 
     def attn_gather(layer):
-        local = attn_local(layer)
-        piece = lax.dynamic_slice(local, (half_depth * row, 0), (half_depth, columns))
-        if layer == 0:
-            line = jnp.pad(gain_line, ((0, 15), (0, columns - gain_line.shape[1])))
-            piece = jnp.concatenate([piece, line], axis=0)
+        local, piece = local_weights(layer, ids, gain_row, (w_key, w_value, w_query, w_out))
         return local, lax.all_gather(piece, "wt", axis=0, tiled=False)
 
     def attn_weights(local, mine, other, after):

time: 743 us -> 739 us (level)
    unnamed x356 -> x372, local copies, waits for them, and re-layouts: 86 us -> 97.5 us
    pallas_call x56 -> x58, Pallas kernels: 233 us -> 235 us  [call(): pl.pallas_call(body, out_shape=outs, in_specs=(in_specs or [WHOLE] * coun...]
  transfers between devices with their start and end apart: 102 -> 102, of which waited for: 44 -> 45; matrix products, arithmetic and copies ran while one was open for 11% -> 11% of each run, Pallas kernels for 27% -> 27%
where the time goes in v5:
time: 739 us; the launch traced here: 730 us
  Pallas kernels  235 us (32%)
  waiting for transfers between devices  229 us (31%)
  local copies, waits for them, and re-layouts  131 us (18%)
  starting transfers between devices  74.2 us (10%)
  other arithmetic  25.5 us (3%)
  matrix products  19.2 us (3%)
  between operations  16.5 us (2%)
    pallas_call x58, Pallas kernels, call(): pl.pallas_call(body, out_shape=outs, in_specs=(in_specs or [WHOLE] * coun...  235 us
    ppermute x92, waiting for transfers between devices, flip(): return lax.ppermute(value, axis, [(i, i ^ bit) for i in range(count)])  190 us
    unnamed x372, local copies, waits for them, and re-layouts  97.5 us
    ppermute x92, starting transfers between devices, flip(): return lax.ppermute(value, axis, [(i, i ^ bit) for i in range(count)])  73.8 us
    all_gather x2, waiting for transfers between devices, attn_gather(): return (local, lax.all_gather(piece, 'wt', axis=0, tiled=False))  34.2 us
  transfers between devices with their start and end apart: 102, of which 45 were waited for; matrix products, arithmetic and copies ran while one was open for 11% of the time, Pallas kernels for 27%

profile of v5, /device:TPU:0, one launch (start us, length us, event | category | flops | bytes accessed | tf_op | source)
XLA Modules:
  0.0 729.9 jit_solution(10914835079249728915)
XLA Ops:
  40.9 21.1 %all-gather.9.cloned.1.call-done = bf16[640,1536]{1,0:T(8,128)(2,1)} async-done(((bf16[160,1536]{1,0:T(8,128)(2,1)}), bf16[640,1536]{1,0:T(8,128)(2,1)}) %all-gather.9.cloned.1.call-update) | async-done | bytes 1966096 | tf_op jit(solution)/shard_map/all_gather | solution.py:1178
  79.8 17.3 %collective-permute-done.1.refs_3_ = bf16[3,144,1536]{2,1,0:T(8,128)(2,1)} collective-permute-done((bf16[3,144,1536]{2,1,0:T(8,128)(2,1)}, bf16[3,144,1536]{2,1,0:T(8,128)(2,1)}, u32[]{:S(2)}, u32[]{:S(2)}) %collective-permute-start.1) | collective-permute-done | bytes 1327136 | tf_op jit(solution)/shard_map/ppermute | solution.py:1128
  136.6 8.3 %shard_map.220 = (bf16[576,640]{1,0:T(8,128)(2,1)S(1)}, f32[9,1,640]{2,1,0:T(1,128)S(1)}) custom-call(bf16[576,640]{1,0:T(8,128)(2,1)S(1)} %copy-done.59, bf16[640,384]{1,0:T(8,128)(2,1)S(1)} %copy-done.74, bf16[384,640]{1,0:T(8,128)(2,1)S(1)} %copy-done.84, bf16[512,384]{1,0:T(8,128)(2,1)S(1)} %copy-done.22, s32[512,1]{1,0:T(8,128)S(1)} %copy-done.33, ...), custom_call_target="tpu_custom_call" | custom-call | flops 1 | bytes 1 | tf_op jit(solution)/shard_map/pallas_call | solution.py:80
  146.4 13.2 %all-gather.13.cloned.1.call-done = bf16[576,1536]{1,0:T(8,128)(2,1)} async-done(((bf16[144,1536]{1,0:T(8,128)(2,1)}), bf16[576,1536]{1,0:T(8,128)(2,1)}) %all-gather.13.cloned.1.call-update) | async-done | bytes 1769488 | tf_op jit(solution)/shard_map/all_gather | solution.py:1178
  175.6 6.1 collective-permute-done.12.refs_9_
  196.6 7.5 %collective-permute-done.13.refs_10_ = bf16[144,1152]{1,0:T(8,128)(2,1)} collective-permute-done((bf16[144,1152]{1,0:T(8,128)(2,1)}, bf16[144,1152]{1,0:T(8,128)(2,1)}, u32[]{:S(2)}, u32[]{:S(2)}) %collective-permute-start.13) | collective-permute-done | bytes 331808 | tf_op jit(solution)/shard_map/ppermute | solution.py:1128
  204.1 5.7 collective-permute-done.11.refs_8_
  211.5 15.7 %shard_map.224 = (bf16[4,1152,768]{2,1,0:T(8,128)(2,1)}, bf16[1536,1152]{1,0:T(8,128)(2,1)}, bf16[640,1536]{1,0:T(8,128)(2,1)}, bf16[640,1536]{1,0:T(8,128)(2,1)...) custom-call(s32[5]{0:T(128)S(1)} %stack.28.refs_0_, bf16[640,1152]{1,0:T(8,128)(2,1)S(1)} %get-tuple-element.130.refs_1_, ...), custom_call_target="tpu_custom_call" | custom-call | flops 1 | bytes 1 | tf_op jit(solution)/shard_map/pallas_call | solution.py:80
  252.4 10.7 %collective-permute-done.16.refs_3_ = bf16[2,288,1152]{2,1,0:T(8,128)(2,1)} collective-permute-done((bf16[2,288,1152]{2,1,0:T(8,128)(2,1)}, bf16[2,288,1152]{2,1,0:T(8,128)(2,1)}, u32[]{:S(2)}, u32[]{:S(2)}) %collective-permute-start.16) | collective-permute-done | bytes 1327136 | tf_op jit(solution)/shard_map/ppermute | solution.py:1128
  279.5 8.3 %shard_map.231 = (bf16[576,640]{1,0:T(8,128)(2,1)S(1)}, f32[9,1,640]{2,1,0:T(1,128)S(1)}) custom-call(bf16[576,640]{1,0:T(8,128)(2,1)S(1)} %get-tuple-element.136.refs_0_, bf16[640,384]{1,0:T(8,128)(2,1)S(1)} %get-tuple-element.137.refs_1_.refs_2_, bf16[384,640]{1,0:T(8,128)(2,1)S(1)} %get-tuple-element.138.refs_2_.refs_3_, ...), custom_call_target="tpu_custom_call" | custom-call | flops 1 | bytes 1 | tf_op jit(solution)/shard_map/pallas_call | solution.py:80
  296.6 10.7 %collective-permute-done.23.refs_6_ = bf16[1,288,1152]{2,1,0:T(8,128)(2,1)S(1)} collective-permute-done((bf16[1,288,1152]{2,1,0:T(8,128)(2,1)S(1)}, bf16[1,288,1152]{2,1,0:T(8,128)(2,1)S(1)}, u32[]{:S(2)}, u32[]{:S(2)}) %collective-permute-start.23) | collective-permute-done | bytes 663584 | tf_op jit(solution)/shard_map/ppermute | solution.py:1128
  318.6 12.6 %shard_map.233 = (bf16[4,1152,768]{2,1,0:T(8,128)(2,1)}, bf16[1536,1152]{1,0:T(8,128)(2,1)S(1)}, bf16[640,1536]{1,0:T(8,128)(2,1)S(1)}, bf16[640,1536]{1,0:T(8,1...) custom-call(s32[5]{0:T(128)S(1)} %stack.28.refs_0_, ...), custom_call_target="tpu_custom_call" | custom-call | flops 1 | bytes 1 | tf_op jit(solution)/shard_map/pallas_call | solution.py:80
  332.5 5.4 shard_map.234
  341.7 19.1 %shard_map.235 = (bf16[1152,768]{1,0:T(8,128)(2,1)}, bf16[1152,768]{1,0:T(8,128)(2,1)}, bf16[1152,768]{1,0:T(8,128)(2,1)}, bf16[1152,768]{1,0:T(8,128)(2,1)}, bf16[640,1152]{1,0:T(8,128)(2,1)S(1)}) custom-call(bf16[640,1152]{1,0:T(8,128)(2,1)S(1)} %copy-done.13, bf16[640,1152]{1,0:T(8,128)(2,1)S(1)} %get-tuple-element.141.refs_1_, ...), custom_call_target="tpu_custom_call" | custom-call | flops 1 | bytes 1 | tf_op jit(solution)/shard_map/pallas_call | solution.py:80
  370.8 5.7 shard_map.237
  380.1 17.3 %shard_map.238 = (bf16[576,640]{1,0:T(8,128)(2,1)S(1)}, f32[512,384]{1,0:T(8,128)S(1)}, f32[512,384]{1,0:T(8,128)S(1)}) custom-call(bf16[576,640]{1,0:T(8,128)(2,1)S(1)} %copy-done.62, bf16[576,640]{1,0:T(8,128)(2,1)S(1)} %convolution_convert_fusion.5.refs_1_, bf16[640,384]{1,0:T(8,128)(2,1)S(1)} %copy-done.77, bf16[384,640]{1,0:T(8,128)(2,1)S(1)} %copy-done.87, ...), custom_call_target="tpu_custom_call" | custom-call | flops 1 | bytes 1 | tf_op jit(solution)/shard_map/pallas_call | solution.py:80
  400.2 11.6 %collective-permute-done.33 = bf16[256,384]{1,0:T(8,128)(2,1)S(1)} collective-permute-done((bf16[256,384]{1,0:T(8,128)(2,1)S(1)}, bf16[256,384]{1,0:T(8,128)(2,1)S(1)}, u32[]{:S(2)}, u32[]{:S(2)}) %collective-permute-start.33) | collective-permute-done | bytes 196640 | tf_op jit(solution)/shard_map/ppermute | solution.py:1128
  413.0 5.4 shard_map.239.refs_3_.refs_5_
  442.3 5.3 shard_map.243
  452.8 12.8 %collective-permute-done.42.refs_2_ = bf16[4,144,768]{2,1,0:T(8,128)(2,1)S(1)} collective-permute-done((bf16[4,144,768]{2,1,0:T(8,128)(2,1)S(1)}, bf16[4,144,768]{2,1,0:T(8,128)(2,1)S(1)}, u32[]{:S(2)}, u32[]{:S(2)}) %collective-permute-start.42) | collective-permute-done | bytes 884768 | tf_op jit(solution)/shard_map/ppermute | solution.py:1128
  488.7 21.5 %shard_map.248 = (bf16[1152,768]{1,0:T(8,128)(2,1)}, bf16[1152,768]{1,0:T(8,128)(2,1)}, bf16[1152,768]{1,0:T(8,128)(2,1)}, bf16[1152,768]{1,0:T(8,128)(2,1)}, bf16[640,1152]{1,0:T(8,128)(2,1)S(1)}) custom-call(bf16[640,1152]{1,0:T(8,128)(2,1)S(1)} %get-tuple-element.174.refs_2_.refs_0_, bf16[640,1152]{1,0:T(8,128)(2,1)S(1)} %copy-done.36, ...), custom_call_target="tpu_custom_call" | custom-call | flops 1 | bytes 1 | tf_op jit(solution)/shard_map/pallas_call | solution.py:80
  523.5 5.7 shard_map.250
  533.2 17.0 %shard_map.251 = (bf16[576,640]{1,0:T(8,128)(2,1)S(1)}, f32[512,384]{1,0:T(8,128)S(1)}, f32[512,384]{1,0:T(8,128)S(1)}) custom-call(bf16[576,640]{1,0:T(8,128)(2,1)S(1)} %copy-done.60, bf16[576,640]{1,0:T(8,128)(2,1)S(1)} %convolution_convert_fusion.4.refs_1_, bf16[640,384]{1,0:T(8,128)(2,1)S(1)} %copy-done.75, bf16[384,640]{1,0:T(8,128)(2,1)S(1)} %copy-done.85, ...), custom_call_target="tpu_custom_call" | custom-call | flops 1 | bytes 1 | tf_op jit(solution)/shard_map/pallas_call | solution.py:80
  552.3 12.3 %collective-permute-done.48 = bf16[256,384]{1,0:T(8,128)(2,1)S(1)} collective-permute-done((bf16[256,384]{1,0:T(8,128)(2,1)S(1)}, bf16[256,384]{1,0:T(8,128)(2,1)S(1)}, u32[]{:S(2)}, u32[]{:S(2)}) %collective-permute-start.48) | collective-permute-done | bytes 196640 | tf_op jit(solution)/shard_map/ppermute | solution.py:1128
  567.0 5.4 shard_map.252.refs_3_.refs_5_
  577.9 13.5 %collective-permute-done.56.refs_1_ = bf16[144,768]{1,0:T(8,128)(2,1)S(1)} collective-permute-done((bf16[144,768]{1,0:T(8,128)(2,1)S(1)}, bf16[144,768]{1,0:T(8,128)(2,1)S(1)}, u32[]{:S(2)}, u32[]{:S(2)}) %collective-permute-start.56) | collective-permute-done | bytes 221216 | tf_op jit(solution)/shard_map/ppermute | solution.py:1128
  595.8 7.1 collective-permute-done.49
  613.1 5.5 collective-permute-done.60.refs_4_
  620.9 6.5 shard_map.259
  643.1 6.0 collective-permute-done.65.refs_2_
  672.6 8.4 %collective-permute-done.80.refs_1_ = bf16[288,768]{1,0:T(8,128)(2,1)S(1)} collective-permute-done((bf16[288,768]{1,0:T(8,128)(2,1)S(1)}, bf16[288,768]{1,0:T(8,128)(2,1)S(1)}, u32[]{:S(2)}, u32[]{:S(2)}) %collective-permute-start.80) | collective-permute-done | bytes 442400 | tf_op jit(solution)/shard_map/ppermute | solution.py:1128
  699.6 6.2 shard_map.266
  (711 shorter events, 378.4 us)
Async XLA Ops:
  7.2 54.8 %all-gather.9.cloned.1.call-start = ((), (), s32[]{:S(2)}) async-start(), calls=%async_computation.12 | async-start | bytes 2457600 | tf_op jit(solution)/shard_map/all_gather | solution.py:1178
  15.5 102.8 %all-gather.11.cloned.1.call-start = ((), (), s32[]{:S(2)}) async-start(), calls=%async_computation.13 | async-start | bytes 3317760 | tf_op jit(solution)/shard_map/all_gather | solution.py:1189
  21.1 138.4 %all-gather.13.cloned.1.call-start = ((), (), s32[]{:S(2)}) async-start(), calls=%async_computation.14 | async-start | bytes 2211840 | tf_op jit(solution)/shard_map/all_gather | solution.py:1178
  28.5 199.3 %all-gather.15.cloned.1.call-start = ((), (), s32[]{:S(2)}) async-start(), calls=%async_computation.15 | async-start | bytes 3317760 | tf_op jit(solution)/shard_map/all_gather | solution.py:1189
  28.6 39.9 %collective-permute-start = (bf16[320,1152]{1,0:T(8,128)(2,1)}, bf16[320,1152]{1,0:T(8,128)(2,1)}, u32[]{:S(2)}, u32[]{:S(2)}) collective-permute-start(bf16[320,1152]{1,0:T(8,128)(2,1)} %bitcast.75), channel_id=1, source_target_pairs={{0,4},{4,0},{8,12},{12,8},{16,20},{20,16},{24,28},{28,24},{1,5},{5... | collective-permute-start | bytes 2211848 | tf_op jit(solution)/shard_map/ppermute | solution.py:1128
  34.6 377.3 %reduce-scatter.7.cloned.1.call-start = ((), (), s32[]{:S(2)}) async-start(), calls=%async_computation.6 | async-start | bytes 2211840 | tf_op jit(solution)/shard_map/reduce_scatter | solution.py:1316
  65.9 31.2 %collective-permute-start.1 = (bf16[3,144,1536]{2,1,0:T(8,128)(2,1)}, bf16[3,144,1536]{2,1,0:T(8,128)(2,1)}, u32[]{:S(2)}, u32[]{:S(2)}) collective-permute-start(bf16[3,144,1536]{2,1,0:T(8,128)(2,1)} %shard_map.213), channel_id=1, source_target_pairs={{0,16},{4,20},{8,24},{12,28},{16,0},{20,4},{24,8},{28,12},{1,17},{... | collective-permute-start | bytes 3981320 | tf_op jit(solution)/shard_map/ppermute | solution.py:1128
  106.0 58.6 %collective-permute-start.4 = (bf16[576,576]{1,0:T(8,128)(2,1)}, bf16[576,576]{1,0:T(8,128)(2,1)}, u32[]{:S(2)}, u32[]{:S(2)}) collective-permute-start(bf16[576,576]{1,0:T(8,128)(2,1)} %constant_dynamic-slice_fusion.1), channel_id=1, source_target_pairs={{0,4},{4,0},{8,12},{12,8},{16,20},{20,16},{24,28},{28,24},{1,5},{5... | collective-permute-start | bytes 1990664 | tf_op jit(solution)/shard_map/ppermute | solution.py:1128
  123.1 47.9 %collective-permute-start.6 = (bf16[2,288,1152]{2,1,0:T(8,128)(2,1)}, bf16[2,288,1152]{2,1,0:T(8,128)(2,1)}, u32[]{:S(2)}, u32[]{:S(2)}) collective-permute-start(bf16[2,288,1152]{2,1,0:T(8,128)(2,1)} %shard_map.218.refs_6_), channel_id=1, source_target_pairs={{0,16},{4,20},{8,24},{12,28},{16,0},{20,4},{24,8},{28,12},{1,17},{... | collective-permute-start | bytes 3981320 | tf_op jit(solution)/shard_map/ppermute | solution.py:1128
  126.4 43.3 %collective-permute-start.7 = (bf16[1,288,1152]{2,1,0:T(8,128)(2,1)}, bf16[1,288,1152]{2,1,0:T(8,128)(2,1)}, u32[]{:S(2)}, u32[]{:S(2)}) collective-permute-start(bf16[1,288,1152]{2,1,0:T(8,128)(2,1)} %shard_map.219.refs_7_), channel_id=1, source_target_pairs={{0,16},{4,20},{8,24},{12,28},{16,0},{20,4},{24,8},{28,12},{1,17},{... | collective-permute-start | bytes 1990664 | tf_op jit(solution)/shard_map/ppermute | solution.py:1128
  129.4 45.6 %collective-permute-start.9 = (bf16[1,288,1152]{2,1,0:T(8,128)(2,1)}, bf16[1,288,1152]{2,1,0:T(8,128)(2,1)}, u32[]{:S(2)}, u32[]{:S(2)}) collective-permute-start(bf16[1,288,1152]{2,1,0:T(8,128)(2,1)} %shard_map.219.refs_7_), channel_id=1, source_target_pairs={{0,8},{4,12},{8,0},{12,4},{16,24},{20,28},{24,16},{28,20},{1,9},{5... | collective-permute-start | bytes 1990664 | tf_op jit(solution)/shard_map/ppermute | solution.py:1128
  130.9 73.2 %collective-permute-start.8 = (bf16[2,288,1152]{2,1,0:T(8,128)(2,1)}, bf16[2,288,1152]{2,1,0:T(8,128)(2,1)}, u32[]{:S(2)}, u32[]{:S(2)}) collective-permute-start(bf16[2,288,1152]{2,1,0:T(8,128)(2,1)} %shard_map.218.refs_6_), channel_id=1, source_target_pairs={{0,8},{4,12},{8,0},{12,4},{16,24},{20,28},{24,16},{28,20},{1,9},{5... | collective-permute-start | bytes 3981320 | tf_op jit(solution)/shard_map/ppermute | solution.py:1128
  164.5 39.5 %collective-permute-start.14 = (bf16[3,144,1536]{2,1,0:T(8,128)(2,1)}, bf16[3,144,1536]{2,1,0:T(8,128)(2,1)}, u32[]{:S(2)}, u32[]{:S(2)}) collective-permute-start(bf16[3,144,1536]{2,1,0:T(8,128)(2,1)} %shard_map.223), channel_id=1, source_target_pairs={{0,16},{4,20},{8,24},{12,28},{16,0},{20,4},{24,8},{28,12},{1,17},{... | collective-permute-start | bytes 3981320 | tf_op jit(solution)/shard_map/ppermute | solution.py:1128
  175.0 29.1 %collective-permute-start.10 = (bf16[288,1152]{1,0:T(8,128)(2,1)}, bf16[288,1152]{1,0:T(8,128)(2,1)}, u32[]{:S(2)}, u32[]{:S(2)}) collective-permute-start(bf16[288,1152]{1,0:T(8,128)(2,1)} %get-tuple-element.250), channel_id=1, source_target_pairs={{0,8},{4,12},{8,0},{12,4},{16,24},{20,28},{24,16},{28,20},{1,9},{5... | collective-permute-start | bytes 1990664 | tf_op jit(solution)/shard_map/ppermute | solution.py:1128
  181.7 28.0 %collective-permute-start.11 = (bf16[288,1152]{1,0:T(8,128)(2,1)}, bf16[288,1152]{1,0:T(8,128)(2,1)}, u32[]{:S(2)}, u32[]{:S(2)}) collective-permute-start(bf16[288,1152]{1,0:T(8,128)(2,1)} %get-tuple-element.249), channel_id=1, source_target_pairs={{0,8},{4,12},{8,0},{12,4},{16,24},{20,28},{24,16},{28,20},{1,9},{5... | collective-permute-start | bytes 1990664 | tf_op jit(solution)/shard_map/ppermute | solution.py:1128
  231.6 31.5 %collective-permute-start.16 = (bf16[2,288,1152]{2,1,0:T(8,128)(2,1)}, bf16[2,288,1152]{2,1,0:T(8,128)(2,1)}, u32[]{:S(2)}, u32[]{:S(2)}) collective-permute-start(bf16[2,288,1152]{2,1,0:T(8,128)(2,1)} %shard_map.228.refs_6_), channel_id=1, source_target_pairs={{0,16},{4,20},{8,24},{12,28},{16,0},{20,4},{24,8},{28,12},{1,17},{... | collective-permute-start | bytes 3981320 | tf_op jit(solution)/shard_map/ppermute | solution.py:1128
  233.2 31.1 %collective-permute-start.17 = (bf16[2,288,1152]{2,1,0:T(8,128)(2,1)}, bf16[2,288,1152]{2,1,0:T(8,128)(2,1)}, u32[]{:S(2)}, u32[]{:S(2)}) collective-permute-start(bf16[2,288,1152]{2,1,0:T(8,128)(2,1)} %shard_map.228.refs_6_), channel_id=1, source_target_pairs={{0,8},{4,12},{8,0},{12,4},{16,24},{20,28},{24,16},{28,20},{1,9},{5... | collective-permute-start | bytes 3981320 | tf_op jit(solution)/shard_map/ppermute | solution.py:1128
  275.7 42.8 %collective-permute-start.24 = (bf16[288,1152]{1,0:T(8,128)(2,1)}, bf16[288,1152]{1,0:T(8,128)(2,1)}, u32[]{:S(2)}, u32[]{:S(2)}) collective-permute-start(bf16[288,1152]{1,0:T(8,128)(2,1)} %slice_bitcast_fusion.1), channel_id=1, source_target_pairs={{0,8},{4,12},{8,0},{12,4},{16,24},{20,28},{24,16},{28,20},{1,9},{5... | collective-permute-start | bytes 1990664 | tf_op jit(solution)/shard_map/ppermute | solution.py:1128
  279.0 28.3 %collective-permute-start.23 = (bf16[1,288,1152]{2,1,0:T(8,128)(2,1)S(1)}, bf16[1,288,1152]{2,1,0:T(8,128)(2,1)S(1)}, u32[]{:S(2)}, u32[]{:S(2)}) collective-permute-start(bf16[1,288,1152]{2,1,0:T(8,128)(2,1)S(1)} %shard_map.230.refs_7_), channel_id=1, source_target_pairs={{0,8},{4,12},{8,0},{12,4},{16,24},{20,28},{24,16},{28,20},{1,9},{5... | collective-permute-start | bytes 1990664 | tf_op jit(solution)/shard_map/ppermute | solution.py:1128
  292.7 25.8 %collective-permute-start.25 = (bf16[288,1152]{1,0:T(8,128)(2,1)}, bf16[288,1152]{1,0:T(8,128)(2,1)}, u32[]{:S(2)}, u32[]{:S(2)}) collective-permute-start(bf16[288,1152]{1,0:T(8,128)(2,1)} %slice_bitcast_fusion), channel_id=1, source_target_pairs={{0,16},{4,20},{8,24},{12,28},{16,0},{20,4},{24,8},{28,12},{1,17},{... | collective-permute-start | bytes 1990664 | tf_op jit(solution)/shard_map/ppermute | solution.py:1128
  366.3 145.9 %reduce-scatter.9.cloned.1.call-start = ((), (), s32[]{:S(2)}) async-start(), calls=%async_computation.7 | async-start | bytes 4423680 | tf_op jit(solution)/shard_map/reduce_scatter | solution.py:1316
  366.4 45.5 %collective-permute-start.35 = (bf16[1152,768]{1,0:T(8,128)(2,1)}, bf16[1152,768]{1,0:T(8,128)(2,1)}, u32[]{:S(2)}, u32[]{:S(2)}) collective-permute-start(bf16[1152,768]{1,0:T(8,128)(2,1)} %get-tuple-element.162), channel_id=1, source_target_pairs={{0,8},{4,12},{8,0},{12,4},{16,24},{20,28},{24,16},{28,20},{1,9},{5... | collective-permute-start | bytes 5308424 | tf_op jit(solution)/shard_map/ppermute | solution.py:1128
  367.2 44.7 %collective-permute-start.36 = (bf16[1152,768]{1,0:T(8,128)(2,1)}, bf16[1152,768]{1,0:T(8,128)(2,1)}, u32[]{:S(2)}, u32[]{:S(2)}) collective-permute-start(bf16[1152,768]{1,0:T(8,128)(2,1)} %get-tuple-element.164), channel_id=1, source_target_pairs={{0,16},{4,20},{8,24},{12,28},{16,0},{20,4},{24,8},{28,12},{1,17},{... | collective-permute-start | bytes 5308424 | tf_op jit(solution)/shard_map/ppermute | solution.py:1128
  418.4 146.3 %reduce-scatter.13.cloned.1.call-start = ((), (), s32[]{:S(2)}) async-start(), calls=%async_computation.9 | async-start | bytes 2211840 | tf_op jit(solution)/shard_map/reduce_scatter | solution.py:1316
  418.5 30.7 %collective-permute-start.28 = (bf16[640,1152]{1,0:T(8,128)(2,1)}, bf16[640,1152]{1,0:T(8,128)(2,1)}, u32[]{:S(2)}, u32[]{:S(2)}) collective-permute-start(bf16[640,1152]{1,0:T(8,128)(2,1)} %get-tuple-element.142), channel_id=1, source_target_pairs={{0,4},{4,0},{8,12},{12,8},{16,20},{20,16},{24,28},{28,24},{1,5},{5... | collective-permute-start | bytes 4423688 | tf_op jit(solution)/shard_map/ppermute | solution.py:1128
  471.1 93.8 %reduce-scatter.11.cloned.1.call-start = ((), (), s32[]{:S(2)}) async-start(), calls=%async_computation.8 | async-start | bytes 2211840 | tf_op jit(solution)/shard_map/reduce_scatter | solution.py:1316
  519.0 148.6 %reduce-scatter.17.cloned.1.call-start = ((), (), s32[]{:S(2)}) async-start(), calls=%async_computation.11 | async-start | bytes 4423680 | tf_op jit(solution)/shard_map/reduce_scatter | solution.py:1316
  519.2 45.5 %collective-permute-start.50 = (bf16[1152,768]{1,0:T(8,128)(2,1)}, bf16[1152,768]{1,0:T(8,128)(2,1)}, u32[]{:S(2)}, u32[]{:S(2)}) collective-permute-start(bf16[1152,768]{1,0:T(8,128)(2,1)} %get-tuple-element.194), channel_id=1, source_target_pairs={{0,8},{4,12},{8,0},{12,4},{16,24},{20,28},{24,16},{28,20},{1,9},{5... | collective-permute-start | bytes 5308424 | tf_op jit(solution)/shard_map/ppermute | solution.py:1128
  519.8 44.9 %collective-permute-start.51 = (bf16[1152,768]{1,0:T(8,128)(2,1)}, bf16[1152,768]{1,0:T(8,128)(2,1)}, u32[]{:S(2)}, u32[]{:S(2)}) collective-permute-start(bf16[1152,768]{1,0:T(8,128)(2,1)} %get-tuple-element.196), channel_id=1, source_target_pairs={{0,16},{4,20},{8,24},{12,28},{16,0},{20,4},{24,8},{28,12},{1,17},{... | collective-permute-start | bytes 5308424 | tf_op jit(solution)/shard_map/ppermute | solution.py:1128
  572.4 124.2 %reduce-scatter.15.cloned.1.call-start = ((), (), s32[]{:S(2)}) async-start(), calls=%async_computation.10 | async-start | bytes 2211840 | tf_op jit(solution)/shard_map/reduce_scatter | solution.py:1316
  577.3 50.6 %collective-permute-start.71 = (bf16[384,1152]{1,0:T(8,128)(2,1)S(1)}, bf16[384,1152]{1,0:T(8,128)(2,1)S(1)}, u32[]{:S(2)}, u32[]{:S(2)}) collective-permute-start(bf16[384,1152]{1,0:T(8,128)(2,1)S(1)} %shard_map.242.refs_5_.refs_9_), channel_id=1, source_target_pairs={{0,4},{4,0},{8,12},{12,8},{16,20},{20,16},{24,28},{28,24},{1,5},{5... | collective-permute-start | bytes 2654216 | tf_op jit(solution)/shard_map/ppermute | solution.py:1128
  658.5 33.5 %collective-permute-start.88 = (bf16[384,1152]{1,0:T(8,128)(2,1)S(1)}, bf16[384,1152]{1,0:T(8,128)(2,1)S(1)}, u32[]{:S(2)}, u32[]{:S(2)}) collective-permute-start(bf16[384,1152]{1,0:T(8,128)(2,1)S(1)} %shard_map.257.refs_5_.refs_9_), channel_id=1, source_target_pairs={{0,4},{4,0},{8,12},{12,8},{16,20},{20,16},{24,28},{28,24},{1,5},{5... | collective-permute-start | bytes 2654216 | tf_op jit(solution)/shard_map/ppermute | solution.py:1128
  (256 other events, 1823.1 us)
Sparse Core Ops, SparseCore 0:
  15.6 46.2 all-gather.8
  64.1 54.1 all-gather.10
  120.4 39.0 all-gather.12
  161.6 54.2 all-gather.14
  366.4 36.8 reduce-scatter.6
  418.5 64.8 reduce-scatter.8
  485.8 38.6 reduce-scatter.12
  527.4 37.4 reduce-scatter.10
  572.5 65.4 reduce-scatter.16
  654.3 37.4 reduce-scatter.14
